TPU v7x, 512 devices: a whole 4x4x16 slice. The times are simulated.
512 devices in a mesh: bins: 64 (over z, y), params: 8 (over x, core).
Axes of the slice: x: 4, y: 4, z: 16, core: 2. Of those that a mesh axis runs over, the one named last changes fastest.
Arguments:
- event_bins: int32 [196608], P('bins'), may hold values from 0 to 65535, as said below
- event_weights: bfloat16 [196608, 3072], P('bins', 'params'), may hold values from -6 to 6
- nominal: bfloat16 [196608], P('bins'), may hold values from 0.5 to 2
- background: float32 [65536], P('bins'), may hold values from 1 to 10
- observed: float32 [65536], P('bins'), may hold values from 1 to 100
Outputs:
- hessian: float32 [3072, 1920], P(('params', 'bins'))
Inputs may be any that keep to these rules, and one draw needn't show every extreme that they name: `event_bins`: each index of bins holds 3072 consecutive events in ascending bin order. The owner of bin b is b // 1024; each owner's bins receive from one index of bins between 24 and 72 of its events, and in every draw every index of bins has some owner that receives exactly 72 of its events.
All inputs are finite; a program needn't handle non-finite values.
Results may differ from a plain program's by a relative error of at most 0.0016.
Values may be sent and summed in bfloat16 or wider, within the bound.
No kernel may reach another device: no remote copies, remote signals or barrier semaphores. Data moves between devices by JAX's collectives and lax.ppermute only.
A program may use at most 64 MiB of HBM per device.

v0:
```python
import math

import jax
import jax.numpy as jnp
from jax import lax
from jax.sharding import Mesh
from jax.sharding import PartitionSpec as P

BINS = ("bins_0", "bins_1")
PARAMS_BINS = ("params", "bins_0", "bins_1")


def from_behind(value, axis, steps):
    count = lax.axis_size(axis)
    pairs = [(source, (source + steps) % count) for source in range(count)]
    return lax.ppermute(value, axis, pairs)


def sum_in_order(tiles, axes, turns):
    inside = tiles.shape[1:]
    tiles = tiles.reshape(*(lax.axis_size(a) for a in axes), *inside)
    tiles = jnp.moveaxis(tiles, turns, range(len(axes))).reshape(-1, *inside)
    for k in turns:
        tiles = lax.psum_scatter(tiles, axes[k], scatter_dimension=0, tiled=True)
    return tiles[0]


def split_up(x, dim, count):
    before, after = (x.shape[:dim], x.shape[dim + 1 :])
    return jnp.moveaxis(x.reshape(*before, count, -1, *after), dim, 0)


def summed_rows_2(x, axes, turns, dim):
    count = lax.axis_size(axes)
    return sum_in_order(split_up(x, dim, count), axes, turns)


def body(event_bins, event_weights, nominal, background, observed):
    owners = lax.axis_size(BINS)
    groups_count = lax.axis_size("params")
    events = event_bins.shape[0]
    width_g = event_weights.shape[1]
    bins_dev = background.shape[0]
    capacity = 3 * events // (2 * owners)
    destination = event_bins // bins_dev
    targets = jnp.arange(owners, dtype=jnp.int32)
    starts = jnp.sum((destination[None, :] < targets[:, None]).astype(jnp.int32), axis=1)
    counts = jnp.sum((destination[None, :] == targets[:, None]).astype(jnp.int32), axis=1)
    slot_ids = jnp.arange(capacity, dtype=jnp.int32)
    filled = slot_ids[None, :] < counts[:, None]
    row_index = jnp.where(filled, starts[:, None] + slot_ids[None, :], 0)
    send_rows = jnp.where(filled[:, :, None], event_weights[row_index], jnp.zeros((), jnp.bfloat16))
    send_nominal = jnp.where(filled, nominal[row_index], jnp.zeros((), jnp.bfloat16))
    send_local = jnp.where(filled, event_bins[row_index] - targets[:, None] * bins_dev, -1)
    got_rows, got_nominal = (
        lax.all_to_all(send_rows, BINS, split_axis=0, concat_axis=0, tiled=True),
        lax.all_to_all(send_nominal, BINS, split_axis=0, concat_axis=0, tiled=True),
    )
    got_local = lax.all_to_all(send_local, BINS, split_axis=0, concat_axis=0, tiled=True)
    total_rows = owners * capacity
    block_rows = math.gcd(total_rows, 512)
    blocks = total_rows // block_rows
    bin_ids = jnp.arange(bins_dev, dtype=jnp.int32)
    dims = (((0,), (0,)), ((), ()))

    def add_block(carry, stacked):
        rows_block, nominal_block, local_block = stacked
        one_hot = (local_block[:, None] == bin_ids[None, :]).astype(jnp.bfloat16)
        hist_part = lax.dot_general(one_hot, rows_block, dims, preferred_element_type=jnp.float32)
        nominal_part = lax.dot_general(
            one_hot, nominal_block, dims, preferred_element_type=jnp.float32
        )
        return ((carry[0] + hist_part, carry[1] + nominal_part), None)

    start_sums = (jnp.zeros((bins_dev, width_g), jnp.float32), jnp.zeros((bins_dev,), jnp.float32))
    stacked_in = (
        got_rows.reshape(blocks, block_rows, width_g),
        got_nominal.reshape(blocks, block_rows),
        got_local.reshape(blocks, block_rows),
    )
    (histogram, nominal_sum), _ = lax.scan(add_block, start_sums, stacked_in)
    templates = histogram.astype(jnp.bfloat16)
    yields = background + nominal_sum
    curvature = observed / (yields * yields)
    weighted = (curvature[:, None] * templates.astype(jnp.float32)).astype(jnp.bfloat16)
    half_groups = groups_count // 2
    pieces = [templates]
    for shift_by in range(1, half_groups + 1):
        pieces.append(from_behind(templates, "params", -shift_by))
    partners = jnp.concatenate(pieces, axis=1)
    summed = summed_rows_2(
        lax.dot_general(weighted, partners, dims, preferred_element_type=jnp.float32),
        BINS,
        (1, 0),
        0,
    )
    return summed * (1.0 / (bins_dev * owners))


def solution(mesh):
    split = Mesh(mesh.devices.reshape(16, 4, mesh.shape["params"]), ("bins_0", "bins_1", "params"))
    placed = (P(BINS), P(BINS, "params"), P(BINS), P(BINS), P(BINS))
    return jax.shard_map(
        body, mesh=split, in_specs=placed, out_specs=P(PARAMS_BINS, None), check_vma=False
    )
```

profile of v0, /device:TPU:6, one launch (start us, length us, event | category | flops | bytes accessed | tf_op | source)
XLA Modules:
  0.0 587.4 jit_solution(1323911377315267502)
XLA Ops:
  7.9 27.3 %gather_fusion.2 = bf16[4608]{0:T(1024)(128)(2,1)S(1)} fusion(bf16[3072]{0:T(1024)(128)(2,1)S(1)} %copy-done.2, s32[5120]{0:T(1024)S(1)} %pad_clamp_fusion), kind=kCustom, calls=%fused_computation.2 | custom fusion | bytes 36864 | tf_op jit(solution)/shard_map/gather | solution.py:53
  36.0 18.7 %all-to-all-start.2 = ((bf16[64,1,72]{2,1,0:T(2,128)(2,1)}), bf16[64,1,72]{2,1,0:T(2,128)(2,1)S(1)}, u32[]{:S(2)}, u32[]{:S(2)}) async-start(bf16[64,1,72]{2,1,0:T(2,128)(2,1)} %copy.13), calls=%async_computation.2 | async-start | bytes 65536 | tf_op jit(solution)/shard_map/all_to_all | solution.py:57
  54.8 24.1 %gather_fusion = s32[4608]{0:T(1024)S(1)} fusion(s32[3072]{0:T(1024)S(1)} %copy-done.1, s32[5120]{0:T(1024)S(1)} %pad_clamp_fusion), kind=kCustom, calls=%fused_computation | custom fusion | bytes 55296 | tf_op jit(solution)/shard_map/gather | solution.py:54
  79.7 13.5 %gather_fusion.1 = bf16[4608,384]{1,0:T(8,128)(2,1)} fusion(bf16[3072,384]{1,0:T(8,128)(2,1)S(1)} %copy-done, s32[5120]{0:T(1024)S(1)} %pad_clamp_fusion), kind=kCustom, calls=%fused_computation.1 | custom fusion | bytes 7096320 | tf_op jit(solution)/shard_map/gather | solution.py:52
  93.2 15.1 %all-to-all-start = ((s32[64,1,72]{2,1,0:T(1,128)}), s32[64,1,72]{2,1,0:T(1,128)S(1)}, u32[]{:S(2)}, u32[]{:S(2)}) async-start(s32[64,1,72]{2,1,0:T(1,128)} %bitcast), calls=%async_computation | async-start | bytes 65536 | tf_op jit(solution)/shard_map/all_to_all | solution.py:59
  108.3 3.7 broadcast_select_fusion
  112.0 10.9 %all-to-all-done = s32[64,1,72]{2,1,0:T(1,128)S(1)} async-done(((s32[64,1,72]{2,1,0:T(1,128)}), s32[64,1,72]{2,1,0:T(1,128)S(1)}, u32[]{:S(2)}, u32[]{:S(2)}) %all-to-all-start) | async-done | bytes 18464 | tf_op jit(solution)/shard_map/all_to_all | solution.py:59
  122.9 5.6 all-to-all-start.1
  130.0 158.7 %all-to-all-done.1 = bf16[64,72,384]{2,1,0:T(8,128)(2,1)} async-done(((bf16[64,72,384]{2,1,0:T(8,128)(2,1)}), bf16[64,72,384]{2,1,0:T(8,128)(2,1)}, u32[]{:S(2)}, u32[]{:S(2)}) %all-to-all-start.1) | async-done | bytes 3538976 | tf_op jit(solution)/shard_map/all_to_all | solution.py:56
  288.7 36.4 %while.13 = (s32[]{:T(128)}, f32[1024,384]{1,0:T(8,128)}, f32[1024]{0:T(1024)S(1)}, s32[9,512]{1,0:T(8,128)S(1)}, bf16[9,512,384]{2,1,0:T(8,128)(2,1)}, /*index=5*/bf16[9,512]{1,0:T(8,128)(2,1)S(1)}, s32[]{:T(128)}, s32[]{:T(128)}) while((s32[]{:T(128)}, f32[1024,384]{1,0:T(8,128)}, f32[1024]{0:T(1024)S(1)}, ...), condition=%wide.region_3.4_spmd.clone, body=%wide.region_2.3_spmd.clone.sunk | while | flops 405538816 | bytes 3566184 | solution.py:81
  288.7 3.1 select_add_fusion.4
  292.3 3.6 select_add_fusion.4
  296.4 3.6 select_add_fusion.4
  300.5 3.6 select_add_fusion.4
  304.6 3.6 select_add_fusion.4
  308.7 3.6 select_add_fusion.4
  312.8 3.6 select_add_fusion.4
  316.9 3.6 select_add_fusion.4
  321.0 3.6 select_add_fusion.4
  326.7 2.7 collective-permute-start.1
  329.4 2.9 collective-permute-start.2
  332.3 4.5 collective-permute-start.3
  336.8 5.5 collective-permute-done
  342.4 16.7 %collective-permute-done.1 = bf16[1024,384]{1,0:T(8,128)(2,1)S(1)} collective-permute-done((bf16[1024,384]{1,0:T(8,128)(2,1)S(1)}, bf16[1024,384]{1,0:T(8,128)(2,1)S(1)}, u32[]{:S(2)}, u32[]{:S(2)}) %collective-permute-start.1) | collective-permute-done | bytes 786464 | tf_op jit(solution)/shard_map/ppermute | solution.py:16
  359.3 16.7 %collective-permute-done.2 = bf16[1024,384]{1,0:T(8,128)(2,1)S(1)} collective-permute-done((bf16[1024,384]{1,0:T(8,128)(2,1)S(1)}, bf16[1024,384]{1,0:T(8,128)(2,1)S(1)}, u32[]{:S(2)}, u32[]{:S(2)}) %collective-permute-start.2) | collective-permute-done | bytes 786464 | tf_op jit(solution)/shard_map/ppermute | solution.py:16
  376.1 12.4 %collective-permute-done.3 = bf16[1024,384]{1,0:T(8,128)(2,1)S(1)} collective-permute-done((bf16[1024,384]{1,0:T(8,128)(2,1)S(1)}, bf16[1024,384]{1,0:T(8,128)(2,1)S(1)}, u32[]{:S(2)}, u32[]{:S(2)}) %collective-permute-start.3) | collective-permute-done | bytes 786464 | tf_op jit(solution)/shard_map/ppermute | solution.py:16
  388.7 3.6 fusion.12
  392.3 4.5 reshape_reshape.3
  396.7 5.4 copy.14
  402.3 35.7 %reduce-scatter.3.cloned.1.call-done = f32[16,6,1920]{2,0,1:T(8,128)} async-done(((f32[64,6,1920]{2,0,1:T(8,128)}), f32[16,6,1920]{2,0,1:T(8,128)}) %reduce-scatter.3.cloned.1.call-update) | async-done | bytes 737296 | tf_op jit(solution)/shard_map/reduce_scatter | solution.py:24
  439.3 138.9 %all-reduce.3.cloned.1.call-done = f32[16,6,1920]{2,0,1:T(8,128)} async-done(((f32[16,6,1920]{2,0,1:T(8,128)}), f32[16,6,1920]{2,0,1:T(8,128)}) %all-reduce.3.cloned.1.call-update) | async-done | bytes 737296
  578.2 1.7 dynamic-slice_multiply_fusion
  (70 shorter events, 13.2 us)
Async XLA Ops:
  6.5 73.2 %copy-start = (bf16[3072,384]{1,0:T(8,128)(2,1)S(1)}, bf16[3072,384]{1,0:T(8,128)(2,1)}, u32[]{:S(2)}) copy-start(bf16[3072,384]{1,0:T(8,128)(2,1)} %param.8) | copy-start | bytes 7077892
  6.5 1.3 copy-start.2
  35.2 19.6 %copy-start.1 = (s32[3072]{0:T(1024)S(1)}, s32[3072]{0:T(1024)}, u32[]{:S(2)}) copy-start(s32[3072]{0:T(1024)} %param.7) | copy-start | bytes 36868
  36.0 57.2 %all-to-all-start.2 = ((bf16[64,1,72]{2,1,0:T(2,128)(2,1)}), bf16[64,1,72]{2,1,0:T(2,128)(2,1)S(1)}, u32[]{:S(2)}, u32[]{:S(2)}) async-start(bf16[64,1,72]{2,1,0:T(2,128)(2,1)} %copy.13), calls=%async_computation.2 | async-start | bytes 65536 | tf_op jit(solution)/shard_map/all_to_all | solution.py:57
  93.2 29.6 %all-to-all-start = ((s32[64,1,72]{2,1,0:T(1,128)}), s32[64,1,72]{2,1,0:T(1,128)S(1)}, u32[]{:S(2)}, u32[]{:S(2)}) async-start(s32[64,1,72]{2,1,0:T(1,128)} %bitcast), calls=%async_computation | async-start | bytes 65536 | tf_op jit(solution)/shard_map/all_to_all | solution.py:59
  122.9 165.8 %all-to-all-start.1 = ((bf16[64,72,384]{2,1,0:T(8,128)(2,1)}), bf16[64,72,384]{2,1,0:T(8,128)(2,1)}, u32[]{:S(2)}, u32[]{:S(2)}) async-start(bf16[64,72,384]{2,1,0:T(8,128)(2,1)} %broadcast_select_fusion), calls=%async_computation.1 | async-start | bytes 7077888 | tf_op jit(solution)/shard_map/all_to_all | solution.py:56
  128.5 309.5 %reduce-scatter.3.cloned.1.call-start = ((), (), s32[]{:S(2)}) async-start(), calls=%async_computation.4 | async-start | bytes 3686400 | tf_op jit(solution)/shard_map/reduce_scatter | solution.py:24
  288.7 48.1 %copy-start.3 = (f32[1024]{0:T(1024)S(1)}, f32[1024]{0:T(1024)}, u32[]{:S(2)}) copy-start(f32[1024]{0:T(1024)} %param.11) | copy-start | bytes 12292
  288.7 48.1 %copy-start.4 = (f32[1024]{0:T(1024)S(1)}, f32[1024]{0:T(1024)}, u32[]{:S(2)}) copy-start(f32[1024]{0:T(1024)} %param.10) | copy-start | bytes 12292
  326.6 15.7 %collective-permute-start = (bf16[1024,384]{1,0:T(8,128)(2,1)S(1)}, bf16[1024,384]{1,0:T(8,128)(2,1)S(1)}, u32[]{:S(2)}, u32[]{:S(2)}) collective-permute-start(bf16[1024,384]{1,0:T(8,128)(2,1)S(1)} %get-tuple-element.83), channel_id=1, source_target_pairs={{0,7},{1,0},{2,1},{3,2},{4,3},{5,4},{6,5},{7,6},{8,15},{9,8},{10,9... | collective-permute-start | bytes 2359304 | tf_op jit(solution)/shard_map/ppermute | solution.py:16
  326.7 32.5 %collective-permute-start.1 = (bf16[1024,384]{1,0:T(8,128)(2,1)S(1)}, bf16[1024,384]{1,0:T(8,128)(2,1)S(1)}, u32[]{:S(2)}, u32[]{:S(2)}) collective-permute-start(bf16[1024,384]{1,0:T(8,128)(2,1)S(1)} %get-tuple-element.83), channel_id=1, source_target_pairs={{0,6},{1,7},{2,0},{3,1},{4,2},{5,3},{6,4},{7,5},{8,14},{9,15},{10,... | collective-permute-start | bytes 2359304 | tf_op jit(solution)/shard_map/ppermute | solution.py:16
  329.4 46.6 %collective-permute-start.2 = (bf16[1024,384]{1,0:T(8,128)(2,1)S(1)}, bf16[1024,384]{1,0:T(8,128)(2,1)S(1)}, u32[]{:S(2)}, u32[]{:S(2)}) collective-permute-start(bf16[1024,384]{1,0:T(8,128)(2,1)S(1)} %get-tuple-element.83), channel_id=1, source_target_pairs={{0,5},{1,6},{2,7},{3,0},{4,1},{5,2},{6,3},{7,4},{8,13},{9,14},{10,... | collective-permute-start | bytes 2359304 | tf_op jit(solution)/shard_map/ppermute | solution.py:16
  332.3 56.3 %collective-permute-start.3 = (bf16[1024,384]{1,0:T(8,128)(2,1)S(1)}, bf16[1024,384]{1,0:T(8,128)(2,1)S(1)}, u32[]{:S(2)}, u32[]{:S(2)}) collective-permute-start(bf16[1024,384]{1,0:T(8,128)(2,1)S(1)} %get-tuple-element.83), channel_id=1, source_target_pairs={{0,4},{1,5},{2,6},{3,7},{4,0},{5,1},{6,2},{7,3},{8,12},{9,13},{10,... | collective-permute-start | bytes 2359304 | tf_op jit(solution)/shard_map/ppermute | solution.py:16
  402.2 176.0 %all-reduce.3.cloned.1.call-start = ((), (), s32[]{:S(2)}) async-start(), calls=%async_computation.5 | async-start | bytes 1474560
Sparse Core Ops, SparseCore 0:
  402.3 35.6 reduce-scatter.2
  440.5 137.7 all-reduce.2
where the time goes:
time: 588 us; the launch traced here: 587 us
  waiting for transfers between devices  396 us (67%)
  local copies, waits for them, and re-layouts  79 us (13%)
  starting transfers between devices  49.6 us (8%)
  matrix products  39.7 us (7%)
  between operations  13.6 us (2%)
  other arithmetic  9.8 us (2%)
    all_to_all x1, waiting for transfers between devices, body(): lax.all_to_all(send_rows, BINS, split_axis=0, concat_axis=0, tiled=True)  159 us
    unnamed x3, waiting for transfers between devices  139 us
    ppermute x4, waiting for transfers between devices, from_behind(): return lax.ppermute(value, axis, pairs)  51.3 us
    reduce_scatter x1, waiting for transfers between devices, sum_in_order(): tiles = lax.psum_scatter(tiles, axes[k], scatter_dimension=0, tiled=True)  35.7 us
    dot_general x9, matrix products, add_block(): lax.dot_general(one_hot, rows_block, dims, preferred_element_type=jnp.flo...  31.8 us
    gather x2, local copies, waits for them, and re-layouts, body(): nominal[row_index]  27.4 us
    gather x2, local copies, waits for them, and re-layouts, body(): event_bins[row_index] - targets[:, None] * bins_dev  24.2 us
    all_to_all x1, starting transfers between devices, body(): lax.all_to_all(send_nominal, BINS, split_axis=0, concat_axis=0, tiled=True)  18.7 us
  transfers between devices with their start and end apart: 9, of which 8 were waited for; matrix products, arithmetic and copies ran while one was open for 8% of the time, Pallas kernels for 0%

commit v1 on v0

v1 whole, which is shorter than its diff:
```python
import functools

import jax
import jax.numpy as jnp
import numpy as np
from jax import lax
from jax.experimental import pallas as pl
from jax.experimental.pallas import tpu as pltpu
from jax.sharding import Mesh
from jax.sharding import PartitionSpec as P

BINS = ("bins_0", "bins_1")
PARAMS_BINS = ("params", "bins_0", "bins_1")
CAP = 72
EXTRA = 8
WIN = 96
COLS = 128
KB = 512
VMEM = pl.BlockSpec(memory_space=pltpu.VMEM)
SMEM = pl.BlockSpec(memory_space=pltpu.SMEM)
PARAMS = pltpu.CompilerParams(vmem_limit_bytes=40 * 2**20)


def cost(flops, moved):
    return pl.CostEstimate(flops=flops, bytes_accessed=moved, transcendentals=0)


def pick_rows(start, w_ref, events, cols):
    base = jnp.minimum((start // 16) * 16, events - WIN)
    base = pl.multiple_of(base, 16)
    off = start - base
    row = lax.broadcasted_iota(jnp.int32, (CAP, WIN), 0)
    col = lax.broadcasted_iota(jnp.int32, (CAP, WIN), 1)
    choose = jnp.where(col == row + off, 1.0, 0.0).astype(jnp.bfloat16)
    window = w_ref[pl.ds(base, WIN), cols]
    return jnp.dot(choose, window, preferred_element_type=jnp.float32)


def pack_first(owners, bins_dev, events, starts_ref, info_ref, w_ref, out_ref):
    lines = lax.broadcasted_iota(jnp.int32, (EXTRA, 128), 0)

    def one(o, _):
        start = starts_ref[o]
        rows = pick_rows(start, w_ref, events, slice(0, COLS))
        at = jnp.minimum((start // 128) * 128, events - 256)
        at = pl.multiple_of(at, 128)
        span = pltpu.roll(info_ref[:, pl.ds(at, 256)], 256 - (start - at), 1)[:, :128]
        local = span[0:1].astype(jnp.int32) - o * bins_dev
        inside = (local >= 0) & (local < bins_dev)
        high = jnp.where(inside, local // 32, -1).astype(jnp.float32)
        low = jnp.where(inside, local % 32, 0).astype(jnp.float32)
        nominal = jnp.where(inside, span[1:2], 0.0)
        extra = jnp.where(lines == 0, high, jnp.where(lines == 1, low, jnp.where(lines == 2, nominal, 0.0)))
        out_ref[o] = jnp.concatenate([rows, extra], axis=0).astype(jnp.bfloat16)
        return 0

    lax.fori_loop(0, owners, one, 0, unroll=4)


def pack_rest(owners, events, starts_ref, w_ref, *out_refs):
    def one(o, _):
        start = starts_ref[o]
        rows = pick_rows(start, w_ref, events, slice(COLS, 3 * COLS)).astype(jnp.bfloat16)
        for i, out_ref in enumerate(out_refs):
            out_ref[o] = rows[:, i * COLS : (i + 1) * COLS]
        return 0

    lax.fori_loop(0, owners, one, 0, unroll=4)


def one_hot_of(bins_ref, at, bins_dev):
    ids = lax.broadcasted_iota(jnp.int32, (bins_dev, KB), 0)
    return jnp.where(ids == bins_ref[:, pl.ds(at, KB)], 1.0, 0.0).astype(jnp.bfloat16)


def hist_first(bins_ref, nominal_ref, rows_ref, background_ref, observed_ref, out_ref, curve_ref, acc, acc_n):
    bins_dev = out_ref.shape[0]
    acc[...] = jnp.zeros_like(acc)
    acc_n[...] = jnp.zeros_like(acc_n)

    def one(i, _):
        at = pl.multiple_of(i * KB, KB)
        hot = one_hot_of(bins_ref, at, bins_dev)
        acc[...] += jnp.dot(hot, rows_ref[pl.ds(at, KB), :], preferred_element_type=jnp.float32)
        acc_n[...] += lax.dot_general(
            hot, nominal_ref[:, pl.ds(at, KB)], (((1,), (1,)), ((), ())), preferred_element_type=jnp.float32
        )
        return 0

    lax.fori_loop(0, rows_ref.shape[0] // KB, one, 0)
    out_ref[...] = acc[...].astype(jnp.bfloat16)
    yields = background_ref[...] + acc_n[:, 0:1]
    curve_ref[...] = observed_ref[...] / (yields * yields)


def hist_next(bins_ref, rows_ref, out_ref, acc):
    bins_dev = out_ref.shape[0]
    acc[...] = jnp.zeros_like(acc)

    def one(i, _):
        at = pl.multiple_of(i * KB, KB)
        hot = one_hot_of(bins_ref, at, bins_dev)
        acc[...] += jnp.dot(hot, rows_ref[pl.ds(at, KB), :], preferred_element_type=jnp.float32)
        return 0

    lax.fori_loop(0, rows_ref.shape[0] // KB, one, 0)
    out_ref[...] = acc[...].astype(jnp.bfloat16)


def gram(turns, curve_ref, order_ref, *refs):
    parts, out_ref = refs[:-1], refs[-1]
    chunks = len(parts) // turns
    own = jnp.concatenate([parts[c][...] for c in range(chunks)], axis=1)
    weighted = (curve_ref[...] * own.astype(jnp.float32)).astype(jnp.bfloat16)
    lhs = lax.dot_general(
        order_ref[...], weighted, (((1,), (1,)), ((), ())), preferred_element_type=jnp.float32
    ).astype(jnp.bfloat16)
    width = own.shape[1]
    step = out_ref.shape[1]
    for k in range(turns):
        partner = jnp.concatenate([parts[k * chunks + c][...] for c in range(chunks)], axis=1)
        full = jnp.dot(lhs, partner, preferred_element_type=jnp.float32).astype(jnp.bfloat16)
        for y in range(out_ref.shape[0]):
            out_ref[y, :, k * width : (k + 1) * width] = full[y * step : (y + 1) * step]


def from_behind(value, axis, steps):
    count = lax.axis_size(axis)
    pairs = [(source, (source + steps) % count) for source in range(count)]
    return lax.ppermute(value, axis, pairs)


def exchange(value, axis):
    return lax.all_to_all(value, axis, split_axis=0, concat_axis=0, tiled=True)


def body(event_bins, event_weights, nominal, background, observed):
    bf16, f32 = jnp.bfloat16, jnp.float32
    n0, n1 = (lax.axis_size(a) for a in BINS)
    owners = n0 * n1
    groups = lax.axis_size("params")
    events, width = event_weights.shape
    bins_dev = background.shape[0]
    chunks = width // COLS
    targets = jnp.arange(owners, dtype=jnp.int32)
    starts = jnp.sum((event_bins[None, :] < targets[:, None] * bins_dev).astype(jnp.int32), axis=1)
    info = jnp.stack([event_bins.astype(f32), nominal.astype(f32)])
    info = jnp.concatenate([info, jnp.zeros((6, events), f32)])

    slab = CAP + EXTRA
    send0 = pl.pallas_call(
        functools.partial(pack_first, owners, bins_dev, events),
        out_shape=jax.ShapeDtypeStruct((owners, slab, COLS), bf16),
        in_specs=[SMEM, VMEM, VMEM],
        out_specs=VMEM,
        compiler_params=PARAMS,
        cost_estimate=cost(2 * owners * CAP * WIN * COLS, 2 * owners * slab * COLS * 2),
        name="pack_first",
    )(starts, info, event_weights)
    rest = pl.pallas_call(
        functools.partial(pack_rest, owners, events),
        out_shape=[jax.ShapeDtypeStruct((owners, CAP, COLS), bf16)] * (chunks - 1),
        in_specs=[SMEM, VMEM],
        out_specs=[VMEM] * (chunks - 1),
        compiler_params=PARAMS,
        cost_estimate=cost(4 * owners * CAP * WIN * COLS, 4 * owners * CAP * COLS * 2),
        name="pack_rest",
    )(starts, event_weights)
    got0 = exchange(send0, BINS)
    got = [exchange(s, BINS) for s in rest]

    extra = got0[:, CAP:, :CAP].astype(f32)
    local = (extra[:, 0] * 32.0 + extra[:, 1]).astype(jnp.int32)
    local_wide = jnp.pad(local, ((0, 0), (0, EXTRA)), constant_values=-1).reshape(1, owners * slab)
    local = local.reshape(1, owners * CAP)
    nom = jnp.pad(extra[:, 2], ((0, 0), (0, EXTRA))).astype(bf16).reshape(1, owners * slab)
    nom = jnp.broadcast_to(nom, (8, owners * slab))
    tile = jax.ShapeDtypeStruct((bins_dev, COLS), bf16)
    acc = pltpu.VMEM((bins_dev, COLS), f32)
    first, curve = pl.pallas_call(
        hist_first,
        out_shape=[tile, jax.ShapeDtypeStruct((bins_dev, 1), f32)],
        in_specs=[VMEM] * 5,
        out_specs=[VMEM] * 2,
        scratch_shapes=[acc, pltpu.VMEM((bins_dev, 8), f32)],
        compiler_params=PARAMS,
        cost_estimate=cost(2 * owners * slab * bins_dev * 256, owners * slab * COLS * 2),
        name="hist_first",
    )(
        local_wide,
        nom,
        got0.reshape(owners * slab, COLS),
        background.reshape(bins_dev, 1),
        observed.reshape(bins_dev, 1),
    )
    tiles = [first]
    for g in got:
        tiles.append(
            pl.pallas_call(
                hist_next,
                out_shape=tile,
                in_specs=[VMEM] * 2,
                out_specs=VMEM,
                scratch_shapes=[acc],
                compiler_params=PARAMS,
                cost_estimate=cost(2 * owners * CAP * bins_dev * 256, owners * CAP * COLS * 2),
                name="hist_next",
            )(local, g.reshape(owners * CAP, COLS))
        )
    turns = groups // 2 + 1
    moved = [[from_behind(t, "params", -k) if k else t for t in tiles] for k in range(turns)]

    lines = width // owners
    j = np.arange(width)
    source = ((j % (width // n1)) // lines * n1 + j // (width // n1)) * lines + j % lines
    order = np.zeros((width, width), np.float32)
    order[j, source] = 1.0
    partial = pl.pallas_call(
        functools.partial(gram, turns),
        out_shape=jax.ShapeDtypeStruct((n1, width // n1, turns * width), bf16),
        in_specs=[VMEM] * (2 + turns * chunks),
        out_specs=VMEM,
        compiler_params=PARAMS,
        cost_estimate=cost(2 * bins_dev * width * width * (turns + 1), turns * width * bins_dev * 2),
        name="gram",
    )(curve, jnp.asarray(order, bf16), *[t for row in moved for t in row])
    across = exchange(partial, BINS[1]).astype(f32).sum(axis=0).astype(bf16)
    along = exchange(across.reshape(n0, lines, turns * width), BINS[0]).astype(f32).sum(axis=0)
    return along * (1.0 / (bins_dev * owners))


def solution(mesh):
    split = Mesh(mesh.devices.reshape(16, 4, mesh.shape["params"]), ("bins_0", "bins_1", "params"))
    placed = (P(BINS), P(BINS, "params"), P(BINS), P(BINS), P(BINS))
    return jax.shard_map(
        body, mesh=split, in_specs=placed, out_specs=P(PARAMS_BINS, None), check_vma=False
    )
```

time: 588 us -> 317 us (0.54)
  waiting for transfers between devices: 396 us -> 86.9 us
  blocking collectives: 0 us -> 126 us
  local copies, waits for them, and re-layouts: 79 us -> 10.9 us
  matrix products: 39.7 us -> 0 us
  Pallas kernels: 0 us -> 29.4 us
  between operations: 13.6 us -> 0.32 us
    unnamed x3 -> x0, waiting for transfers between devices: 139 us -> none
    all_to_all x0 -> x3, blocking collectives: none -> 126 us  [exchange(): return lax.all_to_all(value, axis, split_axis=0, concat_axis=0, tiled=True)]
    all_to_all x3 -> x2, waiting for transfers between devices: 170 us -> 73.4 us  [exchange(): return lax.all_to_all(value, axis, split_axis=0, concat_axis=0, tiled=True)]
    gather x5 -> x0, local copies, waits for them, and re-layouts: 65 us -> none  [the longest x2 27.4 us: body(): nominal[row_index]]
    dot_general x19 -> x0, matrix products: 39.7 us -> none  [the longest x9 31.8 us: add_block(): lax.dot_general(one_hot, rows_block, dims, preferred_element_type=jnp.flo...]
    ppermute x4 -> x12, waiting for transfers between devices: 51.3 us -> 13.5 us  [from_behind(): return lax.ppermute(value, axis, pairs)]
    reduce_scatter x1 -> x0, waiting for transfers between devices: 35.7 us -> none  [sum_in_order(): tiles = lax.psum_scatter(tiles, axes[k], scatter_dimension=0, tiled=True)]
    pallas_call x0 -> x6, Pallas kernels: none -> 29.4 us  [the longest x2 9.31 us: body(): pl.pallas_call(hist_next, out_shape=tile, in_specs=[VMEM] * 2, out_specs=...]
  transfers between devices with their start and end apart: 9 -> 14, of which waited for: 8 -> 6; matrix products, arithmetic and copies ran while one was open for 8% -> 3% of each run, Pallas kernels for 0% -> 7%
where the time goes in v1:
time: 317 us; the launch traced here: 313 us
  blocking collectives  126 us (40%)
  waiting for transfers between devices  86.9 us (27%)
  starting transfers between devices  54.3 us (17%)
  Pallas kernels  29.4 us (9%)
  local copies, waits for them, and re-layouts  10.9 us (3%)
  other arithmetic  5.8 us (2%)
    all_to_all x3, blocking collectives, exchange(): return lax.all_to_all(value, axis, split_axis=0, concat_axis=0, tiled=True)  126 us
    all_to_all x2, waiting for transfers between devices, exchange(): return lax.all_to_all(value, axis, split_axis=0, concat_axis=0, tiled=True)  73.4 us
    ppermute x12, starting transfers between devices, from_behind(): return lax.ppermute(value, axis, pairs)  29.2 us
    all_to_all x2, starting transfers between devices, exchange(): return lax.all_to_all(value, axis, split_axis=0, concat_axis=0, tiled=True)  25.1 us
    ppermute x12, waiting for transfers between devices, from_behind(): return lax.ppermute(value, axis, pairs)  13.5 us
    pallas_call x2, Pallas kernels, body(): pl.pallas_call(hist_next, out_shape=tile, in_specs=[VMEM] * 2, out_specs=...  9.31 us
    pallas_call x1, Pallas kernels, body(): pl.pallas_call(hist_first, out_shape=[tile, jax.ShapeDtypeStruct((bins_de...  8.09 us
  transfers between devices with their start and end apart: 14, of which 6 were waited for; matrix products, arithmetic and copies ran while one was open for 3% of the time, Pallas kernels for 7%

profile of v1, /device:TPU:6, one launch (start us, length us, event | category | flops | bytes accessed | tf_op | source)
XLA Modules:
  0.0 313.2 jit_solution(10288875466002148569)
XLA Ops:
  1.0 1.7 copy-done
  2.6 4.7 %pack_rest.1 = (bf16[64,72,128]{2,1,0:T(8,128)(2,1)}, bf16[64,72,128]{2,1,0:T(8,128)(2,1)S(1)}) custom-call(s32[64]{0:T(128)S(1)} %convert_reduce_fusion.1.starts_ref, bf16[3072,384]{1,0:T(8,128)(2,1)S(1)} %copy-done), custom_call_target="tpu_custom_call" | custom-call | flops 226492416 | bytes 4718592 | tf_op jit(solution)/shard_map/pack_rest/pallas_call | solution.py:160
  7.3 1.0 copy-done.3
  8.3 18.9 %all-to-all-start.2 = ((bf16[64,72,128]{2,1,0:T(8,128)(2,1)}), bf16[64,72,128]{2,1,0:T(8,128)(2,1)S(1)}, u32[]{:S(2)}, u32[]{:S(2)}) async-start(bf16[64,72,128]{2,1,0:T(8,128)(2,1)} %copy-done.3), calls=%async_computation.2 | async-start | bytes 2359296 | tf_op jit(solution)/shard_map/all_to_all | solution.py:134
  28.1 3.6 %pack_first.1 = bf16[64,80,128]{2,1,0:T(8,128)(2,1)S(1)} custom-call(s32[64]{0:T(128)S(1)} %convert_reduce_fusion.1.starts_ref, f32[8,3072]{1,0:T(8,128)S(1)} %maximum_maximum_fusion.info_ref, bf16[3072,384]{1,0:T(8,128)(2,1)S(1)} %copy-done.1), custom_call_target="tpu_custom_call" | custom-call | flops 113246208 | bytes 2621440 | tf_op jit(solution)/shard_map/pack_first/pallas_call | solution.py:151
  31.7 1.1 copy-done.2
  32.8 55.3 %all-to-all-done.2 = bf16[64,72,128]{2,1,0:T(8,128)(2,1)S(1)} async-done(((bf16[64,72,128]{2,1,0:T(8,128)(2,1)}), bf16[64,72,128]{2,1,0:T(8,128)(2,1)S(1)}, u32[]{:S(2)}, u32[]{:S(2)}) %all-to-all-start.2) | async-done | bytes 1179680 | tf_op jit(solution)/shard_map/all_to_all | solution.py:134
  88.1 71.8 %all_to_all.25 = bf16[64,80,128]{2,1,0:T(8,128)(2,1)S(1)} all-to-all(bf16[64,80,128]{2,1,0:T(8,128)(2,1)} %copy-done.2), channel_id=1, replica_groups=mesh['bins_0'=16,'bins_1'=4,'params'=8] {'bins_0','bins_1'}, dimensions={0} | all-to-all | bytes 2621440 | tf_op jit(solution)/shard_map/all_to_all | solution.py:134
  159.9 6.2 %all-to-all-start.1 = ((bf16[64,72,128]{2,1,0:T(8,128)(2,1)}), bf16[64,72,128]{2,1,0:T(8,128)(2,1)}, u32[]{:S(2)}, u32[]{:S(2)}) async-start(bf16[64,72,128]{2,1,0:T(8,128)(2,1)} %get-tuple-element.11), calls=%async_computation.1 | async-start | bytes 2359296 | tf_op jit(solution)/shard_map/all_to_all | solution.py:134
  168.6 2.4 fusion.1
  171.6 1.5 reshape.61.bins_ref
  174.5 8.1 %hist_first.1 = (bf16[1024,128]{1,0:T(8,128)(2,1)}, f32[1024,1]{1,0:T(8,128)S(1)}) custom-call(s32[1,5120]{1,0:T(1,128)S(1)} %copy-done.4, bf16[8,5120]{1,0:T(8,128)(2,1)S(1)} %broadcast_in_dim.14.nominal_ref, bf16[5120,128]{1,0:T(8,128)(2,1)S(1)} %bitcast.11, f32[1024,1]{1,0:T(8,128)S(1)} %copy.9.background_ref, f32[1024,1]{1,0:T(8,128)S(1)} %copy.10.observed_ref), custom_call_target="tpu_custom_call" | custom-call | flops 2684354560 | bytes 1310720 | tf_op jit(solution)/shard_map/hist_first/pallas_call | solution.py:180
  183.4 3.3 %collective-permute-start.9 = (bf16[1024,128]{1,0:T(8,128)(2,1)}, bf16[1024,128]{1,0:T(8,128)(2,1)S(1)}, u32[]{:S(2)}, u32[]{:S(2)}) collective-permute-start(bf16[1024,128]{1,0:T(8,128)(2,1)} %get-tuple-element.10.refs_0_), channel_id=1, source_target_pairs={{0,4},{1,5},{2,6},{3,7},{4,0},{5,1},{6,2},{7,3},{8,12},{9,13},{10,... | collective-permute-start | bytes 786440 | tf_op jit(solution)/shard_map/ppermute | solution.py:130
  186.7 1.9 collective-permute-start.6
  188.6 2.3 collective-permute-start.3
  190.9 2.5 collective-permute-start
  194.4 4.0 %hist_next.3.refs_2_ = bf16[1024,128]{1,0:T(8,128)(2,1)S(1)} custom-call(s32[1,4608]{1,0:T(1,128)S(1)} %convert_element_type.39.bins_ref, bf16[4608,128]{1,0:T(8,128)(2,1)S(1)} %bitcast.12), custom_call_target="tpu_custom_call" | custom-call | flops 2415919104 | bytes 1179648 | tf_op jit(solution)/shard_map/hist_next/pallas_call | solution.py:199
  198.3 3.4 %collective-permute-start.11 = (bf16[1024,128]{1,0:T(8,128)(2,1)S(1)}, bf16[1024,128]{1,0:T(8,128)(2,1)S(1)}, u32[]{:S(2)}, u32[]{:S(2)}) collective-permute-start(bf16[1024,128]{1,0:T(8,128)(2,1)S(1)} %hist_next.3.refs_2_), channel_id=1, source_target_pairs={{0,4},{1,5},{2,6},{3,7},{4,0},{5,1},{6,2},{7,3},{8,12},{9,13},{10,... | collective-permute-start | bytes 786440 | tf_op jit(solution)/shard_map/ppermute | solution.py:130
  201.7 2.3 collective-permute-start.8
  204.0 3.3 %collective-permute-start.5 = (bf16[1024,128]{1,0:T(8,128)(2,1)S(1)}, bf16[1024,128]{1,0:T(8,128)(2,1)S(1)}, u32[]{:S(2)}, u32[]{:S(2)}) collective-permute-start(bf16[1024,128]{1,0:T(8,128)(2,1)S(1)} %hist_next.3.refs_2_), channel_id=1, source_target_pairs={{0,6},{1,7},{2,0},{3,1},{4,2},{5,3},{6,4},{7,5},{8,14},{9,15},{10,... | collective-permute-start | bytes 786440 | tf_op jit(solution)/shard_map/ppermute | solution.py:130
  207.4 18.1 %all-to-all-done.1 = bf16[64,72,128]{2,1,0:T(8,128)(2,1)} async-done(((bf16[64,72,128]{2,1,0:T(8,128)(2,1)}), bf16[64,72,128]{2,1,0:T(8,128)(2,1)}, u32[]{:S(2)}, u32[]{:S(2)}) %all-to-all-start.1) | async-done | bytes 1179680 | tf_op jit(solution)/shard_map/all_to_all | solution.py:134
  225.5 5.3 %hist_next.2.refs_1_ = bf16[1024,128]{1,0:T(8,128)(2,1)S(1)} custom-call(s32[1,4608]{1,0:T(1,128)S(1)} %convert_element_type.39.bins_ref, bf16[4608,128]{1,0:T(8,128)(2,1)} %bitcast.6.rows_ref), custom_call_target="tpu_custom_call" | custom-call | flops 2415919104 | bytes 1179648 | tf_op jit(solution)/shard_map/hist_next/pallas_call | solution.py:199
  230.8 3.3 %collective-permute-start.10 = (bf16[1024,128]{1,0:T(8,128)(2,1)S(1)}, bf16[1024,128]{1,0:T(8,128)(2,1)S(1)}, u32[]{:S(2)}, u32[]{:S(2)}) collective-permute-start(bf16[1024,128]{1,0:T(8,128)(2,1)S(1)} %hist_next.2.refs_1_), channel_id=1, source_target_pairs={{0,4},{1,5},{2,6},{3,7},{4,0},{5,1},{6,2},{7,3},{8,12},{9,13},{10,... | collective-permute-start | bytes 786440 | tf_op jit(solution)/shard_map/ppermute | solution.py:130
  234.2 3.8 %collective-permute-start.7 = (bf16[1024,128]{1,0:T(8,128)(2,1)S(1)}, bf16[1024,128]{1,0:T(8,128)(2,1)S(1)}, u32[]{:S(2)}, u32[]{:S(2)}) collective-permute-start(bf16[1024,128]{1,0:T(8,128)(2,1)S(1)} %hist_next.2.refs_1_), channel_id=1, source_target_pairs={{0,5},{1,6},{2,7},{3,0},{4,1},{5,2},{6,3},{7,4},{8,13},{9,14},{10,... | collective-permute-start | bytes 786440 | tf_op jit(solution)/shard_map/ppermute | solution.py:130
  238.0 2.7 collective-permute-start.4
  241.0 2.4 collective-permute-done.10.refs_13_
  243.4 6.8 %collective-permute-done.7.refs_10_ = bf16[1024,128]{1,0:T(8,128)(2,1)S(1)} collective-permute-done((bf16[1024,128]{1,0:T(8,128)(2,1)S(1)}, bf16[1024,128]{1,0:T(8,128)(2,1)S(1)}, u32[]{:S(2)}, u32[]{:S(2)}) %collective-permute-start.7) | collective-permute-done | bytes 262176 | tf_op jit(solution)/shard_map/ppermute | solution.py:130
  250.2 2.4 collective-permute-done.4.refs_7_
  252.5 1.9 collective-permute-done.1.refs_4_
  254.5 3.7 %gram.1 = bf16[4,96,1920]{2,1,0:T(8,128)(2,1)S(1)} custom-call(f32[1024,1]{1,0:T(8,128)S(1)} %copy-done.7, bf16[384,384]{1,0:T(8,128)(2,1)S(1)} %copy-done.5, bf16[1024,128]{1,0:T(8,128)(2,1)} %get-tuple-element.10.refs_0_, bf16[1024,128]{1,0:T(8,128)(2,1)S(1)} %hist_next.2.refs_1_, bf16[1024,128]{1,0:T(8,128)(2,1)S(1)} %hist_next.3.refs_2_, ...), custom_call_target="tpu_custom_call" | custom-call | flops 1811939328 | bytes 3932160 | tf_op jit(solution)/shard_map/gram/pallas_call | solution.py:218
  258.2 24.0 %all_to_all.26 = bf16[4,96,1920]{2,1,0:T(8,128)(2,1)S(1)} all-to-all(bf16[4,96,1920]{2,1,0:T(8,128)(2,1)S(1)} %gram.1), channel_id=1, replica_groups=mesh['bins_0'=16,'bins_1'=4,'params'=8] {'bins_1'}, dimensions={0} | all-to-all | bytes 2949120 | tf_op jit(solution)/shard_map/all_to_all | solution.py:134
  282.6 29.9 %all_to_all.27 = bf16[16,6,1920]{2,1,0:T(8,128)(2,1)S(1)} all-to-all(bf16[16,6,1920]{2,1,0:T(8,128)(2,1)S(1)} %reshape.67), channel_id=1, replica_groups=mesh['bins_0'=16,'bins_1'=4,'params'=8] {'bins_0'}, dimensions={0} | all-to-all | bytes 737280 | tf_op jit(solution)/shard_map/all_to_all | solution.py:134
  (51 shorter events, 9.3 us)
Async XLA Ops:
  1.0 1.7 copy-start
  2.6 24.6 %copy-start.8 = (s32[3072]{0:T(1024)S(1)}, s32[3072]{0:T(1024)}, u32[]{:S(2)}) copy-start(s32[3072]{0:T(1024)} %param.6) | copy-start | bytes 36868
  7.3 1.0 copy-start.3
  8.3 19.8 %copy-start.1 = (bf16[3072,384]{1,0:T(8,128)(2,1)S(1)}, bf16[3072,384]{1,0:T(8,128)(2,1)}, u32[]{:S(2)}) copy-start(bf16[3072,384]{1,0:T(8,128)(2,1)} %w_ref.3) | copy-start | bytes 7077892
  8.3 79.8 %all-to-all-start.2 = ((bf16[64,72,128]{2,1,0:T(8,128)(2,1)}), bf16[64,72,128]{2,1,0:T(8,128)(2,1)S(1)}, u32[]{:S(2)}, u32[]{:S(2)}) async-start(bf16[64,72,128]{2,1,0:T(8,128)(2,1)} %copy-done.3), calls=%async_computation.2 | async-start | bytes 2359296 | tf_op jit(solution)/shard_map/all_to_all | solution.py:134
  31.7 1.1 copy-start.2
  159.9 6.2 %copy-start.9 = (f32[1024]{0:T(1024)S(1)}, f32[1024]{0:T(1024)}, u32[]{:S(2)}) copy-start(f32[1024]{0:T(1024)} %param.9) | copy-start | bytes 12292
  159.9 6.4 %copy-start.10 = (f32[1024]{0:T(1024)S(1)}, f32[1024]{0:T(1024)}, u32[]{:S(2)}) copy-start(f32[1024]{0:T(1024)} %param.10) | copy-start | bytes 12292
  159.9 65.6 %all-to-all-start.1 = ((bf16[64,72,128]{2,1,0:T(8,128)(2,1)}), bf16[64,72,128]{2,1,0:T(8,128)(2,1)}, u32[]{:S(2)}, u32[]{:S(2)}) async-start(bf16[64,72,128]{2,1,0:T(8,128)(2,1)} %get-tuple-element.11), calls=%async_computation.1 | async-start | bytes 2359296 | tf_op jit(solution)/shard_map/all_to_all | solution.py:134
  173.8 0.7 copy-start.4
  182.6 0.8 copy-start.6
  183.4 18.4 %collective-permute-start.9 = (bf16[1024,128]{1,0:T(8,128)(2,1)}, bf16[1024,128]{1,0:T(8,128)(2,1)S(1)}, u32[]{:S(2)}, u32[]{:S(2)}) collective-permute-start(bf16[1024,128]{1,0:T(8,128)(2,1)} %get-tuple-element.10.refs_0_), channel_id=1, source_target_pairs={{0,4},{1,5},{2,6},{3,7},{4,0},{5,1},{6,2},{7,3},{8,12},{9,13},{10,... | collective-permute-start | bytes 786440 | tf_op jit(solution)/shard_map/ppermute | solution.py:130
  186.7 17.3 %collective-permute-start.6 = (bf16[1024,128]{1,0:T(8,128)(2,1)}, bf16[1024,128]{1,0:T(8,128)(2,1)S(1)}, u32[]{:S(2)}, u32[]{:S(2)}) collective-permute-start(bf16[1024,128]{1,0:T(8,128)(2,1)} %get-tuple-element.10.refs_0_), channel_id=1, source_target_pairs={{0,5},{1,6},{2,7},{3,0},{4,1},{5,2},{6,3},{7,4},{8,13},{9,14},{10,... | collective-permute-start | bytes 786440 | tf_op jit(solution)/shard_map/ppermute | solution.py:130
  188.6 42.2 %collective-permute-start.3 = (bf16[1024,128]{1,0:T(8,128)(2,1)}, bf16[1024,128]{1,0:T(8,128)(2,1)S(1)}, u32[]{:S(2)}, u32[]{:S(2)}) collective-permute-start(bf16[1024,128]{1,0:T(8,128)(2,1)} %get-tuple-element.10.refs_0_), channel_id=1, source_target_pairs={{0,6},{1,7},{2,0},{3,1},{4,2},{5,3},{6,4},{7,5},{8,14},{9,15},{10,... | collective-permute-start | bytes 786440 | tf_op jit(solution)/shard_map/ppermute | solution.py:130
  190.9 39.9 %collective-permute-start = (bf16[1024,128]{1,0:T(8,128)(2,1)}, bf16[1024,128]{1,0:T(8,128)(2,1)S(1)}, u32[]{:S(2)}, u32[]{:S(2)}) collective-permute-start(bf16[1024,128]{1,0:T(8,128)(2,1)} %get-tuple-element.10.refs_0_), channel_id=1, source_target_pairs={{0,7},{1,0},{2,1},{3,2},{4,3},{5,4},{6,5},{7,6},{8,15},{9,8},{10,9... | collective-permute-start | bytes 786440 | tf_op jit(solution)/shard_map/ppermute | solution.py:130
  198.3 35.8 %collective-permute-start.11 = (bf16[1024,128]{1,0:T(8,128)(2,1)S(1)}, bf16[1024,128]{1,0:T(8,128)(2,1)S(1)}, u32[]{:S(2)}, u32[]{:S(2)}) collective-permute-start(bf16[1024,128]{1,0:T(8,128)(2,1)S(1)} %hist_next.3.refs_2_), channel_id=1, source_target_pairs={{0,4},{1,5},{2,6},{3,7},{4,0},{5,1},{6,2},{7,3},{8,12},{9,13},{10,... | collective-permute-start | bytes 786440 | tf_op jit(solution)/shard_map/ppermute | solution.py:130
  201.7 36.3 %collective-permute-start.8 = (bf16[1024,128]{1,0:T(8,128)(2,1)S(1)}, bf16[1024,128]{1,0:T(8,128)(2,1)S(1)}, u32[]{:S(2)}, u32[]{:S(2)}) collective-permute-start(bf16[1024,128]{1,0:T(8,128)(2,1)S(1)} %hist_next.3.refs_2_), channel_id=1, source_target_pairs={{0,5},{1,6},{2,7},{3,0},{4,1},{5,2},{6,3},{7,4},{8,13},{9,14},{10,... | collective-permute-start | bytes 786440 | tf_op jit(solution)/shard_map/ppermute | solution.py:130
  204.0 36.8 %collective-permute-start.5 = (bf16[1024,128]{1,0:T(8,128)(2,1)S(1)}, bf16[1024,128]{1,0:T(8,128)(2,1)S(1)}, u32[]{:S(2)}, u32[]{:S(2)}) collective-permute-start(bf16[1024,128]{1,0:T(8,128)(2,1)S(1)} %hist_next.3.refs_2_), channel_id=1, source_target_pairs={{0,6},{1,7},{2,0},{3,1},{4,2},{5,3},{6,4},{7,5},{8,14},{9,15},{10,... | collective-permute-start | bytes 786440 | tf_op jit(solution)/shard_map/ppermute | solution.py:130
  225.5 29.0 %copy-start.5 = (bf16[384,384]{1,0:T(8,128)(2,1)S(1)}, bf16[384,384]{1,0:T(8,128)(2,1)}, u32[]{:S(2)}) copy-start(bf16[384,384]{1,0:T(8,128)(2,1)} %constant.19.clone.order_ref) | copy-start | bytes 884740
  225.5 29.0 %copy-start.7 = (f32[1024,1]{1,0:T(8,128)S(1)}, f32[1024,1]{1,0:T(8,128)}, u32[]{:S(2)}) copy-start(f32[1024,1]{1,0:T(8,128)} %copy-done.6) | copy-start | bytes 12292
  230.8 10.2 %collective-permute-start.2 = (bf16[1024,128]{1,0:T(8,128)(2,1)S(1)}, bf16[1024,128]{1,0:T(8,128)(2,1)S(1)}, u32[]{:S(2)}, u32[]{:S(2)}) collective-permute-start(bf16[1024,128]{1,0:T(8,128)(2,1)S(1)} %hist_next.3.refs_2_), channel_id=1, source_target_pairs={{0,7},{1,0},{2,1},{3,2},{4,3},{5,4},{6,5},{7,6},{8,15},{9,8},{10,9... | collective-permute-start | bytes 786440 | tf_op jit(solution)/shard_map/ppermute | solution.py:130
  230.8 12.5 %collective-permute-start.10 = (bf16[1024,128]{1,0:T(8,128)(2,1)S(1)}, bf16[1024,128]{1,0:T(8,128)(2,1)S(1)}, u32[]{:S(2)}, u32[]{:S(2)}) collective-permute-start(bf16[1024,128]{1,0:T(8,128)(2,1)S(1)} %hist_next.2.refs_1_), channel_id=1, source_target_pairs={{0,4},{1,5},{2,6},{3,7},{4,0},{5,1},{6,2},{7,3},{8,12},{9,13},{10,... | collective-permute-start | bytes 786440 | tf_op jit(solution)/shard_map/ppermute | solution.py:130
  234.2 16.0 %collective-permute-start.7 = (bf16[1024,128]{1,0:T(8,128)(2,1)S(1)}, bf16[1024,128]{1,0:T(8,128)(2,1)S(1)}, u32[]{:S(2)}, u32[]{:S(2)}) collective-permute-start(bf16[1024,128]{1,0:T(8,128)(2,1)S(1)} %hist_next.2.refs_1_), channel_id=1, source_target_pairs={{0,5},{1,6},{2,7},{3,0},{4,1},{5,2},{6,3},{7,4},{8,13},{9,14},{10,... | collective-permute-start | bytes 786440 | tf_op jit(solution)/shard_map/ppermute | solution.py:130
  238.0 14.5 %collective-permute-start.4 = (bf16[1024,128]{1,0:T(8,128)(2,1)S(1)}, bf16[1024,128]{1,0:T(8,128)(2,1)S(1)}, u32[]{:S(2)}, u32[]{:S(2)}) collective-permute-start(bf16[1024,128]{1,0:T(8,128)(2,1)S(1)} %hist_next.2.refs_1_), channel_id=1, source_target_pairs={{0,6},{1,7},{2,0},{3,1},{4,2},{5,3},{6,4},{7,5},{8,14},{9,15},{10,... | collective-permute-start | bytes 786440 | tf_op jit(solution)/shard_map/ppermute | solution.py:130
  240.8 13.7 %collective-permute-start.1 = (bf16[1024,128]{1,0:T(8,128)(2,1)S(1)}, bf16[1024,128]{1,0:T(8,128)(2,1)S(1)}, u32[]{:S(2)}, u32[]{:S(2)}) collective-permute-start(bf16[1024,128]{1,0:T(8,128)(2,1)S(1)} %hist_next.2.refs_1_), channel_id=1, source_target_pairs={{0,7},{1,0},{2,1},{3,2},{4,3},{5,4},{6,5},{7,6},{8,15},{9,8},{10,9... | collective-permute-start | bytes 786440 | tf_op jit(solution)/shard_map/ppermute | solution.py:130

commit v2 on v1

--- a/solution.py
+++ b/solution.py
@@ -57,37 +57,38 @@
     lax.fori_loop(0, owners, one, 0, unroll=4)
 
 
-def pack_rest(owners, events, starts_ref, w_ref, *out_refs):
-    def one(o, _):
-        start = starts_ref[o]
-        rows = pick_rows(start, w_ref, events, slice(COLS, 3 * COLS)).astype(jnp.bfloat16)
-        for i, out_ref in enumerate(out_refs):
-            out_ref[o] = rows[:, i * COLS : (i + 1) * COLS]
+def pack_rest(n0, n1, events, place_ref, starts_ref, w_ref, *out_refs):
+    def one(z, _):
+        for turn, out_ref in enumerate(out_refs):
+            start = starts_ref[z * n1 + lax.rem(place_ref[0] + turn, n1)]
+            rows = pick_rows(start, w_ref, events, slice(COLS, 3 * COLS)).astype(jnp.bfloat16)
+            for i in range(out_ref.shape[0]):
+                out_ref[i, z] = rows[:, i * COLS : (i + 1) * COLS]
         return 0
 
-    lax.fori_loop(0, owners, one, 0, unroll=4)
-
-
-def one_hot_of(bins_ref, at, bins_dev):
-    ids = lax.broadcasted_iota(jnp.int32, (bins_dev, KB), 0)
-    return jnp.where(ids == bins_ref[:, pl.ds(at, KB)], 1.0, 0.0).astype(jnp.bfloat16)
-
-
-def hist_first(bins_ref, nominal_ref, rows_ref, background_ref, observed_ref, out_ref, curve_ref, acc, acc_n):
+    lax.fori_loop(0, n0, one, 0)
+
+
+def one_hot_of(bins_ref, at, size, bins_dev):
+    ids = lax.broadcasted_iota(jnp.int32, (bins_dev, size), 0)
+    return jnp.where(ids == bins_ref[:, pl.ds(at, size)], 1.0, 0.0).astype(jnp.bfloat16)
+
+
+def hist_first(bins_ref, nominal_ref, background_ref, observed_ref, *refs):
+    rows_refs, (out_ref, curve_ref, acc, acc_n) = refs[:-4], refs[-4:]
     bins_dev = out_ref.shape[0]
     acc[...] = jnp.zeros_like(acc)
     acc_n[...] = jnp.zeros_like(acc_n)
-
-    def one(i, _):
-        at = pl.multiple_of(i * KB, KB)
-        hot = one_hot_of(bins_ref, at, bins_dev)
-        acc[...] += jnp.dot(hot, rows_ref[pl.ds(at, KB), :], preferred_element_type=jnp.float32)
+    size = rows_refs[0].shape[0]
+    for i, rows_ref in enumerate(rows_refs):
+        hot = one_hot_of(bins_ref, i * size, size, bins_dev)
+        acc[...] += jnp.dot(hot, rows_ref[...], preferred_element_type=jnp.float32)
         acc_n[...] += lax.dot_general(
-            hot, nominal_ref[:, pl.ds(at, KB)], (((1,), (1,)), ((), ())), preferred_element_type=jnp.float32
+            hot,
+            nominal_ref[:, i * size : (i + 1) * size],
+            (((1,), (1,)), ((), ())),
+            preferred_element_type=jnp.float32,
         )
-        return 0
-
-    lax.fori_loop(0, rows_ref.shape[0] // KB, one, 0)
     out_ref[...] = acc[...].astype(jnp.bfloat16)
     yields = background_ref[...] + acc_n[:, 0:1]
     curve_ref[...] = observed_ref[...] / (yields * yields)
@@ -99,7 +100,7 @@
 
     def one(i, _):
         at = pl.multiple_of(i * KB, KB)
-        hot = one_hot_of(bins_ref, at, bins_dev)
+        hot = one_hot_of(bins_ref, at, KB, bins_dev)
         acc[...] += jnp.dot(hot, rows_ref[pl.ds(at, KB), :], preferred_element_type=jnp.float32)
         return 0
 
@@ -124,6 +125,25 @@
             out_ref[y, :, k * width : (k + 1) * width] = full[y * step : (y + 1) * step]
 
 
+def add_across(got_ref, out_ref, wide):
+    lanes = got_ref.shape[2] // 128
+    total = jnp.sum(got_ref[...].astype(jnp.float32), axis=0)
+    n0 = out_ref.shape[0]
+    lines = total.shape[0] // n0
+    wide[...] = jnp.zeros_like(wide)
+    for z in range(n0):
+        for j in range(lanes):
+            wide[z, j * lines : (j + 1) * lines] = total[z * lines : (z + 1) * lines, j * 128 : (j + 1) * 128]
+    out_ref[...] = wide[...].astype(jnp.bfloat16)
+
+
+def add_along(scale, got_ref, out_ref):
+    lines = out_ref.shape[0]
+    total = jnp.sum(got_ref[...].astype(jnp.float32), axis=0) * scale
+    for j in range(out_ref.shape[1] // 128):
+        out_ref[:, j * 128 : (j + 1) * 128] = total[j * lines : (j + 1) * lines]
+
+
 def from_behind(value, axis, steps):
     count = lax.axis_size(axis)
     pairs = [(source, (source + steps) % count) for source in range(count)]
@@ -148,7 +168,8 @@
     info = jnp.concatenate([info, jnp.zeros((6, events), f32)])
 
     slab = CAP + EXTRA
-    send0 = pl.pallas_call(
+    place = lax.axis_index(BINS[1])
+    send_a = pl.pallas_call(
         functools.partial(pack_first, owners, bins_dev, events),
         out_shape=jax.ShapeDtypeStruct((owners, slab, COLS), bf16),
         in_specs=[SMEM, VMEM, VMEM],
@@ -157,30 +178,34 @@
         cost_estimate=cost(2 * owners * CAP * WIN * COLS, 2 * owners * slab * COLS * 2),
         name="pack_first",
     )(starts, info, event_weights)
-    rest = pl.pallas_call(
-        functools.partial(pack_rest, owners, events),
-        out_shape=[jax.ShapeDtypeStruct((owners, CAP, COLS), bf16)] * (chunks - 1),
-        in_specs=[SMEM, VMEM],
-        out_specs=[VMEM] * (chunks - 1),
+    send_b = pl.pallas_call(
+        functools.partial(pack_rest, n0, n1, events),
+        out_shape=[jax.ShapeDtypeStruct((chunks - 1, n0, CAP, COLS), bf16)] * n1,
+        in_specs=[SMEM, SMEM, VMEM],
+        out_specs=[VMEM] * n1,
         compiler_params=PARAMS,
         cost_estimate=cost(4 * owners * CAP * WIN * COLS, 4 * owners * CAP * COLS * 2),
         name="pack_rest",
-    )(starts, event_weights)
-    got0 = exchange(send0, BINS)
-    got = [exchange(s, BINS) for s in rest]
-
-    extra = got0[:, CAP:, :CAP].astype(f32)
-    local = (extra[:, 0] * 32.0 + extra[:, 1]).astype(jnp.int32)
-    local_wide = jnp.pad(local, ((0, 0), (0, EXTRA)), constant_values=-1).reshape(1, owners * slab)
-    local = local.reshape(1, owners * CAP)
-    nom = jnp.pad(extra[:, 2], ((0, 0), (0, EXTRA))).astype(bf16).reshape(1, owners * slab)
+    )(place.reshape(1).astype(jnp.int32), starts, event_weights)
+    got_a = exchange(send_a.reshape(n0, n1 * slab, COLS), BINS[0]).reshape(n0, n1, slab, COLS)
+    mid_b = [from_behind(send_b[t], BINS[1], t) if t else send_b[0] for t in range(n1)]
+    got = [exchange(jnp.stack([m[i] for m in mid_b], axis=1), BINS[0]) for i in range(chunks - 1)]
+    pieces = [lax.dynamic_index_in_dim(got_a, lax.rem(place + t, n1), 1, keepdims=False) for t in range(n1)]
+    pieces = [from_behind(x, BINS[1], t) if t else x for t, x in enumerate(pieces)]
+
+    extra = jnp.stack([x[:, CAP:, :CAP] for x in pieces]).astype(f32)
+    local = (extra[:, :, 0] * 32.0 + extra[:, :, 1]).astype(jnp.int32)
+    tail = ((0, 0), (0, 0), (0, EXTRA))
+    local_wide = jnp.pad(local, tail, constant_values=-1).reshape(1, owners * slab)
+    local = jnp.swapaxes(local, 0, 1).reshape(1, owners * CAP)
+    nom = jnp.pad(extra[:, :, 2], tail).astype(bf16).reshape(1, owners * slab)
     nom = jnp.broadcast_to(nom, (8, owners * slab))
     tile = jax.ShapeDtypeStruct((bins_dev, COLS), bf16)
     acc = pltpu.VMEM((bins_dev, COLS), f32)
     first, curve = pl.pallas_call(
         hist_first,
         out_shape=[tile, jax.ShapeDtypeStruct((bins_dev, 1), f32)],
-        in_specs=[VMEM] * 5,
+        in_specs=[VMEM] * (4 + n1),
         out_specs=[VMEM] * 2,
         scratch_shapes=[acc, pltpu.VMEM((bins_dev, 8), f32)],
         compiler_params=PARAMS,
@@ -189,9 +214,9 @@
     )(
         local_wide,
         nom,
-        got0.reshape(owners * slab, COLS),
         background.reshape(bins_dev, 1),
         observed.reshape(bins_dev, 1),
+        *[x.reshape(n0 * slab, COLS) for x in pieces],
     )
     tiles = [first]
     for g in got:
@@ -224,9 +249,24 @@
         cost_estimate=cost(2 * bins_dev * width * width * (turns + 1), turns * width * bins_dev * 2),
         name="gram",
     )(curve, jnp.asarray(order, bf16), *[t for row in moved for t in row])
-    across = exchange(partial, BINS[1]).astype(f32).sum(axis=0).astype(bf16)
-    along = exchange(across.reshape(n0, lines, turns * width), BINS[0]).astype(f32).sum(axis=0)
-    return along * (1.0 / (bins_dev * owners))
+    packed = -(-lines * turns * width // 128 // 16) * 16
+    across = pl.pallas_call(
+        add_across,
+        out_shape=jax.ShapeDtypeStruct((n0, packed, 128), bf16),
+        in_specs=[VMEM],
+        out_specs=VMEM,
+        scratch_shapes=[pltpu.VMEM((n0, packed, 128), f32)],
+        compiler_params=PARAMS,
+        name="add_across",
+    )(exchange(partial, BINS[1]))
+    return pl.pallas_call(
+        functools.partial(add_along, 1.0 / (bins_dev * owners)),
+        out_shape=jax.ShapeDtypeStruct((lines, turns * width), f32),
+        in_specs=[VMEM],
+        out_specs=VMEM,
+        compiler_params=PARAMS,
+        name="add_along",
+    )(exchange(across, BINS[0]))
 
 
 def solution(mesh):

time: 317 us -> 331 us (1.044)
  blocking collectives: 126 us -> 60.4 us
  waiting for transfers between devices: 86.9 us -> 133 us
  starting transfers between devices: 54.3 us -> 82.8 us
  local copies, waits for them, and re-layouts: 10.9 us -> 20.2 us
    all_to_all x3 -> x2, blocking collectives: 126 us -> 60.4 us  [exchange(): return lax.all_to_all(value, axis, split_axis=0, concat_axis=0, tiled=True)]
    ppermute x12 -> x18, waiting for transfers between devices: 13.5 us -> 54.2 us  [from_behind(): return lax.ppermute(value, axis, pairs)]
    ppermute x12 -> x18, starting transfers between devices: 29.2 us -> 52.7 us  [from_behind(): return lax.ppermute(value, axis, pairs)]
    unnamed x23 -> x39, local copies, waits for them, and re-layouts: 5.32 us -> 12.9 us
    all_to_all x2 -> x3, waiting for transfers between devices: 73.4 us -> 78.6 us  [exchange(): return lax.all_to_all(value, axis, split_axis=0, concat_axis=0, tiled=True)]
    all_to_all x2 -> x3, starting transfers between devices: 25.1 us -> 30.1 us  [exchange(): return lax.all_to_all(value, axis, split_axis=0, concat_axis=0, tiled=True)]
    another operation x0 -> x10, local copies, waits for them, and re-layouts: none -> 3.96 us  [the longest x6 2.43 us: body(): jnp.stack([m[i] for m in mid_b], axis=1)]
  transfers between devices with their start and end apart: 14 -> 21, of which waited for: 6 -> 15; matrix products, arithmetic and copies ran while one was open for 3% -> 3% of each run, Pallas kernels for 7% -> 6%
where the time goes in v2:
time: 331 us; the launch traced here: 330 us
  waiting for transfers between devices  133 us (40%)
  starting transfers between devices  82.8 us (25%)
  blocking collectives  60.4 us (18%)
  Pallas kernels  28.3 us (9%)
  local copies, waits for them, and re-layouts  20.2 us (6%)
  other arithmetic  4.59 us (1%)
    all_to_all x3, waiting for transfers between devices, exchange(): return lax.all_to_all(value, axis, split_axis=0, concat_axis=0, tiled=True)  78.6 us
    all_to_all x2, blocking collectives, exchange(): return lax.all_to_all(value, axis, split_axis=0, concat_axis=0, tiled=True)  60.4 us
    ppermute x18, waiting for transfers between devices, from_behind(): return lax.ppermute(value, axis, pairs)  54.2 us
    ppermute x18, starting transfers between devices, from_behind(): return lax.ppermute(value, axis, pairs)  52.7 us
    all_to_all x3, starting transfers between devices, exchange(): return lax.all_to_all(value, axis, split_axis=0, concat_axis=0, tiled=True)  30.1 us
    unnamed x39, local copies, waits for them, and re-layouts  12.9 us
    pallas_call x2, Pallas kernels, body(): pl.pallas_call(hist_next, out_shape=tile, in_specs=[VMEM] * 2, out_specs=...  8.67 us
    pallas_call x1, Pallas kernels, body(): pl.pallas_call(hist_first, out_shape=[tile, jax.ShapeDtypeStruct((bins_de...  7.46 us
  transfers between devices with their start and end apart: 21, of which 15 were waited for; matrix products, arithmetic and copies ran while one was open for 3% of the time, Pallas kernels for 6%

profile of v2, /device:TPU:6, one launch (start us, length us, event | category | flops | bytes accessed | tf_op | source)
XLA Modules:
  0.0 329.5 jit_solution(3011205185131365255)
XLA Ops:
  4.2 3.6 %pack_first.1 = bf16[64,80,128]{2,1,0:T(8,128)(2,1)S(1)} custom-call(s32[64]{0:T(128)S(1)} %convert_reduce_fusion.starts_ref, f32[8,3072]{1,0:T(8,128)S(1)} %maximum_maximum_fusion.info_ref, bf16[3072,384]{1,0:T(8,128)(2,1)S(1)} %copy-done), custom_call_target="tpu_custom_call" | custom-call | flops 113246208 | bytes 2621440 | tf_op jit(solution)/shard_map/pack_first/pallas_call | solution.py:172
  8.9 15.4 %all-to-all-start = ((bf16[16,320,128]{2,1,0:T(8,128)(2,1)}), bf16[16,320,128]{2,1,0:T(8,128)(2,1)}, u32[]{:S(2)}, u32[]{:S(2)}) async-start(bf16[16,320,128]{2,1,0:T(8,128)(2,1)} %bitcast.50), calls=%async_computation | async-start | bytes 2621440 | tf_op jit(solution)/shard_map/all_to_all | solution.py:154
  24.3 3.7 %pack_rest.1 = (bf16[2,16,72,128]{3,2,1,0:T(8,128)(2,1)S(1)}, bf16[2,16,72,128]{3,2,1,0:T(8,128)(2,1)S(1)}, bf16[2,16,72,128]{3,2,1,0:T(8,128)(2,1)S(1)}, bf16[2,16,72,128]{3,2,1,0:T(8,128)(2,1)S(1)}) custom-call(s32[1]{0:T(128)} %bitcast.20.place_ref, s32[64]{0:T(128)S(1)} %convert_reduce_fusion.starts_ref, bf16[3072,384]{1,0:T(8,128)(2,1)S(1)} %copy-done.1), custom_call_target="tpu_custom_call" | custom-call | flops 226492416 | bytes 4718592 | tf_op jit(solution)/shard_map/pack_rest/pallas_call | solution.py:181
  28.0 3.5 %collective-permute-start.3 = (bf16[2,16,72,128]{3,2,1,0:T(8,128)(2,1)S(1)}, bf16[2,16,72,128]{3,2,1,0:T(8,128)(2,1)S(1)}, u32[]{:S(2)}, u32[]{:S(2)}) collective-permute-start(bf16[2,16,72,128]{3,2,1,0:T(8,128)(2,1)S(1)} %get-tuple-element.14), channel_id=1, source_target_pairs={{0,8},{8,16},{16,24},{24,0},{1,9},{9,17},{17,25},{25,1},{2,10},{10... | collective-permute-start | bytes 1769480 | tf_op jit(solution)/shard_map/ppermute | solution.py:150
  31.5 4.8 %collective-permute-start.4 = (bf16[2,16,72,128]{3,2,1,0:T(8,128)(2,1)S(1)}, bf16[2,16,72,128]{3,2,1,0:T(8,128)(2,1)S(1)}, u32[]{:S(2)}, u32[]{:S(2)}) collective-permute-start(bf16[2,16,72,128]{3,2,1,0:T(8,128)(2,1)S(1)} %get-tuple-element.15), channel_id=1, source_target_pairs={{0,16},{8,24},{16,0},{24,8},{1,17},{9,25},{17,1},{25,9},{2,18},{10... | collective-permute-start | bytes 1769480 | tf_op jit(solution)/shard_map/ppermute | solution.py:150
  36.3 3.3 collective-permute-start.5
  39.6 6.6 %collective-permute-done.3 = bf16[2,16,72,128]{3,2,1,0:T(8,128)(2,1)S(1)} collective-permute-done((bf16[2,16,72,128]{3,2,1,0:T(8,128)(2,1)S(1)}, bf16[2,16,72,128]{3,2,1,0:T(8,128)(2,1)S(1)}, u32[]{:S(2)}, u32[]{:S(2)}) %collective-permute-start.3) | collective-permute-done | bytes 589856 | tf_op jit(solution)/shard_map/ppermute | solution.py:150
  46.3 13.5 %collective-permute-done.4 = bf16[2,16,72,128]{3,2,1,0:T(8,128)(2,1)S(1)} collective-permute-done((bf16[2,16,72,128]{3,2,1,0:T(8,128)(2,1)S(1)}, bf16[2,16,72,128]{3,2,1,0:T(8,128)(2,1)S(1)}, u32[]{:S(2)}, u32[]{:S(2)}) %collective-permute-start.4) | collective-permute-done | bytes 589856 | tf_op jit(solution)/shard_map/ppermute | solution.py:150
  62.5 24.7 %all-to-all-done = bf16[16,320,128]{2,1,0:T(8,128)(2,1)} async-done(((bf16[16,320,128]{2,1,0:T(8,128)(2,1)}), bf16[16,320,128]{2,1,0:T(8,128)(2,1)}, u32[]{:S(2)}, u32[]{:S(2)}) %all-to-all-start) | async-done | bytes 1310752 | tf_op jit(solution)/shard_map/all_to_all | solution.py:154
  87.2 6.2 %all-to-all-start.2 = ((bf16[16,4,72,128]{3,2,1,0:T(8,128)(2,1)}), bf16[16,4,72,128]{3,2,1,0:T(8,128)(2,1)S(1)}, u32[]{:S(2)}, u32[]{:S(2)}) async-start(bf16[16,4,72,128]{3,2,1,0:T(8,128)(2,1)} %copy.36), calls=%async_computation.2 | async-start | bytes 2359296 | tf_op jit(solution)/shard_map/all_to_all | solution.py:154
  94.7 53.9 %all-to-all-done.2 = bf16[16,4,72,128]{3,2,1,0:T(8,128)(2,1)S(1)} async-done(((bf16[16,4,72,128]{3,2,1,0:T(8,128)(2,1)}), bf16[16,4,72,128]{3,2,1,0:T(8,128)(2,1)S(1)}, u32[]{:S(2)}, u32[]{:S(2)}) %all-to-all-start.2) | async-done | bytes 1179680 | tf_op jit(solution)/shard_map/all_to_all | solution.py:154
  148.6 8.5 %all-to-all-start.1 = ((bf16[16,4,72,128]{3,2,1,0:T(8,128)(2,1)}), bf16[16,4,72,128]{3,2,1,0:T(8,128)(2,1)S(1)}, u32[]{:S(2)}, u32[]{:S(2)}) async-start(bf16[16,4,72,128]{3,2,1,0:T(8,128)(2,1)} %copy.35), calls=%async_computation.1 | async-start | bytes 2359296 | tf_op jit(solution)/shard_map/all_to_all | solution.py:154
  159.5 4.9 %collective-permute-start.2 = (bf16[16,80,128]{2,1,0:T(8,128)(2,1)}, bf16[16,80,128]{2,1,0:T(8,128)(2,1)}, u32[]{:S(2)}, u32[]{:S(2)}) collective-permute-start(bf16[16,80,128]{2,1,0:T(8,128)(2,1)} %get-tuple-element.18), channel_id=1, source_target_pairs={{0,24},{8,0},{16,8},{24,16},{1,25},{9,1},{17,9},{25,17},{2,26},{10... | collective-permute-start | bytes 983048 | tf_op jit(solution)/shard_map/ppermute | solution.py:150
  168.2 2.9 collective-permute-start
  171.1 7.5 %collective-permute-done.2 = bf16[16,80,128]{2,1,0:T(8,128)(2,1)} collective-permute-done((bf16[16,80,128]{2,1,0:T(8,128)(2,1)}, bf16[16,80,128]{2,1,0:T(8,128)(2,1)}, u32[]{:S(2)}, u32[]{:S(2)}) %collective-permute-start.2) | collective-permute-done | bytes 327712 | tf_op jit(solution)/shard_map/ppermute | solution.py:150
  180.1 4.5 %collective-permute-done = bf16[16,80,128]{2,1,0:T(8,128)(2,1)S(1)} collective-permute-done((bf16[16,80,128]{2,1,0:T(8,128)(2,1)}, bf16[16,80,128]{2,1,0:T(8,128)(2,1)S(1)}, u32[]{:S(2)}, u32[]{:S(2)}) %collective-permute-start) | collective-permute-done | bytes 327712 | tf_op jit(solution)/shard_map/ppermute | solution.py:150
  190.4 7.5 %hist_first.1 = (bf16[1024,128]{1,0:T(8,128)(2,1)}, f32[1024,1]{1,0:T(8,128)S(1)}) custom-call(s32[1,5120]{1,0:T(1,128)S(1)} %reshape.54.bins_ref, bf16[8,5120]{1,0:T(8,128)(2,1)S(1)} %broadcast_in_dim.14.nominal_ref, f32[1024,1]{1,0:T(8,128)S(1)} %copy.32.background_ref, f32[1024,1]{1,0:T(8,128)S(1)} %copy.33.observed_ref, bf16[1280,128]{1,0:T(8,128)(2,1)S(1)} %bitcast.54, ...), custom_call_target="tpu_custom_call" | custom-call | flops 2684354560 | bytes 1310720 | tf_op jit(solution)/shard_map/hist_first/pallas_call | solution.py:205
  198.7 3.3 %collective-permute-start.15 = (bf16[1024,128]{1,0:T(8,128)(2,1)}, bf16[1024,128]{1,0:T(8,128)(2,1)S(1)}, u32[]{:S(2)}, u32[]{:S(2)}) collective-permute-start(bf16[1024,128]{1,0:T(8,128)(2,1)} %get-tuple-element.12.refs_0_), channel_id=1, source_target_pairs={{0,4},{1,5},{2,6},{3,7},{4,0},{5,1},{6,2},{7,3},{8,12},{9,13},{10,... | collective-permute-start | bytes 786440 | tf_op jit(solution)/shard_map/ppermute | solution.py:150
  202.0 3.4 %collective-permute-start.12 = (bf16[1024,128]{1,0:T(8,128)(2,1)}, bf16[1024,128]{1,0:T(8,128)(2,1)S(1)}, u32[]{:S(2)}, u32[]{:S(2)}) collective-permute-start(bf16[1024,128]{1,0:T(8,128)(2,1)} %get-tuple-element.12.refs_0_), channel_id=1, source_target_pairs={{0,5},{1,6},{2,7},{3,0},{4,1},{5,2},{6,3},{7,4},{8,13},{9,14},{10,... | collective-permute-start | bytes 786440 | tf_op jit(solution)/shard_map/ppermute | solution.py:150
  205.4 2.7 collective-permute-start.9
  208.9 4.7 %hist_next.3.refs_2_ = bf16[1024,128]{1,0:T(8,128)(2,1)} custom-call(s32[1,4608]{1,0:T(1,128)S(1)} %reshape.61.bins_ref, bf16[4608,128]{1,0:T(8,128)(2,1)S(1)} %bitcast.52), custom_call_target="tpu_custom_call" | custom-call | flops 2415919104 | bytes 1179648 | tf_op jit(solution)/shard_map/hist_next/pallas_call | solution.py:224
  213.6 3.4 %collective-permute-start.17 = (bf16[1024,128]{1,0:T(8,128)(2,1)}, bf16[1024,128]{1,0:T(8,128)(2,1)S(1)}, u32[]{:S(2)}, u32[]{:S(2)}) collective-permute-start(bf16[1024,128]{1,0:T(8,128)(2,1)} %hist_next.3.refs_2_), channel_id=1, source_target_pairs={{0,4},{1,5},{2,6},{3,7},{4,0},{5,1},{6,2},{7,3},{8,12},{9,13},{10,... | collective-permute-start | bytes 786440 | tf_op jit(solution)/shard_map/ppermute | solution.py:150
  217.0 3.1 collective-permute-start.14
  222.7 4.0 %hist_next.2.refs_1_ = bf16[1024,128]{1,0:T(8,128)(2,1)S(1)} custom-call(s32[1,4608]{1,0:T(1,128)S(1)} %reshape.61.bins_ref, bf16[4608,128]{1,0:T(8,128)(2,1)S(1)} %bitcast.51), custom_call_target="tpu_custom_call" | custom-call | flops 2415919104 | bytes 1179648 | tf_op jit(solution)/shard_map/hist_next/pallas_call | solution.py:224
  228.1 4.0 %collective-permute-start.16 = (bf16[1024,128]{1,0:T(8,128)(2,1)S(1)}, bf16[1024,128]{1,0:T(8,128)(2,1)S(1)}, u32[]{:S(2)}, u32[]{:S(2)}) collective-permute-start(bf16[1024,128]{1,0:T(8,128)(2,1)S(1)} %hist_next.2.refs_1_), channel_id=1, source_target_pairs={{0,4},{1,5},{2,6},{3,7},{4,0},{5,1},{6,2},{7,3},{8,12},{9,13},{10,... | collective-permute-start | bytes 786440 | tf_op jit(solution)/shard_map/ppermute | solution.py:150
  240.0 2.8 collective-permute-done.11.refs_8_
  245.6 2.8 collective-permute-done.8.refs_5_
  248.4 7.2 %collective-permute-done.16.refs_13_ = bf16[1024,128]{1,0:T(8,128)(2,1)S(1)} collective-permute-done((bf16[1024,128]{1,0:T(8,128)(2,1)S(1)}, bf16[1024,128]{1,0:T(8,128)(2,1)S(1)}, u32[]{:S(2)}, u32[]{:S(2)}) %collective-permute-start.16) | collective-permute-done | bytes 262176 | tf_op jit(solution)/shard_map/ppermute | solution.py:150
  255.8 3.9 %collective-permute-done.10.refs_7_ = bf16[1024,128]{1,0:T(8,128)(2,1)S(1)} collective-permute-done((bf16[1024,128]{1,0:T(8,128)(2,1)S(1)}, bf16[1024,128]{1,0:T(8,128)(2,1)S(1)}, u32[]{:S(2)}, u32[]{:S(2)}) %collective-permute-start.10) | collective-permute-done | bytes 262176 | tf_op jit(solution)/shard_map/ppermute | solution.py:150
  264.3 3.8 %gram.1 = bf16[4,96,1920]{2,1,0:T(8,128)(2,1)S(1)} custom-call(f32[1024,1]{1,0:T(8,128)S(1)} %copy-done.16, bf16[384,384]{1,0:T(8,128)(2,1)S(1)} %copy-done.14, bf16[1024,128]{1,0:T(8,128)(2,1)} %get-tuple-element.12.refs_0_, bf16[1024,128]{1,0:T(8,128)(2,1)S(1)} %hist_next.2.refs_1_, bf16[1024,128]{1,0:T(8,128)(2,1)} %hist_next.3.refs_2_, ...), custom_call_target="tpu_custom_call" | custom-call | flops 1811939328 | bytes 3932160 | tf_op jit(solution)/shard_map/gram/pallas_call | solution.py:243
  268.0 22.1 %all_to_all.25.got_ref = bf16[4,96,1920]{2,1,0:T(8,128)(2,1)S(1)} all-to-all(bf16[4,96,1920]{2,1,0:T(8,128)(2,1)S(1)} %gram.1), channel_id=1, replica_groups=mesh['bins_0'=16,'bins_1'=4,'params'=8] {'bins_1'}, dimensions={0} | all-to-all | bytes 2949120 | tf_op jit(solution)/shard_map/all_to_all | solution.py:154
  290.6 38.3 %all_to_all.26.got_ref = bf16[16,96,128]{2,1,0:T(8,128)(2,1)S(1)} all-to-all(bf16[16,96,128]{2,1,0:T(8,128)(2,1)S(1)} %add_across.1), channel_id=1, replica_groups=mesh['bins_0'=16,'bins_1'=4,'params'=8] {'bins_0'}, dimensions={0} | all-to-all | bytes 786432 | tf_op jit(solution)/shard_map/all_to_all | solution.py:154
  (91 shorter events, 44.8 us)
Async XLA Ops:
  2.5 1.7 copy-start
  7.8 1.1 copy-start.2
  8.9 15.4 %copy-start.1 = (bf16[3072,384]{1,0:T(8,128)(2,1)S(1)}, bf16[3072,384]{1,0:T(8,128)(2,1)}, u32[]{:S(2)}) copy-start(bf16[3072,384]{1,0:T(8,128)(2,1)} %w_ref.3) | copy-start | bytes 7077892
  8.9 78.3 %all-to-all-start = ((bf16[16,320,128]{2,1,0:T(8,128)(2,1)}), bf16[16,320,128]{2,1,0:T(8,128)(2,1)}, u32[]{:S(2)}, u32[]{:S(2)}) async-start(bf16[16,320,128]{2,1,0:T(8,128)(2,1)} %bitcast.50), calls=%async_computation | async-start | bytes 2621440 | tf_op jit(solution)/shard_map/all_to_all | solution.py:154
  28.0 18.3 %collective-permute-start.3 = (bf16[2,16,72,128]{3,2,1,0:T(8,128)(2,1)S(1)}, bf16[2,16,72,128]{3,2,1,0:T(8,128)(2,1)S(1)}, u32[]{:S(2)}, u32[]{:S(2)}) collective-permute-start(bf16[2,16,72,128]{3,2,1,0:T(8,128)(2,1)S(1)} %get-tuple-element.14), channel_id=1, source_target_pairs={{0,8},{8,16},{16,24},{24,0},{1,9},{9,17},{17,25},{25,1},{2,10},{10... | collective-permute-start | bytes 1769480 | tf_op jit(solution)/shard_map/ppermute | solution.py:150
  31.5 28.3 %collective-permute-start.4 = (bf16[2,16,72,128]{3,2,1,0:T(8,128)(2,1)S(1)}, bf16[2,16,72,128]{3,2,1,0:T(8,128)(2,1)S(1)}, u32[]{:S(2)}, u32[]{:S(2)}) collective-permute-start(bf16[2,16,72,128]{3,2,1,0:T(8,128)(2,1)S(1)} %get-tuple-element.15), channel_id=1, source_target_pairs={{0,16},{8,24},{16,0},{24,8},{1,17},{9,25},{17,1},{25,9},{2,18},{10... | collective-permute-start | bytes 1769480 | tf_op jit(solution)/shard_map/ppermute | solution.py:150
  36.3 24.8 %collective-permute-start.5 = (bf16[2,16,72,128]{3,2,1,0:T(8,128)(2,1)S(1)}, bf16[2,16,72,128]{3,2,1,0:T(8,128)(2,1)S(1)}, u32[]{:S(2)}, u32[]{:S(2)}) collective-permute-start(bf16[2,16,72,128]{3,2,1,0:T(8,128)(2,1)S(1)} %get-tuple-element.16), channel_id=1, source_target_pairs={{0,24},{8,0},{16,8},{24,16},{1,25},{9,1},{17,9},{25,17},{2,26},{10... | collective-permute-start | bytes 1769480 | tf_op jit(solution)/shard_map/ppermute | solution.py:150
  87.2 61.4 %all-to-all-start.2 = ((bf16[16,4,72,128]{3,2,1,0:T(8,128)(2,1)}), bf16[16,4,72,128]{3,2,1,0:T(8,128)(2,1)S(1)}, u32[]{:S(2)}, u32[]{:S(2)}) async-start(bf16[16,4,72,128]{3,2,1,0:T(8,128)(2,1)} %copy.36), calls=%async_computation.2 | async-start | bytes 2359296 | tf_op jit(solution)/shard_map/all_to_all | solution.py:154
  148.6 74.1 %all-to-all-start.1 = ((bf16[16,4,72,128]{3,2,1,0:T(8,128)(2,1)}), bf16[16,4,72,128]{3,2,1,0:T(8,128)(2,1)S(1)}, u32[]{:S(2)}, u32[]{:S(2)}) async-start(bf16[16,4,72,128]{3,2,1,0:T(8,128)(2,1)} %copy.35), calls=%async_computation.1 | async-start | bytes 2359296 | tf_op jit(solution)/shard_map/all_to_all | solution.py:154
  157.1 7.3 %copy-start.17 = (f32[1024]{0:T(1024)S(1)}, f32[1024]{0:T(1024)}, u32[]{:S(2)}) copy-start(f32[1024]{0:T(1024)} %param.9) | copy-start | bytes 12292
  157.1 7.6 %copy-start.18 = (f32[1024]{0:T(1024)S(1)}, f32[1024]{0:T(1024)}, u32[]{:S(2)}) copy-start(f32[1024]{0:T(1024)} %param.10) | copy-start | bytes 12292
  159.5 19.1 %collective-permute-start.2 = (bf16[16,80,128]{2,1,0:T(8,128)(2,1)}, bf16[16,80,128]{2,1,0:T(8,128)(2,1)}, u32[]{:S(2)}, u32[]{:S(2)}) collective-permute-start(bf16[16,80,128]{2,1,0:T(8,128)(2,1)} %get-tuple-element.18), channel_id=1, source_target_pairs={{0,24},{8,0},{16,8},{24,16},{1,25},{9,1},{17,9},{25,17},{2,26},{10... | collective-permute-start | bytes 983048 | tf_op jit(solution)/shard_map/ppermute | solution.py:150
  164.9 14.5 %collective-permute-start.1 = (bf16[16,80,128]{2,1,0:T(8,128)(2,1)}, bf16[16,80,128]{2,1,0:T(8,128)(2,1)S(1)}, u32[]{:S(2)}, u32[]{:S(2)}) collective-permute-start(bf16[16,80,128]{2,1,0:T(8,128)(2,1)} %get-tuple-element.19), channel_id=1, source_target_pairs={{0,16},{8,24},{16,0},{24,8},{1,17},{9,25},{17,1},{25,9},{2,18},{10... | collective-permute-start | bytes 983048 | tf_op jit(solution)/shard_map/ppermute | solution.py:150
  168.2 16.4 %collective-permute-start = (bf16[16,80,128]{2,1,0:T(8,128)(2,1)}, bf16[16,80,128]{2,1,0:T(8,128)(2,1)S(1)}, u32[]{:S(2)}, u32[]{:S(2)}) collective-permute-start(bf16[16,80,128]{2,1,0:T(8,128)(2,1)} %get-tuple-element.20), channel_id=1, source_target_pairs={{0,8},{8,16},{16,24},{24,0},{1,9},{9,17},{17,25},{25,1},{2,10},{10... | collective-permute-start | bytes 983048 | tf_op jit(solution)/shard_map/ppermute | solution.py:150
  187.5 1.0 copy-start.3
  188.5 1.0 copy-start.5
  189.4 1.0 copy-start.7
  198.7 18.3 %collective-permute-start.15 = (bf16[1024,128]{1,0:T(8,128)(2,1)}, bf16[1024,128]{1,0:T(8,128)(2,1)S(1)}, u32[]{:S(2)}, u32[]{:S(2)}) collective-permute-start(bf16[1024,128]{1,0:T(8,128)(2,1)} %get-tuple-element.12.refs_0_), channel_id=1, source_target_pairs={{0,4},{1,5},{2,6},{3,7},{4,0},{5,1},{6,2},{7,3},{8,12},{9,13},{10,... | collective-permute-start | bytes 786440 | tf_op jit(solution)/shard_map/ppermute | solution.py:150
  202.0 18.2 %collective-permute-start.12 = (bf16[1024,128]{1,0:T(8,128)(2,1)}, bf16[1024,128]{1,0:T(8,128)(2,1)S(1)}, u32[]{:S(2)}, u32[]{:S(2)}) collective-permute-start(bf16[1024,128]{1,0:T(8,128)(2,1)} %get-tuple-element.12.refs_0_), channel_id=1, source_target_pairs={{0,5},{1,6},{2,7},{3,0},{4,1},{5,2},{6,3},{7,4},{8,13},{9,14},{10,... | collective-permute-start | bytes 786440 | tf_op jit(solution)/shard_map/ppermute | solution.py:150
  205.4 21.3 %collective-permute-start.9 = (bf16[1024,128]{1,0:T(8,128)(2,1)}, bf16[1024,128]{1,0:T(8,128)(2,1)S(1)}, u32[]{:S(2)}, u32[]{:S(2)}) collective-permute-start(bf16[1024,128]{1,0:T(8,128)(2,1)} %get-tuple-element.12.refs_0_), channel_id=1, source_target_pairs={{0,6},{1,7},{2,0},{3,1},{4,2},{5,3},{6,4},{7,5},{8,14},{9,15},{10,... | collective-permute-start | bytes 786440 | tf_op jit(solution)/shard_map/ppermute | solution.py:150
  208.1 20.0 %collective-permute-start.6 = (bf16[1024,128]{1,0:T(8,128)(2,1)}, bf16[1024,128]{1,0:T(8,128)(2,1)S(1)}, u32[]{:S(2)}, u32[]{:S(2)}) collective-permute-start(bf16[1024,128]{1,0:T(8,128)(2,1)} %get-tuple-element.12.refs_0_), channel_id=1, source_target_pairs={{0,7},{1,0},{2,1},{3,2},{4,3},{5,4},{6,5},{7,6},{8,15},{9,8},{10,9... | collective-permute-start | bytes 786440 | tf_op jit(solution)/shard_map/ppermute | solution.py:150
  213.6 20.3 %collective-permute-start.17 = (bf16[1024,128]{1,0:T(8,128)(2,1)}, bf16[1024,128]{1,0:T(8,128)(2,1)S(1)}, u32[]{:S(2)}, u32[]{:S(2)}) collective-permute-start(bf16[1024,128]{1,0:T(8,128)(2,1)} %hist_next.3.refs_2_), channel_id=1, source_target_pairs={{0,4},{1,5},{2,6},{3,7},{4,0},{5,1},{6,2},{7,3},{8,12},{9,13},{10,... | collective-permute-start | bytes 786440 | tf_op jit(solution)/shard_map/ppermute | solution.py:150
  217.0 20.1 %collective-permute-start.14 = (bf16[1024,128]{1,0:T(8,128)(2,1)}, bf16[1024,128]{1,0:T(8,128)(2,1)S(1)}, u32[]{:S(2)}, u32[]{:S(2)}) collective-permute-start(bf16[1024,128]{1,0:T(8,128)(2,1)} %hist_next.3.refs_2_), channel_id=1, source_target_pairs={{0,5},{1,6},{2,7},{3,0},{4,1},{5,2},{6,3},{7,4},{8,13},{9,14},{10,... | collective-permute-start | bytes 786440 | tf_op jit(solution)/shard_map/ppermute | solution.py:150
  220.1 22.6 %collective-permute-start.11 = (bf16[1024,128]{1,0:T(8,128)(2,1)}, bf16[1024,128]{1,0:T(8,128)(2,1)S(1)}, u32[]{:S(2)}, u32[]{:S(2)}) collective-permute-start(bf16[1024,128]{1,0:T(8,128)(2,1)} %hist_next.3.refs_2_), channel_id=1, source_target_pairs={{0,6},{1,7},{2,0},{3,1},{4,2},{5,3},{6,4},{7,5},{8,14},{9,15},{10,... | collective-permute-start | bytes 786440 | tf_op jit(solution)/shard_map/ppermute | solution.py:150
  222.6 38.8 %copy-start.14 = (bf16[384,384]{1,0:T(8,128)(2,1)S(1)}, bf16[384,384]{1,0:T(8,128)(2,1)}, u32[]{:S(2)}) copy-start(bf16[384,384]{1,0:T(8,128)(2,1)} %constant.46.clone.order_ref) | copy-start | bytes 884740
  222.7 38.8 %copy-start.16 = (f32[1024,1]{1,0:T(8,128)S(1)}, f32[1024,1]{1,0:T(8,128)}, u32[]{:S(2)}) copy-start(f32[1024,1]{1,0:T(8,128)} %copy-done.15) | copy-start | bytes 12292
  226.7 21.7 %collective-permute-start.8 = (bf16[1024,128]{1,0:T(8,128)(2,1)}, bf16[1024,128]{1,0:T(8,128)(2,1)S(1)}, u32[]{:S(2)}, u32[]{:S(2)}) collective-permute-start(bf16[1024,128]{1,0:T(8,128)(2,1)} %hist_next.3.refs_2_), channel_id=1, source_target_pairs={{0,7},{1,0},{2,1},{3,2},{4,3},{5,4},{6,5},{7,6},{8,15},{9,8},{10,9... | collective-permute-start | bytes 786440 | tf_op jit(solution)/shard_map/ppermute | solution.py:150
  228.1 27.5 %collective-permute-start.16 = (bf16[1024,128]{1,0:T(8,128)(2,1)S(1)}, bf16[1024,128]{1,0:T(8,128)(2,1)S(1)}, u32[]{:S(2)}, u32[]{:S(2)}) collective-permute-start(bf16[1024,128]{1,0:T(8,128)(2,1)S(1)} %hist_next.2.refs_1_), channel_id=1, source_target_pairs={{0,4},{1,5},{2,6},{3,7},{4,0},{5,1},{6,2},{7,3},{8,12},{9,13},{10,... | collective-permute-start | bytes 786440 | tf_op jit(solution)/shard_map/ppermute | solution.py:150
  234.6 21.2 %collective-permute-start.13 = (bf16[1024,128]{1,0:T(8,128)(2,1)S(1)}, bf16[1024,128]{1,0:T(8,128)(2,1)S(1)}, u32[]{:S(2)}, u32[]{:S(2)}) collective-permute-start(bf16[1024,128]{1,0:T(8,128)(2,1)S(1)} %hist_next.2.refs_1_), channel_id=1, source_target_pairs={{0,5},{1,6},{2,7},{3,0},{4,1},{5,2},{6,3},{7,4},{8,13},{9,14},{10,... | collective-permute-start | bytes 786440 | tf_op jit(solution)/shard_map/ppermute | solution.py:150
  237.9 21.8 %collective-permute-start.10 = (bf16[1024,128]{1,0:T(8,128)(2,1)S(1)}, bf16[1024,128]{1,0:T(8,128)(2,1)S(1)}, u32[]{:S(2)}, u32[]{:S(2)}) collective-permute-start(bf16[1024,128]{1,0:T(8,128)(2,1)S(1)} %hist_next.2.refs_1_), channel_id=1, source_target_pairs={{0,6},{1,7},{2,0},{3,1},{4,2},{5,3},{6,4},{7,5},{8,14},{9,15},{10,... | collective-permute-start | bytes 786440 | tf_op jit(solution)/shard_map/ppermute | solution.py:150
  243.5 17.9 %collective-permute-start.7 = (bf16[1024,128]{1,0:T(8,128)(2,1)S(1)}, bf16[1024,128]{1,0:T(8,128)(2,1)S(1)}, u32[]{:S(2)}, u32[]{:S(2)}) collective-permute-start(bf16[1024,128]{1,0:T(8,128)(2,1)S(1)} %hist_next.2.refs_1_), channel_id=1, source_target_pairs={{0,7},{1,0},{2,1},{3,2},{4,3},{5,4},{6,5},{7,6},{8,15},{9,8},{10,9... | collective-permute-start | bytes 786440 | tf_op jit(solution)/shard_map/ppermute | solution.py:150
  261.4 1.0 copy-start.9
  (8 other events, 6.3 us)

commit v3 on v2

--- a/solution.py
+++ b/solution.py
@@ -18,7 +18,7 @@
 KB = 512
 VMEM = pl.BlockSpec(memory_space=pltpu.VMEM)
 SMEM = pl.BlockSpec(memory_space=pltpu.SMEM)
-PARAMS = pltpu.CompilerParams(vmem_limit_bytes=40 * 2**20)
+PARAMS = pltpu.CompilerParams(vmem_limit_bytes=24 * 2**20)
 
 
 def cost(flops, moved):
@@ -41,7 +41,7 @@
 
     def one(o, _):
         start = starts_ref[o]
-        rows = pick_rows(start, w_ref, events, slice(0, COLS))
+        rows = pick_rows(start, w_ref, events, slice(0, 2 * COLS))
         at = jnp.minimum((start // 128) * 128, events - 256)
         at = pl.multiple_of(at, 128)
         span = pltpu.roll(info_ref[:, pl.ds(at, 256)], 256 - (start - at), 1)[:, :128]
@@ -51,22 +51,19 @@
         low = jnp.where(inside, local % 32, 0).astype(jnp.float32)
         nominal = jnp.where(inside, span[1:2], 0.0)
         extra = jnp.where(lines == 0, high, jnp.where(lines == 1, low, jnp.where(lines == 2, nominal, 0.0)))
-        out_ref[o] = jnp.concatenate([rows, extra], axis=0).astype(jnp.bfloat16)
+        out_ref[o] = jnp.concatenate([rows[:, :COLS], rows[:, COLS:], extra], axis=0).astype(jnp.bfloat16)
         return 0
 
     lax.fori_loop(0, owners, one, 0, unroll=4)
 
 
-def pack_rest(n0, n1, events, place_ref, starts_ref, w_ref, *out_refs):
-    def one(z, _):
-        for turn, out_ref in enumerate(out_refs):
-            start = starts_ref[z * n1 + lax.rem(place_ref[0] + turn, n1)]
-            rows = pick_rows(start, w_ref, events, slice(COLS, 3 * COLS)).astype(jnp.bfloat16)
-            for i in range(out_ref.shape[0]):
-                out_ref[i, z] = rows[:, i * COLS : (i + 1) * COLS]
-        return 0
-
-    lax.fori_loop(0, n0, one, 0)
+def pack_rest(owners, events, starts_ref, w_ref, out_ref):
+    def one(o, _):
+        rows = pick_rows(starts_ref[o], w_ref, events, slice(2 * COLS, 3 * COLS))
+        out_ref[o] = rows.astype(jnp.bfloat16)
+        return 0
+
+    lax.fori_loop(0, owners, one, 0, unroll=4)
 
 
 def one_hot_of(bins_ref, at, size, bins_dev):
@@ -74,21 +71,22 @@
     return jnp.where(ids == bins_ref[:, pl.ds(at, size)], 1.0, 0.0).astype(jnp.bfloat16)
 
 
-def hist_first(bins_ref, nominal_ref, background_ref, observed_ref, *refs):
-    rows_refs, (out_ref, curve_ref, acc, acc_n) = refs[:-4], refs[-4:]
+def hist_first(bins_ref, nominal_ref, background_ref, observed_ref, left_ref, right_ref, out_ref, curve_ref, acc, acc_n):
     bins_dev = out_ref.shape[0]
     acc[...] = jnp.zeros_like(acc)
     acc_n[...] = jnp.zeros_like(acc_n)
-    size = rows_refs[0].shape[0]
-    for i, rows_ref in enumerate(rows_refs):
-        hot = one_hot_of(bins_ref, i * size, size, bins_dev)
-        acc[...] += jnp.dot(hot, rows_ref[...], preferred_element_type=jnp.float32)
+
+    def one(i, _):
+        at = pl.multiple_of(i * KB, KB)
+        hot = one_hot_of(bins_ref, at, KB, bins_dev)
+        rows = jnp.concatenate([left_ref[pl.ds(at, KB), :], right_ref[pl.ds(at, KB), :]], axis=1)
+        acc[...] += jnp.dot(hot, rows, preferred_element_type=jnp.float32)
         acc_n[...] += lax.dot_general(
-            hot,
-            nominal_ref[:, i * size : (i + 1) * size],
-            (((1,), (1,)), ((), ())),
-            preferred_element_type=jnp.float32,
+            hot, nominal_ref[:, pl.ds(at, KB)], (((1,), (1,)), ((), ())), preferred_element_type=jnp.float32
         )
+        return 0
+
+    lax.fori_loop(0, left_ref.shape[0] // KB, one, 0)
     out_ref[...] = acc[...].astype(jnp.bfloat16)
     yields = background_ref[...] + acc_n[:, 0:1]
     curve_ref[...] = observed_ref[...] / (yields * yields)
@@ -161,77 +159,61 @@
     groups = lax.axis_size("params")
     events, width = event_weights.shape
     bins_dev = background.shape[0]
-    chunks = width // COLS
     targets = jnp.arange(owners, dtype=jnp.int32)
     starts = jnp.sum((event_bins[None, :] < targets[:, None] * bins_dev).astype(jnp.int32), axis=1)
     info = jnp.stack([event_bins.astype(f32), nominal.astype(f32)])
     info = jnp.concatenate([info, jnp.zeros((6, events), f32)])
 
-    slab = CAP + EXTRA
-    place = lax.axis_index(BINS[1])
+    slab = 2 * CAP + EXTRA
     send_a = pl.pallas_call(
         functools.partial(pack_first, owners, bins_dev, events),
         out_shape=jax.ShapeDtypeStruct((owners, slab, COLS), bf16),
         in_specs=[SMEM, VMEM, VMEM],
         out_specs=VMEM,
         compiler_params=PARAMS,
-        cost_estimate=cost(2 * owners * CAP * WIN * COLS, 2 * owners * slab * COLS * 2),
+        cost_estimate=cost(4 * owners * CAP * WIN * COLS, 2 * owners * slab * COLS * 2),
         name="pack_first",
     )(starts, info, event_weights)
+    got_a = exchange(send_a, BINS)
     send_b = pl.pallas_call(
-        functools.partial(pack_rest, n0, n1, events),
-        out_shape=[jax.ShapeDtypeStruct((chunks - 1, n0, CAP, COLS), bf16)] * n1,
-        in_specs=[SMEM, SMEM, VMEM],
-        out_specs=[VMEM] * n1,
-        compiler_params=PARAMS,
-        cost_estimate=cost(4 * owners * CAP * WIN * COLS, 4 * owners * CAP * COLS * 2),
+        functools.partial(pack_rest, owners, events),
+        out_shape=jax.ShapeDtypeStruct((owners, CAP, COLS), bf16),
+        in_specs=[SMEM, VMEM],
+        out_specs=VMEM,
+        compiler_params=PARAMS,
+        cost_estimate=cost(2 * owners * CAP * WIN * COLS, 2 * owners * CAP * COLS * 2),
         name="pack_rest",
-    )(place.reshape(1).astype(jnp.int32), starts, event_weights)
-    got_a = exchange(send_a.reshape(n0, n1 * slab, COLS), BINS[0]).reshape(n0, n1, slab, COLS)
-    mid_b = [from_behind(send_b[t], BINS[1], t) if t else send_b[0] for t in range(n1)]
-    got = [exchange(jnp.stack([m[i] for m in mid_b], axis=1), BINS[0]) for i in range(chunks - 1)]
-    pieces = [lax.dynamic_index_in_dim(got_a, lax.rem(place + t, n1), 1, keepdims=False) for t in range(n1)]
-    pieces = [from_behind(x, BINS[1], t) if t else x for t, x in enumerate(pieces)]
-
-    extra = jnp.stack([x[:, CAP:, :CAP] for x in pieces]).astype(f32)
-    local = (extra[:, :, 0] * 32.0 + extra[:, :, 1]).astype(jnp.int32)
-    tail = ((0, 0), (0, 0), (0, EXTRA))
-    local_wide = jnp.pad(local, tail, constant_values=-1).reshape(1, owners * slab)
-    local = jnp.swapaxes(local, 0, 1).reshape(1, owners * CAP)
-    nom = jnp.pad(extra[:, :, 2], tail).astype(bf16).reshape(1, owners * slab)
-    nom = jnp.broadcast_to(nom, (8, owners * slab))
-    tile = jax.ShapeDtypeStruct((bins_dev, COLS), bf16)
-    acc = pltpu.VMEM((bins_dev, COLS), f32)
+    )(starts, event_weights)
+    send_b, got_a = lax.optimization_barrier((send_b, got_a))
+    got_b = exchange(send_b, BINS)
+
+    total = owners * CAP
+    extra = got_a[:, 2 * CAP :, :CAP].astype(f32)
+    local = (extra[:, 0] * 32.0 + extra[:, 1]).astype(jnp.int32).reshape(1, total)
+    nom = jnp.broadcast_to(extra[:, 2].astype(bf16).reshape(1, total), (8, total))
+    left, right = (got_a[:, i * CAP : (i + 1) * CAP].reshape(total, COLS) for i in range(2))
     first, curve = pl.pallas_call(
         hist_first,
-        out_shape=[tile, jax.ShapeDtypeStruct((bins_dev, 1), f32)],
-        in_specs=[VMEM] * (4 + n1),
+        out_shape=[jax.ShapeDtypeStruct((bins_dev, 2 * COLS), bf16), jax.ShapeDtypeStruct((bins_dev, 1), f32)],
+        in_specs=[VMEM] * 6,
         out_specs=[VMEM] * 2,
-        scratch_shapes=[acc, pltpu.VMEM((bins_dev, 8), f32)],
-        compiler_params=PARAMS,
-        cost_estimate=cost(2 * owners * slab * bins_dev * 256, owners * slab * COLS * 2),
+        scratch_shapes=[pltpu.VMEM((bins_dev, 2 * COLS), f32), pltpu.VMEM((bins_dev, 8), f32)],
+        compiler_params=PARAMS,
+        cost_estimate=cost(2 * total * bins_dev * 512, 2 * total * COLS * 2),
         name="hist_first",
-    )(
-        local_wide,
-        nom,
-        background.reshape(bins_dev, 1),
-        observed.reshape(bins_dev, 1),
-        *[x.reshape(n0 * slab, COLS) for x in pieces],
-    )
-    tiles = [first]
-    for g in got:
-        tiles.append(
-            pl.pallas_call(
-                hist_next,
-                out_shape=tile,
-                in_specs=[VMEM] * 2,
-                out_specs=VMEM,
-                scratch_shapes=[acc],
-                compiler_params=PARAMS,
-                cost_estimate=cost(2 * owners * CAP * bins_dev * 256, owners * CAP * COLS * 2),
-                name="hist_next",
-            )(local, g.reshape(owners * CAP, COLS))
-        )
+    )(local, nom, background.reshape(bins_dev, 1), observed.reshape(bins_dev, 1), left, right)
+    last = pl.pallas_call(
+        hist_next,
+        out_shape=jax.ShapeDtypeStruct((bins_dev, COLS), bf16),
+        in_specs=[VMEM] * 2,
+        out_specs=VMEM,
+        scratch_shapes=[pltpu.VMEM((bins_dev, COLS), f32)],
+        compiler_params=PARAMS,
+        cost_estimate=cost(2 * total * bins_dev * 256, total * COLS * 2),
+        name="hist_next",
+    )(local, got_b.reshape(total, COLS))
+    tiles = [first, last]
+    chunks = len(tiles)
     turns = groups // 2 + 1
     moved = [[from_behind(t, "params", -k) if k else t for t in tiles] for k in range(turns)]
 

time: 331 us -> 293 us (0.89)
  starting transfers between devices: 82.8 us -> 44.7 us
  waiting for transfers between devices: 133 us -> 164 us
  local copies, waits for them, and re-layouts: 20.2 us -> 6.06 us
  blocking collectives: 60.4 us -> 46.9 us
    all_to_all x3 -> x2, waiting for transfers between devices: 78.6 us -> 151 us  [exchange(): return lax.all_to_all(value, axis, split_axis=0, concat_axis=0, tiled=True)]
    ppermute x18 -> x8, waiting for transfers between devices: 54.2 us -> 13.1 us  [from_behind(): return lax.ppermute(value, axis, pairs)]
    ppermute x18 -> x8, starting transfers between devices: 52.7 us -> 19.8 us  [from_behind(): return lax.ppermute(value, axis, pairs)]
    all_to_all x2, blocking collectives: 60.4 us -> 46.9 us  [exchange(): return lax.all_to_all(value, axis, split_axis=0, concat_axis=0, tiled=True)]
    unnamed x39 -> x14, local copies, waits for them, and re-layouts: 12.9 us -> 2.48 us
    all_to_all x3 -> x2, starting transfers between devices: 30.1 us -> 24.9 us  [exchange(): return lax.all_to_all(value, axis, split_axis=0, concat_axis=0, tiled=True)]
    pallas_call x4 -> x3, Pallas kernels: 19.9 us -> 15.2 us  [the longest x1 6.55 us: body(): pl.pallas_call(hist_first, out_shape=[jax.ShapeDtypeStruct((bins_dev, 2 *...]
    another operation x10 -> x0, local copies, waits for them, and re-layouts: 3.96 us -> none  [the longest x6 2.43 us: body(): jnp.stack([m[i] for m in mid_b], axis=1)]
  transfers between devices with their start and end apart: 21 -> 10, of which waited for: 15 -> 4; matrix products, arithmetic and copies ran while one was open for 3% -> 2% of each run, Pallas kernels for 6% -> 5%
where the time goes in v3:
time: 293 us; the launch traced here: 290 us
  waiting for transfers between devices  164 us (56%)
  blocking collectives  46.9 us (16%)
  starting transfers between devices  44.7 us (15%)
  Pallas kernels  25.2 us (9%)
  local copies, waits for them, and re-layouts  6.06 us (2%)
  other arithmetic  3.51 us (1%)
    all_to_all x2, waiting for transfers between devices, exchange(): return lax.all_to_all(value, axis, split_axis=0, concat_axis=0, tiled=True)  151 us
    all_to_all x2, blocking collectives, exchange(): return lax.all_to_all(value, axis, split_axis=0, concat_axis=0, tiled=True)  46.9 us
    all_to_all x2, starting transfers between devices, exchange(): return lax.all_to_all(value, axis, split_axis=0, concat_axis=0, tiled=True)  24.9 us
    ppermute x8, starting transfers between devices, from_behind(): return lax.ppermute(value, axis, pairs)  19.8 us
    ppermute x8, waiting for transfers between devices, from_behind(): return lax.ppermute(value, axis, pairs)  13.1 us
    pallas_call x1, Pallas kernels, body(): pl.pallas_call(hist_first, out_shape=[jax.ShapeDtypeStruct((bins_dev, 2 *...  6.55 us
  transfers between devices with their start and end apart: 10, of which 4 were waited for; matrix products, arithmetic and copies ran while one was open for 2% of the time, Pallas kernels for 5%

profile of v3, /device:TPU:6, one launch (start us, length us, event | category | flops | bytes accessed | tf_op | source)
XLA Modules:
  0.0 290.3 jit_solution(1527233510312594052)
XLA Ops:
  0.0 0.7 convert_element_type.32
  0.7 0.9 convert_reduce_fusion.starts_ref
  1.7 0.7 stack.12
  2.5 1.7 copy-done
  4.2 5.1 %pack_first.1 = bf16[64,152,128]{2,1,0:T(8,128)(2,1)} custom-call(s32[64]{0:T(128)S(1)} %convert_reduce_fusion.starts_ref, f32[8,3072]{1,0:T(8,128)S(1)} %maximum_maximum_fusion.info_ref, bf16[3072,384]{1,0:T(8,128)(2,1)S(1)} %copy-done), custom_call_target="tpu_custom_call" | custom-call | flops 226492416 | bytes 4980736 | tf_op jit(solution)/shard_map/pack_first/pallas_call | solution.py:168
  9.3 19.1 %all-to-all-start = ((bf16[64,152,128]{2,1,0:T(8,128)(2,1)}), bf16[64,152,128]{2,1,0:T(8,128)(2,1)}, u32[]{:S(2)}, u32[]{:S(2)}) async-start(bf16[64,152,128]{2,1,0:T(8,128)(2,1)} %pack_first.1), calls=%async_computation | async-start | bytes 4980736 | tf_op jit(solution)/shard_map/all_to_all | solution.py:152
  28.4 4.7 %pack_rest.1 = bf16[64,72,128]{2,1,0:T(8,128)(2,1)} custom-call(s32[64]{0:T(128)S(1)} %convert_reduce_fusion.starts_ref, bf16[3072,384]{1,0:T(8,128)(2,1)S(1)} %copy-done.1), custom_call_target="tpu_custom_call" | custom-call | flops 113246208 | bytes 2359296 | tf_op jit(solution)/shard_map/pack_rest/pallas_call | solution.py:178
  33.1 112.3 %all-to-all-done = bf16[64,152,128]{2,1,0:T(8,128)(2,1)} async-done(((bf16[64,152,128]{2,1,0:T(8,128)(2,1)}), bf16[64,152,128]{2,1,0:T(8,128)(2,1)}, u32[]{:S(2)}, u32[]{:S(2)}) %all-to-all-start) | async-done | bytes 2490400 | tf_op jit(solution)/shard_map/all_to_all | solution.py:152
  145.4 5.8 %all-to-all-start.1 = ((bf16[64,72,128]{2,1,0:T(8,128)(2,1)}), bf16[64,72,128]{2,1,0:T(8,128)(2,1)S(1)}, u32[]{:S(2)}, u32[]{:S(2)}) async-start(bf16[64,72,128]{2,1,0:T(8,128)(2,1)} %pack_rest.1), calls=%async_computation.1 | async-start | bytes 2359296 | tf_op jit(solution)/shard_map/all_to_all | solution.py:152
  151.2 0.2 copy.10.observed_ref
  151.5 0.2 copy.9.background_ref
  151.7 0.9 slice_convert_fusion
  152.6 0.1 fusion.1
  152.9 1.0 slice_reduce_fusion
  154.0 1.8 fusion.2
  155.8 6.5 %hist_first.1 = (bf16[1024,256]{1,0:T(8,128)(2,1)S(1)}, f32[1024,1]{1,0:T(8,128)S(1)}) custom-call(s32[1,4608]{1,0:T(1,128)S(1)} %convert_element_type.35.bins_ref, bf16[8,4608]{1,0:T(8,128)(2,1)S(1)} %broadcast_in_dim.5.nominal_ref, f32[1024,1]{1,0:T(8,128)S(1)} %copy.9.background_ref, f32[1024,1]{1,0:T(8,128)S(1)} %copy.10.observed_ref, ...), custom_call_target="tpu_custom_call" | custom-call | flops 4831838208 | bytes 2359296 | tf_op jit(solution)/shard_map/hist_first/pallas_call | solution.py:195
  162.4 0.8 copy-done.3
  163.2 2.7 collective-permute-start.2
  165.9 2.8 collective-permute-start.4
  168.8 4.3 %collective-permute-start.6 = (bf16[1024,256]{1,0:T(8,128)(2,1)S(1)}, bf16[1024,256]{1,0:T(8,128)(2,1)}, u32[]{:S(2)}, u32[]{:S(2)}) collective-permute-start(bf16[1024,256]{1,0:T(8,128)(2,1)S(1)} %get-tuple-element.11.refs_0_), channel_id=1, source_target_pairs={{0,4},{1,5},{2,6},{3,7},{4,0},{5,1},{6,2},{7,3},{8,12},{9,13},{10,... | collective-permute-start | bytes 1572872 | tf_op jit(solution)/shard_map/ppermute | solution.py:148
  173.1 38.3 %all-to-all-done.1 = bf16[64,72,128]{2,1,0:T(8,128)(2,1)S(1)} async-done(((bf16[64,72,128]{2,1,0:T(8,128)(2,1)}), bf16[64,72,128]{2,1,0:T(8,128)(2,1)S(1)}, u32[]{:S(2)}, u32[]{:S(2)}) %all-to-all-start.1) | async-done | bytes 1179680 | tf_op jit(solution)/shard_map/all_to_all | solution.py:152
  211.4 4.0 %hist_next.1.refs_1_ = bf16[1024,128]{1,0:T(8,128)(2,1)S(1)} custom-call(s32[1,4608]{1,0:T(1,128)S(1)} %convert_element_type.35.bins_ref, bf16[4608,128]{1,0:T(8,128)(2,1)S(1)} %bitcast.7), custom_call_target="tpu_custom_call" | custom-call | flops 2415919104 | bytes 1179648 | tf_op jit(solution)/shard_map/hist_next/pallas_call | solution.py:205
  215.4 2.7 collective-permute-start.3
  218.2 2.8 collective-permute-start.5
  221.0 4.3 %collective-permute-start.7 = (bf16[1024,128]{1,0:T(8,128)(2,1)S(1)}, bf16[1024,128]{1,0:T(8,128)(2,1)S(1)}, u32[]{:S(2)}, u32[]{:S(2)}) collective-permute-start(bf16[1024,128]{1,0:T(8,128)(2,1)S(1)} %hist_next.1.refs_1_), channel_id=1, source_target_pairs={{0,4},{1,5},{2,6},{3,7},{4,0},{5,1},{6,2},{7,3},{8,12},{9,13},{10,... | collective-permute-start | bytes 786440 | tf_op jit(solution)/shard_map/ppermute | solution.py:148
  225.4 2.3 collective-permute-done.3.refs_5_
  227.7 10.7 %collective-permute-done.5.refs_7_ = bf16[1024,128]{1,0:T(8,128)(2,1)S(1)} collective-permute-done((bf16[1024,128]{1,0:T(8,128)(2,1)S(1)}, bf16[1024,128]{1,0:T(8,128)(2,1)S(1)}, u32[]{:S(2)}, u32[]{:S(2)}) %collective-permute-start.5) | collective-permute-done | bytes 262176 | tf_op jit(solution)/shard_map/ppermute | solution.py:148
  238.5 3.8 %gram.1 = bf16[4,96,1920]{2,1,0:T(8,128)(2,1)S(1)} custom-call(f32[1024,1]{1,0:T(8,128)S(1)} %copy-done.4, bf16[384,384]{1,0:T(8,128)(2,1)S(1)} %copy-done.2, bf16[1024,256]{1,0:T(8,128)(2,1)S(1)} %get-tuple-element.11.refs_0_, bf16[1024,128]{1,0:T(8,128)(2,1)S(1)} %hist_next.1.refs_1_, bf16[1024,256]{1,0:T(8,128)(2,1)S(1)} %collective-permute-done.refs_2_, ...), custom_call_target="tpu_custom_call" | custom-call | flops 1811939328 | bytes 3932160 | tf_op jit(solution)/shard_map/gram/pallas_call | solution.py:225
  242.3 22.8 %all_to_all.20.got_ref = bf16[4,96,1920]{2,1,0:T(8,128)(2,1)S(1)} all-to-all(bf16[4,96,1920]{2,1,0:T(8,128)(2,1)S(1)} %gram.1), channel_id=1, replica_groups=mesh['bins_0'=16,'bins_1'=4,'params'=8] {'bins_1'}, dimensions={0} | all-to-all | bytes 2949120 | tf_op jit(solution)/shard_map/all_to_all | solution.py:152
  265.0 0.4 add_across.1
  265.5 24.1 %all_to_all.21.got_ref = bf16[16,96,128]{2,1,0:T(8,128)(2,1)S(1)} all-to-all(bf16[16,96,128]{2,1,0:T(8,128)(2,1)S(1)} %add_across.1), channel_id=1, replica_groups=mesh['bins_0'=16,'bins_1'=4,'params'=8] {'bins_0'}, dimensions={0} | all-to-all | bytes 786432 | tf_op jit(solution)/shard_map/all_to_all | solution.py:152
  289.6 0.7 add_along.1
  (27 shorter events, 0.4 us)
Async XLA Ops:
  2.5 1.7 copy-start
  9.3 19.1 %copy-start.1 = (bf16[3072,384]{1,0:T(8,128)(2,1)S(1)}, bf16[3072,384]{1,0:T(8,128)(2,1)}, u32[]{:S(2)}) copy-start(bf16[3072,384]{1,0:T(8,128)(2,1)} %w_ref.3) | copy-start | bytes 7077892
  9.3 136.1 %all-to-all-start = ((bf16[64,152,128]{2,1,0:T(8,128)(2,1)}), bf16[64,152,128]{2,1,0:T(8,128)(2,1)}, u32[]{:S(2)}, u32[]{:S(2)}) async-start(bf16[64,152,128]{2,1,0:T(8,128)(2,1)} %pack_first.1), calls=%async_computation | async-start | bytes 4980736 | tf_op jit(solution)/shard_map/all_to_all | solution.py:152
  33.1 118.1 %copy-start.5 = (f32[1024]{0:T(1024)S(1)}, f32[1024]{0:T(1024)}, u32[]{:S(2)}) copy-start(f32[1024]{0:T(1024)} %param.10) | copy-start | bytes 12292
  33.1 118.4 %copy-start.6 = (f32[1024]{0:T(1024)S(1)}, f32[1024]{0:T(1024)}, u32[]{:S(2)}) copy-start(f32[1024]{0:T(1024)} %param.9) | copy-start | bytes 12292
  145.4 66.0 %all-to-all-start.1 = ((bf16[64,72,128]{2,1,0:T(8,128)(2,1)}), bf16[64,72,128]{2,1,0:T(8,128)(2,1)S(1)}, u32[]{:S(2)}, u32[]{:S(2)}) async-start(bf16[64,72,128]{2,1,0:T(8,128)(2,1)} %pack_rest.1), calls=%async_computation.1 | async-start | bytes 2359296 | tf_op jit(solution)/shard_map/all_to_all | solution.py:152
  162.4 0.8 copy-start.3
  163.2 52.2 %collective-permute-start = (bf16[1024,256]{1,0:T(8,128)(2,1)S(1)}, bf16[1024,256]{1,0:T(8,128)(2,1)S(1)}, u32[]{:S(2)}, u32[]{:S(2)}) collective-permute-start(bf16[1024,256]{1,0:T(8,128)(2,1)S(1)} %get-tuple-element.11.refs_0_), channel_id=1, source_target_pairs={{0,7},{1,0},{2,1},{3,2},{4,3},{5,4},{6,5},{7,6},{8,15},{9,8},{10,9... | collective-permute-start | bytes 1572872 | tf_op jit(solution)/shard_map/ppermute | solution.py:148
  163.2 55.0 %collective-permute-start.2 = (bf16[1024,256]{1,0:T(8,128)(2,1)S(1)}, bf16[1024,256]{1,0:T(8,128)(2,1)S(1)}, u32[]{:S(2)}, u32[]{:S(2)}) collective-permute-start(bf16[1024,256]{1,0:T(8,128)(2,1)S(1)} %get-tuple-element.11.refs_0_), channel_id=1, source_target_pairs={{0,6},{1,7},{2,0},{3,1},{4,2},{5,3},{6,4},{7,5},{8,14},{9,15},{10,... | collective-permute-start | bytes 1572872 | tf_op jit(solution)/shard_map/ppermute | solution.py:148
  165.9 55.1 %collective-permute-start.4 = (bf16[1024,256]{1,0:T(8,128)(2,1)S(1)}, bf16[1024,256]{1,0:T(8,128)(2,1)S(1)}, u32[]{:S(2)}, u32[]{:S(2)}) collective-permute-start(bf16[1024,256]{1,0:T(8,128)(2,1)S(1)} %get-tuple-element.11.refs_0_), channel_id=1, source_target_pairs={{0,5},{1,6},{2,7},{3,0},{4,1},{5,2},{6,3},{7,4},{8,13},{9,14},{10,... | collective-permute-start | bytes 1572872 | tf_op jit(solution)/shard_map/ppermute | solution.py:148
  168.8 56.6 %collective-permute-start.6 = (bf16[1024,256]{1,0:T(8,128)(2,1)S(1)}, bf16[1024,256]{1,0:T(8,128)(2,1)}, u32[]{:S(2)}, u32[]{:S(2)}) collective-permute-start(bf16[1024,256]{1,0:T(8,128)(2,1)S(1)} %get-tuple-element.11.refs_0_), channel_id=1, source_target_pairs={{0,4},{1,5},{2,6},{3,7},{4,0},{5,1},{6,2},{7,3},{8,12},{9,13},{10,... | collective-permute-start | bytes 1572872 | tf_op jit(solution)/shard_map/ppermute | solution.py:148
  211.4 27.1 %copy-start.2 = (bf16[384,384]{1,0:T(8,128)(2,1)S(1)}, bf16[384,384]{1,0:T(8,128)(2,1)}, u32[]{:S(2)}) copy-start(bf16[384,384]{1,0:T(8,128)(2,1)} %constant.10.clone.order_ref) | copy-start | bytes 884740
  211.4 27.1 %copy-start.4 = (f32[1024,1]{1,0:T(8,128)S(1)}, f32[1024,1]{1,0:T(8,128)}, u32[]{:S(2)}) copy-start(f32[1024,1]{1,0:T(8,128)} %copy-done.3) | copy-start | bytes 12292
  215.4 10.0 %collective-permute-start.1 = (bf16[1024,128]{1,0:T(8,128)(2,1)S(1)}, bf16[1024,128]{1,0:T(8,128)(2,1)S(1)}, u32[]{:S(2)}, u32[]{:S(2)}) collective-permute-start(bf16[1024,128]{1,0:T(8,128)(2,1)S(1)} %hist_next.1.refs_1_), channel_id=1, source_target_pairs={{0,7},{1,0},{2,1},{3,2},{4,3},{5,4},{6,5},{7,6},{8,15},{9,8},{10,9... | collective-permute-start | bytes 786440 | tf_op jit(solution)/shard_map/ppermute | solution.py:148
  215.4 12.3 %collective-permute-start.3 = (bf16[1024,128]{1,0:T(8,128)(2,1)S(1)}, bf16[1024,128]{1,0:T(8,128)(2,1)S(1)}, u32[]{:S(2)}, u32[]{:S(2)}) collective-permute-start(bf16[1024,128]{1,0:T(8,128)(2,1)S(1)} %hist_next.1.refs_1_), channel_id=1, source_target_pairs={{0,6},{1,7},{2,0},{3,1},{4,2},{5,3},{6,4},{7,5},{8,14},{9,15},{10,... | collective-permute-start | bytes 786440 | tf_op jit(solution)/shard_map/ppermute | solution.py:148
  218.2 20.3 %collective-permute-start.5 = (bf16[1024,128]{1,0:T(8,128)(2,1)S(1)}, bf16[1024,128]{1,0:T(8,128)(2,1)S(1)}, u32[]{:S(2)}, u32[]{:S(2)}) collective-permute-start(bf16[1024,128]{1,0:T(8,128)(2,1)S(1)} %hist_next.1.refs_1_), channel_id=1, source_target_pairs={{0,5},{1,6},{2,7},{3,0},{4,1},{5,2},{6,3},{7,4},{8,13},{9,14},{10,... | collective-permute-start | bytes 786440 | tf_op jit(solution)/shard_map/ppermute | solution.py:148
  221.0 17.4 %collective-permute-start.7 = (bf16[1024,128]{1,0:T(8,128)(2,1)S(1)}, bf16[1024,128]{1,0:T(8,128)(2,1)S(1)}, u32[]{:S(2)}, u32[]{:S(2)}) collective-permute-start(bf16[1024,128]{1,0:T(8,128)(2,1)S(1)} %hist_next.1.refs_1_), channel_id=1, source_target_pairs={{0,4},{1,5},{2,6},{3,7},{4,0},{5,1},{6,2},{7,3},{8,12},{9,13},{10,... | collective-permute-start | bytes 786440 | tf_op jit(solution)/shard_map/ppermute | solution.py:148

commit v4 on v3

v4 whole, which is shorter than its diff:
```python
import functools

import jax
import jax.numpy as jnp
import numpy as np
from jax import lax
from jax.experimental import pallas as pl
from jax.experimental.pallas import tpu as pltpu
from jax.sharding import Mesh
from jax.sharding import PartitionSpec as P

BINS = ("bins_0", "bins_1")
PARAMS_BINS = ("params", "bins_0", "bins_1")
CAP = 72
EXTRA = 8
COLS = 128
KB = 512
VMEM = pl.BlockSpec(memory_space=pltpu.VMEM)
SMEM = pl.BlockSpec(memory_space=pltpu.SMEM)
PARAMS = pltpu.CompilerParams(vmem_limit_bytes=24 * 2**20)
SMALL_PARAMS = pltpu.CompilerParams(vmem_limit_bytes=12 * 2**20)
F32 = jnp.float32
BF16 = jnp.bfloat16


def cost(flops, moved):
    return pl.CostEstimate(flops=flops, bytes_accessed=moved, transcendentals=0)


def dot(a, b):
    return jnp.dot(a, b, preferred_element_type=F32)


def dot_t(a, b):
    return lax.dot_general(a, b, (((1,), (1,)), ((), ())), preferred_element_type=F32)


def spread(w_ref, turn_ref, tiles):
    events = w_ref.shape[0]
    step = 512 if events % 512 == 0 else events

    def one(i, _):
        at = pl.multiple_of(i * step, step)
        rows = dot(w_ref[pl.ds(at, step), :], turn_ref[...])
        for t, tile in enumerate(tiles):
            tile[pl.ds(at, step), :] = rows[:, t * COLS : (t + 1) * COLS]
        return 0

    lax.fori_loop(0, events // step, one, 0)
    for tile in tiles:
        tile[events:, :] = jnp.zeros((tile.shape[0] - events, COLS), F32)


def pack_first(owners, bins_dev, events, starts_ref, info_ref, w_ref, turn_ref, out_ref, left, right):
    lines = lax.broadcasted_iota(jnp.int32, (EXTRA, 128), 0)
    spread(w_ref, turn_ref, (left, right))

    def one(o, _):
        start = starts_ref[o]
        at = jnp.minimum((start // 128) * 128, events - 256)
        at = pl.multiple_of(at, 128)
        span = pltpu.roll(info_ref[:, pl.ds(at, 256)], 256 - (start - at), 1)[:, :128]
        local = span[0:1].astype(jnp.int32) - o * bins_dev
        inside = (local >= 0) & (local < bins_dev)
        high = jnp.where(inside, local // 32, -1).astype(F32)
        low = jnp.where(inside, local % 32, 0).astype(F32)
        nominal = jnp.where(inside, span[1:2], 0.0)
        extra = jnp.where(lines == 0, high, jnp.where(lines == 1, low, jnp.where(lines == 2, nominal, 0.0)))
        rows = [tile[pl.ds(start, CAP), :] for tile in (left, right)]
        out_ref[o] = jnp.concatenate([*rows, extra], axis=0).astype(BF16)
        return 0

    lax.fori_loop(0, owners, one, 0, unroll=4)


def pack_rest(owners, starts_ref, w_ref, turn_ref, out_ref, tile):
    spread(w_ref, turn_ref, (tile,))

    def one(o, _):
        out_ref[o] = tile[pl.ds(starts_ref[o], CAP), :].astype(BF16)
        return 0

    lax.fori_loop(0, owners, one, 0, unroll=4)


def one_hot_of(bins_ref, at, size, bins_dev):
    ids = lax.broadcasted_iota(jnp.int32, (bins_dev, size), 0)
    return jnp.where(ids == bins_ref[:, pl.ds(at, size)], 1.0, 0.0).astype(BF16)


def hist_first(bins_ref, nominal_ref, background_ref, observed_ref, left_ref, right_ref, out_ref, curve_ref, acc, acc_n):
    bins_dev = out_ref.shape[0]
    acc[...] = jnp.zeros_like(acc)
    acc_n[...] = jnp.zeros_like(acc_n)

    def one(i, _):
        at = pl.multiple_of(i * KB, KB)
        hot = one_hot_of(bins_ref, at, KB, bins_dev)
        rows = jnp.concatenate([left_ref[pl.ds(at, KB), :], right_ref[pl.ds(at, KB), :]], axis=1)
        acc[...] += dot(hot, rows)
        acc_n[...] += dot_t(hot, nominal_ref[:, pl.ds(at, KB)])
        return 0

    lax.fori_loop(0, left_ref.shape[0] // KB, one, 0)
    out_ref[...] = acc[...].astype(BF16)
    yields = background_ref[...] + acc_n[:, 0:1]
    curve_ref[...] = observed_ref[...] / (yields * yields)


def hist_next(bins_ref, rows_ref, out_ref, acc):
    bins_dev = out_ref.shape[0]
    acc[...] = jnp.zeros_like(acc)

    def one(i, _):
        at = pl.multiple_of(i * KB, KB)
        hot = one_hot_of(bins_ref, at, KB, bins_dev)
        acc[...] += dot(hot, rows_ref[pl.ds(at, KB), :])
        return 0

    lax.fori_loop(0, rows_ref.shape[0] // KB, one, 0)
    out_ref[...] = acc[...].astype(BF16)


def left_side(curve_ref, own_ref):
    weighted = (curve_ref[...] * own_ref[...].astype(F32)).astype(BF16)
    size = weighted.shape[1]
    row = lax.broadcasted_iota(jnp.int32, (size, size), 0)
    col = lax.broadcasted_iota(jnp.int32, (size, size), 1)
    return dot_t(jnp.where(row == col, 1.0, 0.0).astype(BF16), weighted).astype(BF16)


def gram_early(curve_ref, *refs):
    parts, out_ref = refs[:-1], refs[-1]
    n1, step, _ = out_ref.shape
    lhs = left_side(curve_ref, parts[0])
    wide = 2 * COLS
    for k, part in enumerate(parts):
        full = dot(lhs, part[...]).astype(BF16)
        for y in range(n1):
            out_ref[y, :, k * wide : (k + 1) * wide] = full[y * step : (y + 1) * step]


def gram_late(turns, curve_ref, *refs):
    first, last, out_ref = refs[:turns], refs[turns:-1], refs[-1]
    n1 = out_ref.shape[0]
    lhs_a = left_side(curve_ref, first[0])
    lhs_b = left_side(curve_ref, last[0])
    for k in range(turns):
        partner = last[k][...]
        side = dot(lhs_a, partner).astype(BF16)
        low = jnp.concatenate([dot(lhs_b, first[k][...]), dot(lhs_b, partner)], axis=1).astype(BF16)
        sa, sb = side.shape[0] // n1, low.shape[0] // n1
        for y in range(n1):
            out_ref[y, k * sa : (k + 1) * sa] = side[y * sa : (y + 1) * sa]
            for t in range(3):
                at = turns * sa + (3 * k + t) * sb
                out_ref[y, at : at + sb] = low[y * sb : (y + 1) * sb, t * COLS : (t + 1) * COLS]


def add_across(turns, early_ref, late_ref, turn_ref, out_ref, wide):
    n0 = out_ref.shape[0]
    early = jnp.sum(early_ref[...].astype(F32), axis=0).astype(BF16)
    late = jnp.sum(late_ref[...].astype(F32), axis=0).astype(BF16)
    sa = early.shape[0]
    sb = sa // 2
    la, lb = sa // n0, sb // n0
    lines = la + lb
    wide[...] = jnp.zeros_like(wide)
    for k in range(turns):
        high = jnp.concatenate(
            [early[:, 2 * k * COLS : 2 * (k + 1) * COLS], late[k * sa : (k + 1) * sa]], axis=1
        )
        at = turns * sa + 3 * k * sb
        low = jnp.concatenate([late[at + t * sb : at + (t + 1) * sb] for t in range(3)], axis=1)
        high = dot_t(high, turn_ref[...])
        low = dot_t(low, turn_ref[...])
        for t in range(3):
            lanes = slice(t * COLS, (t + 1) * COLS)
            for z in range(n0):
                at = (3 * k + t) * lines
                wide[z, at : at + la] = high[z * la : (z + 1) * la, lanes]
                wide[z, at + la : at + lines] = low[z * lb : (z + 1) * lb, lanes]
    out_ref[...] = wide[...].astype(BF16)


def add_along(scale, got_ref, out_ref):
    lines = out_ref.shape[0]
    total = jnp.sum(got_ref[...].astype(F32), axis=0) * scale
    for j in range(out_ref.shape[1] // 128):
        out_ref[:, j * 128 : (j + 1) * 128] = total[j * lines : (j + 1) * lines]


def from_behind(value, axis, steps):
    count = lax.axis_size(axis)
    pairs = [(source, (source + steps) % count) for source in range(count)]
    return lax.ppermute(value, axis, pairs)


def exchange(value, axis):
    return lax.all_to_all(value, axis, split_axis=0, concat_axis=0, tiled=True)


def column_order(n0, n1, width):
    lines = width // (n0 * n1)
    la = 2 * lines // 3
    m = np.arange(width)
    owner, r = m // lines, m % lines
    rank = (owner % n1) * n0 + owner // n1
    place = np.where(r < la, rank * la + r, n0 * n1 * la + rank * (lines - la) + r - la)
    turn = np.zeros((width, width), np.float32)
    turn[m, place] = 1.0
    return turn


def body(event_bins, event_weights, nominal, background, observed):
    n0, n1 = (lax.axis_size(a) for a in BINS)
    owners = n0 * n1
    groups = lax.axis_size("params")
    events, width = event_weights.shape
    bins_dev = background.shape[0]
    turns = groups // 2 + 1
    lines = width // owners
    turn = column_order(n0, n1, width)
    targets = jnp.arange(owners, dtype=jnp.int32)
    starts = jnp.sum((event_bins[None, :] < targets[:, None] * bins_dev).astype(jnp.int32), axis=1)
    info = jnp.stack([event_bins.astype(F32), nominal.astype(F32)])
    info = jnp.concatenate([info, jnp.zeros((6, events), F32)])

    slab = 2 * CAP + EXTRA
    scratch = pltpu.VMEM((events + CAP, COLS), F32)
    send_a = pl.pallas_call(
        functools.partial(pack_first, owners, bins_dev, events),
        out_shape=jax.ShapeDtypeStruct((owners, slab, COLS), BF16),
        in_specs=[SMEM, VMEM, VMEM, VMEM],
        out_specs=VMEM,
        scratch_shapes=[scratch, scratch],
        compiler_params=PARAMS,
        cost_estimate=cost(2 * events * width * 2 * COLS, 2 * owners * slab * COLS * 2),
        name="pack_first",
    )(starts, info, event_weights, jnp.asarray(turn[:, : 2 * COLS], BF16))
    got_a = exchange(send_a, BINS)
    send_b = pl.pallas_call(
        functools.partial(pack_rest, owners),
        out_shape=jax.ShapeDtypeStruct((owners, CAP, COLS), BF16),
        in_specs=[SMEM, VMEM, VMEM],
        out_specs=VMEM,
        scratch_shapes=[scratch],
        compiler_params=PARAMS,
        cost_estimate=cost(2 * events * width * COLS, 2 * owners * CAP * COLS * 2),
        name="pack_rest",
    )(starts, event_weights, jnp.asarray(turn[:, 2 * COLS :], BF16))
    send_b, got_a = lax.optimization_barrier((send_b, got_a))
    got_b = exchange(send_b, BINS)

    total = owners * CAP
    extra = got_a[:, 2 * CAP :, :CAP].astype(F32)
    local = (extra[:, 0] * 32.0 + extra[:, 1]).astype(jnp.int32).reshape(1, total)
    nom = jnp.broadcast_to(extra[:, 2].astype(BF16).reshape(1, total), (8, total))
    left, right = (got_a[:, i * CAP : (i + 1) * CAP].reshape(total, COLS) for i in range(2))
    first, curve = pl.pallas_call(
        hist_first,
        out_shape=[jax.ShapeDtypeStruct((bins_dev, 2 * COLS), BF16), jax.ShapeDtypeStruct((bins_dev, 1), F32)],
        in_specs=[VMEM] * 6,
        out_specs=[VMEM] * 2,
        scratch_shapes=[pltpu.VMEM((bins_dev, 2 * COLS), F32), pltpu.VMEM((bins_dev, 8), F32)],
        compiler_params=SMALL_PARAMS,
        cost_estimate=cost(2 * total * bins_dev * 512, 2 * total * COLS * 2),
        name="hist_first",
    )(local, nom, background.reshape(bins_dev, 1), observed.reshape(bins_dev, 1), left, right)
    firsts = [first] + [from_behind(first, "params", -k) for k in range(1, turns)]
    early = pl.pallas_call(
        gram_early,
        out_shape=jax.ShapeDtypeStruct((n1, 2 * COLS // n1, turns * 2 * COLS), BF16),
        in_specs=[VMEM] * (1 + turns),
        out_specs=VMEM,
        compiler_params=SMALL_PARAMS,
        cost_estimate=cost(2 * bins_dev * 4 * COLS * COLS * (turns + 1), 2 * turns * COLS * bins_dev * 2),
        name="gram_early",
    )(curve, *firsts)
    early, got_b = lax.optimization_barrier((early, got_b))
    early = exchange(early, BINS[1])

    last = pl.pallas_call(
        hist_next,
        out_shape=jax.ShapeDtypeStruct((bins_dev, COLS), BF16),
        in_specs=[VMEM] * 2,
        out_specs=VMEM,
        scratch_shapes=[pltpu.VMEM((bins_dev, COLS), F32)],
        compiler_params=SMALL_PARAMS,
        cost_estimate=cost(2 * total * bins_dev * 256, total * COLS * 2),
        name="hist_next",
    )(local, got_b.reshape(total, COLS))
    lasts = [last] + [from_behind(last, "params", -k) for k in range(1, turns)]
    rows_late = turns * (2 * COLS + 3 * COLS) // n1
    late = pl.pallas_call(
        functools.partial(gram_late, turns),
        out_shape=jax.ShapeDtypeStruct((n1, rows_late, COLS), BF16),
        in_specs=[VMEM] * (1 + 2 * turns),
        out_specs=VMEM,
        compiler_params=SMALL_PARAMS,
        cost_estimate=cost(2 * bins_dev * 5 * COLS * COLS * (turns + 1), 3 * turns * COLS * bins_dev * 2),
        name="gram_late",
    )(curve, *firsts, *lasts)
    late = exchange(late, BINS[1])

    packed = -(-lines * turns * width // 128 // 16) * 16
    across = pl.pallas_call(
        functools.partial(add_across, turns),
        out_shape=jax.ShapeDtypeStruct((n0, packed, 128), BF16),
        in_specs=[VMEM] * 3,
        out_specs=VMEM,
        scratch_shapes=[pltpu.VMEM((n0, packed, 128), F32)],
        compiler_params=SMALL_PARAMS,
        name="add_across",
    )(early, late, jnp.asarray(turn, BF16))
    return pl.pallas_call(
        functools.partial(add_along, 1.0 / (bins_dev * owners)),
        out_shape=jax.ShapeDtypeStruct((lines, turns * width), F32),
        in_specs=[VMEM],
        out_specs=VMEM,
        compiler_params=SMALL_PARAMS,
        name="add_along",
    )(exchange(across, BINS[0]))


def solution(mesh):
    split = Mesh(mesh.devices.reshape(16, 4, mesh.shape["params"]), ("bins_0", "bins_1", "params"))
    placed = (P(BINS), P(BINS, "params"), P(BINS), P(BINS), P(BINS))
    return jax.shard_map(
        body, mesh=split, in_specs=placed, out_specs=P(PARAMS_BINS, None), check_vma=False
    )
```

time: 293 us -> 299 us (1.020)
  local copies, waits for them, and re-layouts: 6.06 us -> 11.8 us
  starting transfers between devices: 44.7 us -> 49 us
  waiting for transfers between devices: 164 us -> 160 us
    all_to_all x2 -> x3, waiting for transfers between devices: 151 us -> 115 us  [exchange(): return lax.all_to_all(value, axis, split_axis=0, concat_axis=0, tiled=True)]
    ppermute x8, waiting for transfers between devices: 13.1 us -> 45.7 us  [from_behind(): return lax.ppermute(value, axis, pairs)]
    unnamed x14 -> x32, local copies, waits for them, and re-layouts: 2.48 us -> 7.32 us
    all_to_all x2 -> x3, starting transfers between devices: 24.9 us -> 29.2 us  [exchange(): return lax.all_to_all(value, axis, split_axis=0, concat_axis=0, tiled=True)]
    pallas_call x3 -> x4, Pallas kernels: 8.87 us -> 8.45 us  [the longest x1 3.39 us: body(): pl.pallas_call(functools.partial(pack_rest, owners), out_shape=jax.ShapeD...]
  transfers between devices with their start and end apart: 10 -> 11, of which waited for: 4 -> 7; matrix products, arithmetic and copies ran while one was open for 2% -> 2% of each run, Pallas kernels for 5% -> 6%
where the time goes in v4:
time: 299 us; the launch traced here: 298 us
  waiting for transfers between devices  160 us (54%)
  starting transfers between devices  49 us (16%)
  blocking collectives  48 us (16%)
  Pallas kernels  25.3 us (8%)
  local copies, waits for them, and re-layouts  11.8 us (4%)
  other arithmetic  3.5 us (1%)
    all_to_all x3, waiting for transfers between devices, exchange(): return lax.all_to_all(value, axis, split_axis=0, concat_axis=0, tiled=True)  115 us
    all_to_all x2, blocking collectives, exchange(): return lax.all_to_all(value, axis, split_axis=0, concat_axis=0, tiled=True)  48 us
    ppermute x8, waiting for transfers between devices, from_behind(): return lax.ppermute(value, axis, pairs)  45.7 us
    all_to_all x3, starting transfers between devices, exchange(): return lax.all_to_all(value, axis, split_axis=0, concat_axis=0, tiled=True)  29.2 us
    ppermute x8, starting transfers between devices, from_behind(): return lax.ppermute(value, axis, pairs)  19.8 us
    unnamed x32, local copies, waits for them, and re-layouts  7.32 us
    pallas_call x1, Pallas kernels, body(): pl.pallas_call(hist_first, out_shape=[jax.ShapeDtypeStruct((bins_dev, 2 *...  6.59 us
  transfers between devices with their start and end apart: 11, of which 7 were waited for; matrix products, arithmetic and copies ran while one was open for 2% of the time, Pallas kernels for 6%

profile of v4, /device:TPU:6, one launch (start us, length us, event | category | flops | bytes accessed | tf_op | source)
XLA Modules:
  0.0 298.2 jit_solution(1635893045576895251)
XLA Ops:
  0.7 0.9 convert_reduce_fusion.starts_ref
  2.5 1.7 copy-done
  4.2 0.9 copy-done.12
  5.1 5.6 %pack_first.1 = bf16[64,152,128]{2,1,0:T(8,128)(2,1)} custom-call(s32[64]{0:T(128)S(1)} %convert_reduce_fusion.starts_ref, f32[8,3072]{1,0:T(8,128)S(1)} %maximum_maximum_fusion.info_ref, bf16[3072,384]{1,0:T(8,128)(2,1)S(1)} %copy-done, bf16[384,256]{1,0:T(8,128)(2,1)S(1)} %copy-done.12), custom_call_target="tpu_custom_call" | custom-call | flops 603979776 | bytes 4980736 | tf_op jit(solution)/shard_map/pack_first/pallas_call | solution.py:231
  10.7 19.1 %all-to-all-start = ((bf16[64,152,128]{2,1,0:T(8,128)(2,1)}), bf16[64,152,128]{2,1,0:T(8,128)(2,1)}, u32[]{:S(2)}, u32[]{:S(2)}) async-start(bf16[64,152,128]{2,1,0:T(8,128)(2,1)} %pack_first.1), calls=%async_computation | async-start | bytes 4980736 | tf_op jit(solution)/shard_map/all_to_all | solution.py:200
  29.9 3.4 %pack_rest.1 = bf16[64,72,128]{2,1,0:T(8,128)(2,1)} custom-call(s32[64]{0:T(128)S(1)} %convert_reduce_fusion.starts_ref, bf16[3072,384]{1,0:T(8,128)(2,1)S(1)} %copy-done.1, bf16[384,128]{1,0:T(8,128)(2,1)S(1)} %copy-done.13), custom_call_target="tpu_custom_call" | custom-call | flops 301989888 | bytes 2359296 | tf_op jit(solution)/shard_map/pack_rest/pallas_call | solution.py:242
  33.3 113.5 %all-to-all-done = bf16[64,152,128]{2,1,0:T(8,128)(2,1)} async-done(((bf16[64,152,128]{2,1,0:T(8,128)(2,1)}), bf16[64,152,128]{2,1,0:T(8,128)(2,1)}, u32[]{:S(2)}, u32[]{:S(2)}) %all-to-all-start) | async-done | bytes 2490400 | tf_op jit(solution)/shard_map/all_to_all | solution.py:200
  146.8 5.8 %all-to-all-start.1 = ((bf16[64,72,128]{2,1,0:T(8,128)(2,1)}), bf16[64,72,128]{2,1,0:T(8,128)(2,1)S(1)}, u32[]{:S(2)}, u32[]{:S(2)}) async-start(bf16[64,72,128]{2,1,0:T(8,128)(2,1)} %pack_rest.1), calls=%async_computation.1 | async-start | bytes 2359296 | tf_op jit(solution)/shard_map/all_to_all | solution.py:200
  152.9 1.0 copy.12.observed_ref
  155.1 1.0 slice_reduce_fusion
  156.2 1.9 fusion.2
  158.2 6.6 %hist_first.1 = (bf16[1024,256]{1,0:T(8,128)(2,1)S(1)}, f32[1024,1]{1,0:T(8,128)S(1)}) custom-call(s32[1,4608]{1,0:T(1,128)S(1)} %convert_element_type.35.bins_ref, bf16[8,4608]{1,0:T(8,128)(2,1)S(1)} %broadcast_in_dim.5.nominal_ref, f32[1024,1]{1,0:T(8,128)S(1)} %copy.11.background_ref, f32[1024,1]{1,0:T(8,128)S(1)} %copy-done.10, ...), custom_call_target="tpu_custom_call" | custom-call | flops 4831838208 | bytes 2359296 | tf_op jit(solution)/shard_map/hist_first/pallas_call | solution.py:260
  164.8 2.7 collective-permute-start.1
  167.5 2.8 collective-permute-start.2
  170.3 4.3 %collective-permute-start.3 = (bf16[1024,256]{1,0:T(8,128)(2,1)S(1)}, bf16[1024,256]{1,0:T(8,128)(2,1)S(1)}, u32[]{:S(2)}, u32[]{:S(2)}) collective-permute-start(bf16[1024,256]{1,0:T(8,128)(2,1)S(1)} %get-tuple-element.13.refs_0_), channel_id=1, source_target_pairs={{0,4},{1,5},{2,6},{3,7},{4,0},{5,1},{6,2},{7,3},{8,12},{9,13},{10,... | collective-permute-start | bytes 1572872 | tf_op jit(solution)/shard_map/ppermute | solution.py:196
  174.8 12.6 %collective-permute-done.1.refs_2_ = bf16[1024,256]{1,0:T(8,128)(2,1)S(1)} collective-permute-done((bf16[1024,256]{1,0:T(8,128)(2,1)S(1)}, bf16[1024,256]{1,0:T(8,128)(2,1)S(1)}, u32[]{:S(2)}, u32[]{:S(2)}) %collective-permute-start.1) | collective-permute-done | bytes 524320 | tf_op jit(solution)/shard_map/ppermute | solution.py:196
  187.4 19.9 %collective-permute-done.2.refs_3_ = bf16[1024,256]{1,0:T(8,128)(2,1)S(1)} collective-permute-done((bf16[1024,256]{1,0:T(8,128)(2,1)S(1)}, bf16[1024,256]{1,0:T(8,128)(2,1)S(1)}, u32[]{:S(2)}, u32[]{:S(2)}) %collective-permute-start.2) | collective-permute-done | bytes 524320 | tf_op jit(solution)/shard_map/ppermute | solution.py:196
  207.3 2.0 gram_early.1
  211.7 1.1 all-to-all-done.1
  212.8 1.0 copy-done.8
  213.9 4.2 %all-to-all-start.2 = ((bf16[4,64,1280]{2,1,0:T(8,128)(2,1)}), bf16[4,64,1280]{2,1,0:T(8,128)(2,1)S(1)}, u32[]{:S(2)}, u32[]{:S(2)}) async-start(bf16[4,64,1280]{2,1,0:T(8,128)(2,1)} %gram_early.1), calls=%async_computation.2 | async-start | bytes 1310720 | tf_op jit(solution)/shard_map/all_to_all | solution.py:200
  218.1 1.3 copy-done.9
  219.4 4.0 %hist_next.1.refs_5_ = bf16[1024,128]{1,0:T(8,128)(2,1)S(1)} custom-call(s32[1,4608]{1,0:T(1,128)S(1)} %convert_element_type.35.bins_ref, bf16[4608,128]{1,0:T(8,128)(2,1)S(1)} %bitcast.7), custom_call_target="tpu_custom_call" | custom-call | flops 2415919104 | bytes 1179648 | tf_op jit(solution)/shard_map/hist_next/pallas_call | solution.py:283
  223.4 2.9 collective-permute-start.5
  226.3 2.7 collective-permute-start.6
  229.0 4.3 %collective-permute-start.7 = (bf16[1024,128]{1,0:T(8,128)(2,1)S(1)}, bf16[1024,128]{1,0:T(8,128)(2,1)S(1)}, u32[]{:S(2)}, u32[]{:S(2)}) collective-permute-start(bf16[1024,128]{1,0:T(8,128)(2,1)S(1)} %hist_next.1.refs_5_), channel_id=1, source_target_pairs={{0,4},{1,5},{2,6},{3,7},{4,0},{5,1},{6,2},{7,3},{8,12},{9,13},{10,... | collective-permute-start | bytes 786440 | tf_op jit(solution)/shard_map/ppermute | solution.py:196
  233.3 2.6 collective-permute-done.5.refs_7_
  236.0 10.5 %collective-permute-done.6.refs_8_ = bf16[1024,128]{1,0:T(8,128)(2,1)S(1)} collective-permute-done((bf16[1024,128]{1,0:T(8,128)(2,1)S(1)}, bf16[1024,128]{1,0:T(8,128)(2,1)S(1)}, u32[]{:S(2)}, u32[]{:S(2)}) %collective-permute-start.6) | collective-permute-done | bytes 262176 | tf_op jit(solution)/shard_map/ppermute | solution.py:196
  246.5 1.9 gram_late.1
  248.4 16.3 %all_to_all.25.late_ref = bf16[4,800,128]{2,1,0:T(8,128)(2,1)S(1)} all-to-all(bf16[4,800,128]{2,1,0:T(8,128)(2,1)S(1)} %gram_late.1), channel_id=1, replica_groups=mesh['bins_0'=16,'bins_1'=4,'params'=8] {'bins_1'}, dimensions={0} | all-to-all | bytes 1638400 | tf_op jit(solution)/shard_map/all_to_all | solution.py:200
  264.7 1.1 add_across.1
  265.8 31.7 %all_to_all.26.got_ref = bf16[16,96,128]{2,1,0:T(8,128)(2,1)S(1)} all-to-all(bf16[16,96,128]{2,1,0:T(8,128)(2,1)S(1)} %add_across.1), channel_id=1, replica_groups=mesh['bins_0'=16,'bins_1'=4,'params'=8] {'bins_0'}, dimensions={0} | all-to-all | bytes 786432 | tf_op jit(solution)/shard_map/all_to_all | solution.py:200
  (48 shorter events, 6.3 us)
Async XLA Ops:
  2.5 1.7 copy-start
  4.2 0.9 copy-start.12
  10.7 19.1 %copy-start.1 = (bf16[3072,384]{1,0:T(8,128)(2,1)S(1)}, bf16[3072,384]{1,0:T(8,128)(2,1)}, u32[]{:S(2)}) copy-start(bf16[3072,384]{1,0:T(8,128)(2,1)} %w_ref.3) | copy-start | bytes 7077892
  10.7 19.1 %copy-start.13 = (bf16[384,128]{1,0:T(8,128)(2,1)S(1)}, bf16[384,128]{1,0:T(8,128)(2,1)}, u32[]{:S(2)}) copy-start(bf16[384,128]{1,0:T(8,128)(2,1)} %constant.15.clone.turn_ref) | copy-start | bytes 294916
  10.7 136.1 %all-to-all-start = ((bf16[64,152,128]{2,1,0:T(8,128)(2,1)}), bf16[64,152,128]{2,1,0:T(8,128)(2,1)}, u32[]{:S(2)}, u32[]{:S(2)}) async-start(bf16[64,152,128]{2,1,0:T(8,128)(2,1)} %pack_first.1), calls=%async_computation | async-start | bytes 4980736 | tf_op jit(solution)/shard_map/all_to_all | solution.py:200
  29.8 122.8 %copy-start.14 = (f32[1024]{0:T(1024)S(1)}, f32[1024]{0:T(1024)}, u32[]{:S(2)}) copy-start(f32[1024]{0:T(1024)} %param.11) | copy-start | bytes 12292
  29.9 123.0 %copy-start.15 = (f32[1024]{0:T(1024)S(1)}, f32[1024]{0:T(1024)}, u32[]{:S(2)}) copy-start(f32[1024]{0:T(1024)} %param.12) | copy-start | bytes 12292
  146.8 66.0 %all-to-all-start.1 = ((bf16[64,72,128]{2,1,0:T(8,128)(2,1)}), bf16[64,72,128]{2,1,0:T(8,128)(2,1)S(1)}, u32[]{:S(2)}, u32[]{:S(2)}) async-start(bf16[64,72,128]{2,1,0:T(8,128)(2,1)} %pack_rest.1), calls=%async_computation.1 | async-start | bytes 2359296 | tf_op jit(solution)/shard_map/all_to_all | solution.py:200
  156.2 1.9 copy-start.10
  164.7 10.0 %collective-permute-start = (bf16[1024,256]{1,0:T(8,128)(2,1)S(1)}, bf16[1024,256]{1,0:T(8,128)(2,1)S(1)}, u32[]{:S(2)}, u32[]{:S(2)}) collective-permute-start(bf16[1024,256]{1,0:T(8,128)(2,1)S(1)} %get-tuple-element.13.refs_0_), channel_id=1, source_target_pairs={{0,7},{1,0},{2,1},{3,2},{4,3},{5,4},{6,5},{7,6},{8,15},{9,8},{10,9... | collective-permute-start | bytes 1572872 | tf_op jit(solution)/shard_map/ppermute | solution.py:196
  164.8 22.6 %collective-permute-start.1 = (bf16[1024,256]{1,0:T(8,128)(2,1)S(1)}, bf16[1024,256]{1,0:T(8,128)(2,1)S(1)}, u32[]{:S(2)}, u32[]{:S(2)}) collective-permute-start(bf16[1024,256]{1,0:T(8,128)(2,1)S(1)} %get-tuple-element.13.refs_0_), channel_id=1, source_target_pairs={{0,6},{1,7},{2,0},{3,1},{4,2},{5,3},{6,4},{7,5},{8,14},{9,15},{10,... | collective-permute-start | bytes 1572872 | tf_op jit(solution)/shard_map/ppermute | solution.py:196
  167.5 39.8 %collective-permute-start.2 = (bf16[1024,256]{1,0:T(8,128)(2,1)S(1)}, bf16[1024,256]{1,0:T(8,128)(2,1)S(1)}, u32[]{:S(2)}, u32[]{:S(2)}) collective-permute-start(bf16[1024,256]{1,0:T(8,128)(2,1)S(1)} %get-tuple-element.13.refs_0_), channel_id=1, source_target_pairs={{0,5},{1,6},{2,7},{3,0},{4,1},{5,2},{6,3},{7,4},{8,13},{9,14},{10,... | collective-permute-start | bytes 1572872 | tf_op jit(solution)/shard_map/ppermute | solution.py:196
  170.3 37.0 %collective-permute-start.3 = (bf16[1024,256]{1,0:T(8,128)(2,1)S(1)}, bf16[1024,256]{1,0:T(8,128)(2,1)S(1)}, u32[]{:S(2)}, u32[]{:S(2)}) collective-permute-start(bf16[1024,256]{1,0:T(8,128)(2,1)S(1)} %get-tuple-element.13.refs_0_), channel_id=1, source_target_pairs={{0,4},{1,5},{2,6},{3,7},{4,0},{5,1},{6,2},{7,3},{8,12},{9,13},{10,... | collective-permute-start | bytes 1572872 | tf_op jit(solution)/shard_map/ppermute | solution.py:196
  209.3 0.8 copy-start.2
  210.1 0.8 copy-start.4
  210.9 0.8 copy-start.6
  212.8 1.0 copy-start.8
  213.9 34.5 %all-to-all-start.2 = ((bf16[4,64,1280]{2,1,0:T(8,128)(2,1)}), bf16[4,64,1280]{2,1,0:T(8,128)(2,1)S(1)}, u32[]{:S(2)}, u32[]{:S(2)}) async-start(bf16[4,64,1280]{2,1,0:T(8,128)(2,1)} %gram_early.1), calls=%async_computation.2 | async-start | bytes 1310720 | tf_op jit(solution)/shard_map/all_to_all | solution.py:200
  218.1 1.3 copy-start.9
  219.4 27.1 %copy-start.3 = (bf16[1024,256]{1,0:T(8,128)(2,1)S(1)}, bf16[1024,256]{1,0:T(8,128)(2,1)}, u32[]{:S(2)}) copy-start(bf16[1024,256]{1,0:T(8,128)(2,1)} %copy-done.2) | copy-start | bytes 1572868
  219.4 27.1 %copy-start.5 = (bf16[1024,256]{1,0:T(8,128)(2,1)S(1)}, bf16[1024,256]{1,0:T(8,128)(2,1)}, u32[]{:S(2)}) copy-start(bf16[1024,256]{1,0:T(8,128)(2,1)} %copy-done.4) | copy-start | bytes 1572868
  219.4 27.1 %copy-start.7 = (bf16[1024,256]{1,0:T(8,128)(2,1)S(1)}, bf16[1024,256]{1,0:T(8,128)(2,1)}, u32[]{:S(2)}) copy-start(bf16[1024,256]{1,0:T(8,128)(2,1)} %copy-done.6) | copy-start | bytes 1572868
  223.4 41.3 %copy-start.11 = (bf16[384,384]{1,0:T(8,128)(2,1)S(1)}, bf16[384,384]{1,0:T(8,128)(2,1)}, u32[]{:S(2)}) copy-start(bf16[384,384]{1,0:T(8,128)(2,1)} %constant.16.clone.turn_ref) | copy-start | bytes 884740
  223.4 9.9 %collective-permute-start.4 = (bf16[1024,128]{1,0:T(8,128)(2,1)S(1)}, bf16[1024,128]{1,0:T(8,128)(2,1)S(1)}, u32[]{:S(2)}, u32[]{:S(2)}) collective-permute-start(bf16[1024,128]{1,0:T(8,128)(2,1)S(1)} %hist_next.1.refs_5_), channel_id=1, source_target_pairs={{0,7},{1,0},{2,1},{3,2},{4,3},{5,4},{6,5},{7,6},{8,15},{9,8},{10,9... | collective-permute-start | bytes 786440 | tf_op jit(solution)/shard_map/ppermute | solution.py:196
  223.4 12.5 %collective-permute-start.5 = (bf16[1024,128]{1,0:T(8,128)(2,1)S(1)}, bf16[1024,128]{1,0:T(8,128)(2,1)S(1)}, u32[]{:S(2)}, u32[]{:S(2)}) collective-permute-start(bf16[1024,128]{1,0:T(8,128)(2,1)S(1)} %hist_next.1.refs_5_), channel_id=1, source_target_pairs={{0,6},{1,7},{2,0},{3,1},{4,2},{5,3},{6,4},{7,5},{8,14},{9,15},{10,... | collective-permute-start | bytes 786440 | tf_op jit(solution)/shard_map/ppermute | solution.py:196
  226.3 20.2 %collective-permute-start.6 = (bf16[1024,128]{1,0:T(8,128)(2,1)S(1)}, bf16[1024,128]{1,0:T(8,128)(2,1)S(1)}, u32[]{:S(2)}, u32[]{:S(2)}) collective-permute-start(bf16[1024,128]{1,0:T(8,128)(2,1)S(1)} %hist_next.1.refs_5_), channel_id=1, source_target_pairs={{0,5},{1,6},{2,7},{3,0},{4,1},{5,2},{6,3},{7,4},{8,13},{9,14},{10,... | collective-permute-start | bytes 786440 | tf_op jit(solution)/shard_map/ppermute | solution.py:196
  229.0 17.5 %collective-permute-start.7 = (bf16[1024,128]{1,0:T(8,128)(2,1)S(1)}, bf16[1024,128]{1,0:T(8,128)(2,1)S(1)}, u32[]{:S(2)}, u32[]{:S(2)}) collective-permute-start(bf16[1024,128]{1,0:T(8,128)(2,1)S(1)} %hist_next.1.refs_5_), channel_id=1, source_target_pairs={{0,4},{1,5},{2,6},{3,7},{4,0},{5,1},{6,2},{7,3},{8,12},{9,13},{10,... | collective-permute-start | bytes 786440 | tf_op jit(solution)/shard_map/ppermute | solution.py:196

commit v5 on v3

--- a/solution.py
+++ b/solution.py
@@ -36,34 +36,46 @@
     return jnp.dot(choose, window, preferred_element_type=jnp.float32)
 
 
-def pack_first(owners, bins_dev, events, starts_ref, info_ref, w_ref, out_ref):
+def lanes_from(ref, start):
+    line = start // 128
+    after = jnp.minimum(line + 1, ref.shape[0] - 1)
+    off = start - line * 128
+    back = lax.rem(128 - off, 128)
+    lane = lax.broadcasted_iota(jnp.int32, (1, 128), 1)
+    here = pltpu.roll(ref[pl.ds(line, 1), :], back, 1)
+    there = pltpu.roll(ref[pl.ds(after, 1), :], back, 1)
+    return jnp.where(lane < 128 - off, here, there)
+
+
+def pack_first(owners, bins_dev, starts_ref, bins_ref, nominal_ref, w_ref, out_ref):
+    events = w_ref.shape[0]
     lines = lax.broadcasted_iota(jnp.int32, (EXTRA, 128), 0)
 
     def one(o, _):
         start = starts_ref[o]
         rows = pick_rows(start, w_ref, events, slice(0, 2 * COLS))
-        at = jnp.minimum((start // 128) * 128, events - 256)
-        at = pl.multiple_of(at, 128)
-        span = pltpu.roll(info_ref[:, pl.ds(at, 256)], 256 - (start - at), 1)[:, :128]
-        local = span[0:1].astype(jnp.int32) - o * bins_dev
+        local = lanes_from(bins_ref, start) - o * bins_dev
         inside = (local >= 0) & (local < bins_dev)
-        high = jnp.where(inside, local // 32, -1).astype(jnp.float32)
-        low = jnp.where(inside, local % 32, 0).astype(jnp.float32)
-        nominal = jnp.where(inside, span[1:2], 0.0)
+        high = jnp.where(inside, local >> 5, -1).astype(jnp.float32)
+        low = jnp.where(inside, local & 31, 0).astype(jnp.float32)
+        nominal = jnp.where(inside, lanes_from(nominal_ref, start), 0.0)
         extra = jnp.where(lines == 0, high, jnp.where(lines == 1, low, jnp.where(lines == 2, nominal, 0.0)))
         out_ref[o] = jnp.concatenate([rows[:, :COLS], rows[:, COLS:], extra], axis=0).astype(jnp.bfloat16)
         return 0
 
-    lax.fori_loop(0, owners, one, 0, unroll=4)
-
-
-def pack_rest(owners, events, starts_ref, w_ref, out_ref):
-    def one(o, _):
-        rows = pick_rows(starts_ref[o], w_ref, events, slice(2 * COLS, 3 * COLS))
-        out_ref[o] = rows.astype(jnp.bfloat16)
+    lax.fori_loop(0, owners, one, 0, unroll=8)
+
+
+def pack_rest(n0, n1, place_ref, starts_ref, w_ref, *out_refs):
+    events = w_ref.shape[0]
+
+    def one(z, _):
+        for turn, out_ref in enumerate(out_refs):
+            start = starts_ref[z * n1 + lax.rem(place_ref[0] + turn, n1)]
+            out_ref[z] = pick_rows(start, w_ref, events, slice(2 * COLS, 3 * COLS)).astype(jnp.bfloat16)
         return 0
 
-    lax.fori_loop(0, owners, one, 0, unroll=4)
+    lax.fori_loop(0, n0, one, 0, unroll=2)
 
 
 def one_hot_of(bins_ref, at, size, bins_dev):
@@ -106,32 +118,48 @@
     out_ref[...] = acc[...].astype(jnp.bfloat16)
 
 
-def gram(turns, curve_ref, order_ref, *refs):
-    parts, out_ref = refs[:-1], refs[-1]
-    chunks = len(parts) // turns
-    own = jnp.concatenate([parts[c][...] for c in range(chunks)], axis=1)
+def left_side(curve_ref, order_ref, first_ref, last_ref):
+    own = jnp.concatenate([first_ref[...], last_ref[...]], axis=1)
     weighted = (curve_ref[...] * own.astype(jnp.float32)).astype(jnp.bfloat16)
-    lhs = lax.dot_general(
+    return lax.dot_general(
         order_ref[...], weighted, (((1,), (1,)), ((), ())), preferred_element_type=jnp.float32
     ).astype(jnp.bfloat16)
-    width = own.shape[1]
-    step = out_ref.shape[1]
+
+
+def gram_first(curve_ref, order_ref, last_ref, *refs):
+    firsts, (out_ref, lhs_ref) = refs[:-2], refs[-2:]
+    lhs = left_side(curve_ref, order_ref, firsts[0], last_ref)
+    lhs_ref[...] = lhs
+    wide, step = firsts[0].shape[1], out_ref.shape[1]
+    for k, part in enumerate(firsts):
+        full = jnp.dot(lhs, part[...], preferred_element_type=jnp.float32).astype(jnp.bfloat16)
+        for y in range(out_ref.shape[0]):
+            out_ref[y, :, k * wide : (k + 1) * wide] = full[y * step : (y + 1) * step]
+
+
+def gram_last(lhs_ref, *refs):
+    lasts, out_ref = refs[:-1], refs[-1]
+    lhs = lhs_ref[...]
+    wide, step = lasts[0].shape[1], out_ref.shape[1]
+    for k, part in enumerate(lasts):
+        full = jnp.dot(lhs, part[...], preferred_element_type=jnp.float32).astype(jnp.bfloat16)
+        for y in range(out_ref.shape[0]):
+            out_ref[y, :, k * wide : (k + 1) * wide] = full[y * step : (y + 1) * step]
+
+
+def add_across(turns, first_ref, last_ref, out_ref, wide):
+    n0 = out_ref.shape[0]
+    lines = first_ref.shape[1] // n0
+    first = jnp.sum(first_ref[...].astype(jnp.float32), axis=0)
+    last = jnp.sum(last_ref[...].astype(jnp.float32), axis=0)
+    wide[...] = jnp.zeros_like(wide)
     for k in range(turns):
-        partner = jnp.concatenate([parts[k * chunks + c][...] for c in range(chunks)], axis=1)
-        full = jnp.dot(lhs, partner, preferred_element_type=jnp.float32).astype(jnp.bfloat16)
-        for y in range(out_ref.shape[0]):
-            out_ref[y, :, k * width : (k + 1) * width] = full[y * step : (y + 1) * step]
-
-
-def add_across(got_ref, out_ref, wide):
-    lanes = got_ref.shape[2] // 128
-    total = jnp.sum(got_ref[...].astype(jnp.float32), axis=0)
-    n0 = out_ref.shape[0]
-    lines = total.shape[0] // n0
-    wide[...] = jnp.zeros_like(wide)
-    for z in range(n0):
-        for j in range(lanes):
-            wide[z, j * lines : (j + 1) * lines] = total[z * lines : (z + 1) * lines, j * 128 : (j + 1) * 128]
+        for t in range(3):
+            tile, at = (last, k * COLS) if t == 2 else (first, (2 * k + t) * COLS)
+            tile = tile[:, at : at + COLS]
+            at = (3 * k + t) * lines
+            for z in range(n0):
+                wide[z, at : at + lines] = tile[z * lines : (z + 1) * lines]
     out_ref[...] = wide[...].astype(jnp.bfloat16)
 
 
@@ -161,35 +189,38 @@
     bins_dev = background.shape[0]
     targets = jnp.arange(owners, dtype=jnp.int32)
     starts = jnp.sum((event_bins[None, :] < targets[:, None] * bins_dev).astype(jnp.int32), axis=1)
-    info = jnp.stack([event_bins.astype(f32), nominal.astype(f32)])
-    info = jnp.concatenate([info, jnp.zeros((6, events), f32)])
-
+    place = lax.axis_index(BINS[1])
     slab = 2 * CAP + EXTRA
     send_a = pl.pallas_call(
-        functools.partial(pack_first, owners, bins_dev, events),
+        functools.partial(pack_first, owners, bins_dev),
         out_shape=jax.ShapeDtypeStruct((owners, slab, COLS), bf16),
-        in_specs=[SMEM, VMEM, VMEM],
+        in_specs=[SMEM, VMEM, VMEM, VMEM],
         out_specs=VMEM,
         compiler_params=PARAMS,
         cost_estimate=cost(4 * owners * CAP * WIN * COLS, 2 * owners * slab * COLS * 2),
         name="pack_first",
-    )(starts, info, event_weights)
+    )(starts, event_bins.reshape(-1, 128), nominal.astype(f32).reshape(-1, 128), event_weights)
     got_a = exchange(send_a, BINS)
-    send_b = pl.pallas_call(
-        functools.partial(pack_rest, owners, events),
-        out_shape=jax.ShapeDtypeStruct((owners, CAP, COLS), bf16),
-        in_specs=[SMEM, VMEM],
-        out_specs=VMEM,
+    sends = pl.pallas_call(
+        functools.partial(pack_rest, n0, n1),
+        out_shape=[jax.ShapeDtypeStruct((n0, CAP, COLS), bf16)] * n1,
+        in_specs=[SMEM, SMEM, VMEM],
+        out_specs=[VMEM] * n1,
         compiler_params=PARAMS,
         cost_estimate=cost(2 * owners * CAP * WIN * COLS, 2 * owners * CAP * COLS * 2),
         name="pack_rest",
-    )(starts, event_weights)
-    send_b, got_a = lax.optimization_barrier((send_b, got_a))
-    got_b = exchange(send_b, BINS)
+    )(place.reshape(1).astype(jnp.int32), starts, event_weights)
+    mid = jnp.stack([from_behind(x, BINS[1], t) if t else x for t, x in enumerate(sends)], axis=1)
+    mid, got_a = lax.optimization_barrier((mid, got_a))
+    got_b = exchange(mid, BINS[0])
 
     total = owners * CAP
     extra = got_a[:, 2 * CAP :, :CAP].astype(f32)
-    local = (extra[:, 0] * 32.0 + extra[:, 1]).astype(jnp.int32).reshape(1, total)
+    local = (extra[:, 0] * 32.0 + extra[:, 1]).astype(jnp.int32)
+    back = local.reshape(n0, n1, CAP)[:, ::-1]
+    local_b = lax.dynamic_slice_in_dim(jnp.concatenate([back, back], axis=1), n1 - 1 - place, n1, axis=1)
+    local_b = local_b.reshape(1, total)
+    local = local.reshape(1, total)
     nom = jnp.broadcast_to(extra[:, 2].astype(bf16).reshape(1, total), (8, total))
     left, right = (got_a[:, i * CAP : (i + 1) * CAP].reshape(total, COLS) for i in range(2))
     first, curve = pl.pallas_call(
@@ -211,36 +242,49 @@
         compiler_params=PARAMS,
         cost_estimate=cost(2 * total * bins_dev * 256, total * COLS * 2),
         name="hist_next",
-    )(local, got_b.reshape(total, COLS))
-    tiles = [first, last]
-    chunks = len(tiles)
+    )(local_b, got_b.reshape(total, COLS))
     turns = groups // 2 + 1
-    moved = [[from_behind(t, "params", -k) if k else t for t in tiles] for k in range(turns)]
+    firsts = [from_behind(first, "params", -k) if k else first for k in range(turns)]
+    lasts = [from_behind(last, "params", -k) if k else last for k in range(turns)]
 
     lines = width // owners
     j = np.arange(width)
     source = ((j % (width // n1)) // lines * n1 + j // (width // n1)) * lines + j % lines
     order = np.zeros((width, width), np.float32)
     order[j, source] = 1.0
-    partial = pl.pallas_call(
-        functools.partial(gram, turns),
-        out_shape=jax.ShapeDtypeStruct((n1, width // n1, turns * width), bf16),
-        in_specs=[VMEM] * (2 + turns * chunks),
-        out_specs=VMEM,
-        compiler_params=PARAMS,
-        cost_estimate=cost(2 * bins_dev * width * width * (turns + 1), turns * width * bins_dev * 2),
-        name="gram",
-    )(curve, jnp.asarray(order, bf16), *[t for row in moved for t in row])
+    part_a, lhs = pl.pallas_call(
+        gram_first,
+        out_shape=[
+            jax.ShapeDtypeStruct((n1, width // n1, turns * 2 * COLS), bf16),
+            jax.ShapeDtypeStruct((width, bins_dev), bf16),
+        ],
+        in_specs=[VMEM] * (3 + turns),
+        out_specs=[VMEM] * 2,
+        compiler_params=PARAMS,
+        cost_estimate=cost(2 * bins_dev * width * 2 * COLS * (turns + 1), 2 * turns * COLS * bins_dev * 2),
+        name="gram_first",
+    )(curve, jnp.asarray(order, bf16), last, *firsts)
+    part_a, lhs = lax.optimization_barrier((exchange(part_a, BINS[1]), lhs))
+    part_b = pl.pallas_call(
+        gram_last,
+        out_shape=jax.ShapeDtypeStruct((n1, width // n1, turns * COLS), bf16),
+        in_specs=[VMEM] * (1 + turns),
+        out_specs=VMEM,
+        compiler_params=PARAMS,
+        cost_estimate=cost(2 * bins_dev * width * COLS * turns, turns * COLS * bins_dev * 2),
+        name="gram_last",
+    )(lhs, *lasts)
+    part_b = exchange(part_b, BINS[1])
     packed = -(-lines * turns * width // 128 // 16) * 16
     across = pl.pallas_call(
-        add_across,
+        functools.partial(add_across, turns),
         out_shape=jax.ShapeDtypeStruct((n0, packed, 128), bf16),
-        in_specs=[VMEM],
+        in_specs=[VMEM] * 2,
         out_specs=VMEM,
         scratch_shapes=[pltpu.VMEM((n0, packed, 128), f32)],
         compiler_params=PARAMS,
         name="add_across",
-    )(exchange(partial, BINS[1]))
+    )(part_a, part_b)
     return pl.pallas_call(
         functools.partial(add_along, 1.0 / (bins_dev * owners)),
         out_shape=jax.ShapeDtypeStruct((lines, turns * width), f32),

time: 293 us -> 290 us (0.990)
  waiting for transfers between devices: 164 us -> 143 us
  starting transfers between devices: 44.7 us -> 58.4 us
  local copies, waits for them, and re-layouts: 6.06 us -> 10.3 us
  blocking collectives: 46.9 us -> 49.9 us
    all_to_all x2 -> x3, waiting for transfers between devices: 151 us -> 119 us  [exchange(): return lax.all_to_all(value, axis, split_axis=0, concat_axis=0, tiled=True)]
    ppermute x8 -> x11, starting transfers between devices: 19.8 us -> 31.8 us  [from_behind(): return lax.ppermute(value, axis, pairs)]
    ppermute x8 -> x11, waiting for transfers between devices: 13.1 us -> 24 us  [from_behind(): return lax.ppermute(value, axis, pairs)]
    all_to_all x2, blocking collectives: 46.9 us -> 49.9 us  [exchange(): return lax.all_to_all(value, axis, split_axis=0, concat_axis=0, tiled=True)]
    pallas_call x4 -> x5, Pallas kernels: 14 us -> 12.1 us  [the longest x1 4.1 us: body(): pl.pallas_call(functools.partial(pack_first, owners, bins_dev), out_shape...]
    all_to_all x2 -> x3, starting transfers between devices: 24.9 us -> 26.6 us  [exchange(): return lax.all_to_all(value, axis, split_axis=0, concat_axis=0, tiled=True)]
  transfers between devices with their start and end apart: 10 -> 14, of which waited for: 4 -> 8; matrix products, arithmetic and copies ran while one was open for 2% -> 2% of each run, Pallas kernels for 5% -> 5%
where the time goes in v5:
time: 290 us; the launch traced here: 289 us
  waiting for transfers between devices  143 us (49%)
  starting transfers between devices  58.4 us (20%)
  blocking collectives  49.9 us (17%)
  Pallas kernels  23.3 us (8%)
  local copies, waits for them, and re-layouts  10.3 us (4%)
  other arithmetic  3.55 us (1%)
    all_to_all x3, waiting for transfers between devices, exchange(): return lax.all_to_all(value, axis, split_axis=0, concat_axis=0, tiled=True)  119 us
    all_to_all x2, blocking collectives, exchange(): return lax.all_to_all(value, axis, split_axis=0, concat_axis=0, tiled=True)  49.9 us
    ppermute x11, starting transfers between devices, from_behind(): return lax.ppermute(value, axis, pairs)  31.8 us
    all_to_all x3, starting transfers between devices, exchange(): return lax.all_to_all(value, axis, split_axis=0, concat_axis=0, tiled=True)  26.6 us
    ppermute x11, waiting for transfers between devices, from_behind(): return lax.ppermute(value, axis, pairs)  24 us
    pallas_call x1, Pallas kernels, body(): pl.pallas_call(hist_first, out_shape=[jax.ShapeDtypeStruct((bins_dev, 2 *...  6.55 us
  transfers between devices with their start and end apart: 14, of which 8 were waited for; matrix products, arithmetic and copies ran while one was open for 2% of the time, Pallas kernels for 5%

profile of v5, /device:TPU:6, one launch (start us, length us, event | category | flops | bytes accessed | tf_op | source)
XLA Modules:
  0.0 289.0 jit_solution(7423106691190618417)
XLA Ops:
  0.7 0.9 convert_reduce_fusion.starts_ref
  1.7 1.7 copy-done
  4.0 4.1 %pack_first.1 = bf16[64,152,128]{2,1,0:T(8,128)(2,1)} custom-call(s32[64]{0:T(128)S(1)} %convert_reduce_fusion.starts_ref, s32[24,128]{1,0:T(8,128)S(1)} %bitcast.19, f32[24,128]{1,0:T(8,128)S(1)} %bitcast_convert_fusion.nominal_ref, bf16[3072,384]{1,0:T(8,128)(2,1)S(1)} %copy-done), custom_call_target="tpu_custom_call" | custom-call | flops 226492416 | bytes 4980736 | tf_op jit(solution)/shard_map/pack_first/pallas_call | solution.py:194
  8.1 19.1 %all-to-all-start = ((bf16[64,152,128]{2,1,0:T(8,128)(2,1)}), bf16[64,152,128]{2,1,0:T(8,128)(2,1)}, u32[]{:S(2)}, u32[]{:S(2)}) async-start(bf16[64,152,128]{2,1,0:T(8,128)(2,1)} %pack_first.1), calls=%async_computation | async-start | bytes 4980736 | tf_op jit(solution)/shard_map/all_to_all | solution.py:180
  27.3 2.5 pack_rest.1
  29.8 3.4 %collective-permute-start = (bf16[16,72,128]{2,1,0:T(8,128)(2,1)S(1)}, bf16[16,72,128]{2,1,0:T(8,128)(2,1)S(1)}, u32[]{:S(2)}, u32[]{:S(2)}) collective-permute-start(bf16[16,72,128]{2,1,0:T(8,128)(2,1)S(1)} %get-tuple-element.18), channel_id=1, source_target_pairs={{0,8},{8,16},{16,24},{24,0},{1,9},{9,17},{17,25},{25,1},{2,10},{10... | collective-permute-start | bytes 884744 | tf_op jit(solution)/shard_map/ppermute | solution.py:176
  33.2 4.6 %collective-permute-start.1 = (bf16[16,72,128]{2,1,0:T(8,128)(2,1)S(1)}, bf16[16,72,128]{2,1,0:T(8,128)(2,1)S(1)}, u32[]{:S(2)}, u32[]{:S(2)}) collective-permute-start(bf16[16,72,128]{2,1,0:T(8,128)(2,1)S(1)} %get-tuple-element.19), channel_id=1, source_target_pairs={{0,16},{8,24},{16,0},{24,8},{1,17},{9,25},{17,1},{25,9},{2,18},{10... | collective-permute-start | bytes 884744 | tf_op jit(solution)/shard_map/ppermute | solution.py:176
  37.8 3.4 %collective-permute-start.2 = (bf16[16,72,128]{2,1,0:T(8,128)(2,1)S(1)}, bf16[16,72,128]{2,1,0:T(8,128)(2,1)S(1)}, u32[]{:S(2)}, u32[]{:S(2)}) collective-permute-start(bf16[16,72,128]{2,1,0:T(8,128)(2,1)S(1)} %get-tuple-element.20), channel_id=1, source_target_pairs={{0,24},{8,0},{16,8},{24,16},{1,25},{9,1},{17,9},{25,17},{2,26},{10... | collective-permute-start | bytes 884744 | tf_op jit(solution)/shard_map/ppermute | solution.py:176
  41.2 4.1 %collective-permute-done = bf16[16,72,128]{2,1,0:T(8,128)(2,1)S(1)} collective-permute-done((bf16[16,72,128]{2,1,0:T(8,128)(2,1)S(1)}, bf16[16,72,128]{2,1,0:T(8,128)(2,1)S(1)}, u32[]{:S(2)}, u32[]{:S(2)}) %collective-permute-start) | collective-permute-done | bytes 294944 | tf_op jit(solution)/shard_map/ppermute | solution.py:176
  45.3 9.4 %collective-permute-done.1 = bf16[16,72,128]{2,1,0:T(8,128)(2,1)S(1)} collective-permute-done((bf16[16,72,128]{2,1,0:T(8,128)(2,1)S(1)}, bf16[16,72,128]{2,1,0:T(8,128)(2,1)S(1)}, u32[]{:S(2)}, u32[]{:S(2)}) %collective-permute-start.1) | collective-permute-done | bytes 294944 | tf_op jit(solution)/shard_map/ppermute | solution.py:176
  54.8 89.4 %all-to-all-done = bf16[64,152,128]{2,1,0:T(8,128)(2,1)} async-done(((bf16[64,152,128]{2,1,0:T(8,128)(2,1)}), bf16[64,152,128]{2,1,0:T(8,128)(2,1)}, u32[]{:S(2)}, u32[]{:S(2)}) %all-to-all-start) | async-done | bytes 2490400 | tf_op jit(solution)/shard_map/all_to_all | solution.py:180
  144.2 1.1 copy.16
  145.3 3.8 %all-to-all-start.1 = ((bf16[16,4,72,128]{3,2,1,0:T(8,128)(2,1)}), bf16[16,4,72,128]{3,2,1,0:T(8,128)(2,1)S(1)}, u32[]{:S(2)}, u32[]{:S(2)}) async-start(bf16[16,4,72,128]{3,2,1,0:T(8,128)(2,1)} %copy.16), calls=%async_computation.1 | async-start | bytes 2359296 | tf_op jit(solution)/shard_map/all_to_all | solution.py:180
  152.0 1.0 slice_reduce_fusion
  153.1 1.8 fusion.4
  154.9 6.5 %hist_first.1 = (bf16[1024,256]{1,0:T(8,128)(2,1)S(1)}, f32[1024,1]{1,0:T(8,128)S(1)}) custom-call(s32[1,4608]{1,0:T(1,128)S(1)} %convert_element_type.35.bins_ref, bf16[8,4608]{1,0:T(8,128)(2,1)S(1)} %broadcast_in_dim.2.nominal_ref, f32[1024,1]{1,0:T(8,128)S(1)} %copy.14.background_ref, f32[1024,1]{1,0:T(8,128)S(1)} %copy.15.observed_ref, ...), custom_call_target="tpu_custom_call" | custom-call | flops 4831838208 | bytes 2359296 | tf_op jit(solution)/shard_map/hist_first/pallas_call | solution.py:226
  162.3 2.7 collective-permute-start.4
  165.0 2.9 collective-permute-start.5
  167.9 4.3 %collective-permute-start.6 = (bf16[1024,256]{1,0:T(8,128)(2,1)S(1)}, bf16[1024,256]{1,0:T(8,128)(2,1)}, u32[]{:S(2)}, u32[]{:S(2)}) collective-permute-start(bf16[1024,256]{1,0:T(8,128)(2,1)S(1)} %get-tuple-element.24.refs_0_), channel_id=1, source_target_pairs={{0,4},{1,5},{2,6},{3,7},{4,0},{5,1},{6,2},{7,3},{8,12},{9,13},{10,... | collective-permute-start | bytes 1572872 | tf_op jit(solution)/shard_map/ppermute | solution.py:176
  172.4 29.6 %all-to-all-done.1 = bf16[16,4,72,128]{3,2,1,0:T(8,128)(2,1)S(1)} async-done(((bf16[16,4,72,128]{3,2,1,0:T(8,128)(2,1)}), bf16[16,4,72,128]{3,2,1,0:T(8,128)(2,1)S(1)}, u32[]{:S(2)}, u32[]{:S(2)}) %all-to-all-start.1) | async-done | bytes 1179680 | tf_op jit(solution)/shard_map/all_to_all | solution.py:180
  202.1 4.0 %hist_next.1.last_ref.refs_0_ = bf16[1024,128]{1,0:T(8,128)(2,1)S(1)} custom-call(s32[1,4608]{1,0:T(1,128)S(1)} %reshape.85.bins_ref, bf16[4608,128]{1,0:T(8,128)(2,1)S(1)} %bitcast.15), custom_call_target="tpu_custom_call" | custom-call | flops 2415919104 | bytes 1179648 | tf_op jit(solution)/shard_map/hist_next/pallas_call | solution.py:236
  206.9 1.0 copy-done.4
  208.0 3.8 %gram_first.1 = (bf16[4,96,1280]{2,1,0:T(8,128)(2,1)}, bf16[384,1024]{1,0:T(8,128)(2,1)S(1)}) custom-call(f32[1024,1]{1,0:T(8,128)S(1)} %copy-done.7, bf16[384,384]{1,0:T(8,128)(2,1)S(1)} %copy-done.5, bf16[1024,128]{1,0:T(8,128)(2,1)S(1)} %hist_next.1.last_ref.refs_0_, bf16[1024,256]{1,0:T(8,128)(2,1)S(1)} %get-tuple-element.24.refs_0_, ...), custom_call_target="tpu_custom_call" | custom-call | flops 1207959552 | bytes 2621440 | tf_op jit(solution)/shard_map/gram_first/pallas_call | solution.py:255
  211.8 3.7 %all-to-all-start.2 = ((bf16[4,96,1280]{2,1,0:T(8,128)(2,1)}), bf16[4,96,1280]{2,1,0:T(8,128)(2,1)S(1)}, u32[]{:S(2)}, u32[]{:S(2)}) async-start(bf16[4,96,1280]{2,1,0:T(8,128)(2,1)} %get-tuple-element.25), calls=%async_computation.2 | async-start | bytes 1966080 | tf_op jit(solution)/shard_map/all_to_all | solution.py:180
  215.5 3.3 %collective-permute-start.10 = (bf16[1024,128]{1,0:T(8,128)(2,1)S(1)}, bf16[1024,128]{1,0:T(8,128)(2,1)S(1)}, u32[]{:S(2)}, u32[]{:S(2)}) collective-permute-start(bf16[1024,128]{1,0:T(8,128)(2,1)S(1)} %hist_next.1.last_ref.refs_0_), channel_id=1, source_target_pairs={{0,4},{1,5},{2,6},{3,7},{4,0},{5,1},{6,2},{7,3},{8,12},{9,13},{10,... | collective-permute-start | bytes 786440 | tf_op jit(solution)/shard_map/ppermute | solution.py:176
  218.8 1.9 collective-permute-start.8
  220.8 5.3 %collective-permute-start.9 = (bf16[1024,128]{1,0:T(8,128)(2,1)S(1)}, bf16[1024,128]{1,0:T(8,128)(2,1)S(1)}, u32[]{:S(2)}, u32[]{:S(2)}) collective-permute-start(bf16[1024,128]{1,0:T(8,128)(2,1)S(1)} %hist_next.1.last_ref.refs_0_), channel_id=1, source_target_pairs={{0,5},{1,6},{2,7},{3,0},{4,1},{5,2},{6,3},{7,4},{8,13},{9,14},{10,... | collective-permute-start | bytes 786440 | tf_op jit(solution)/shard_map/ppermute | solution.py:176
  226.3 3.1 %collective-permute-done.7.refs_1_ = bf16[1024,128]{1,0:T(8,128)(2,1)S(1)} collective-permute-done((bf16[1024,128]{1,0:T(8,128)(2,1)S(1)}, bf16[1024,128]{1,0:T(8,128)(2,1)S(1)}, u32[]{:S(2)}, u32[]{:S(2)}) %collective-permute-start.7) | collective-permute-done | bytes 262176 | tf_op jit(solution)/shard_map/ppermute | solution.py:176
  229.4 7.0 %collective-permute-done.8.refs_2_ = bf16[1024,128]{1,0:T(8,128)(2,1)S(1)} collective-permute-done((bf16[1024,128]{1,0:T(8,128)(2,1)S(1)}, bf16[1024,128]{1,0:T(8,128)(2,1)S(1)}, u32[]{:S(2)}, u32[]{:S(2)}) %collective-permute-start.8) | collective-permute-done | bytes 262176 | tf_op jit(solution)/shard_map/ppermute | solution.py:176
  236.8 1.2 gram_last.1
  238.0 14.0 %all_to_all.25.last_ref = bf16[4,96,640]{2,1,0:T(8,128)(2,1)S(1)} all-to-all(bf16[4,96,640]{2,1,0:T(8,128)(2,1)S(1)} %gram_last.1), channel_id=1, replica_groups=mesh['bins_0'=16,'bins_1'=4,'params'=8] {'bins_1'}, dimensions={0} | all-to-all | bytes 983040 | tf_op jit(solution)/shard_map/all_to_all | solution.py:180
  252.4 35.9 %all_to_all.26.got_ref = bf16[16,96,128]{2,1,0:T(8,128)(2,1)S(1)} all-to-all(bf16[16,96,128]{2,1,0:T(8,128)(2,1)S(1)} %add_across.1), channel_id=1, replica_groups=mesh['bins_0'=16,'bins_1'=4,'params'=8] {'bins_0'}, dimensions={0} | all-to-all | bytes 786432 | tf_op jit(solution)/shard_map/all_to_all | solution.py:180
  (44 shorter events, 8.0 us)
Async XLA Ops:
  1.7 1.7 copy-start
  3.3 0.7 copy-start.2
  8.1 19.1 %copy-start.1 = (bf16[3072,384]{1,0:T(8,128)(2,1)S(1)}, bf16[3072,384]{1,0:T(8,128)(2,1)}, u32[]{:S(2)}) copy-start(bf16[3072,384]{1,0:T(8,128)(2,1)} %w_ref.3) | copy-start | bytes 7077892
  8.1 136.1 %all-to-all-start = ((bf16[64,152,128]{2,1,0:T(8,128)(2,1)}), bf16[64,152,128]{2,1,0:T(8,128)(2,1)}, u32[]{:S(2)}, u32[]{:S(2)}) async-start(bf16[64,152,128]{2,1,0:T(8,128)(2,1)} %pack_first.1), calls=%async_computation | async-start | bytes 4980736 | tf_op jit(solution)/shard_map/all_to_all | solution.py:180
  29.8 15.5 %collective-permute-start = (bf16[16,72,128]{2,1,0:T(8,128)(2,1)S(1)}, bf16[16,72,128]{2,1,0:T(8,128)(2,1)S(1)}, u32[]{:S(2)}, u32[]{:S(2)}) collective-permute-start(bf16[16,72,128]{2,1,0:T(8,128)(2,1)S(1)} %get-tuple-element.18), channel_id=1, source_target_pairs={{0,8},{8,16},{16,24},{24,0},{1,9},{9,17},{17,25},{25,1},{2,10},{10... | collective-permute-start | bytes 884744 | tf_op jit(solution)/shard_map/ppermute | solution.py:176
  33.2 21.4 %collective-permute-start.1 = (bf16[16,72,128]{2,1,0:T(8,128)(2,1)S(1)}, bf16[16,72,128]{2,1,0:T(8,128)(2,1)S(1)}, u32[]{:S(2)}, u32[]{:S(2)}) collective-permute-start(bf16[16,72,128]{2,1,0:T(8,128)(2,1)S(1)} %get-tuple-element.19), channel_id=1, source_target_pairs={{0,16},{8,24},{16,0},{24,8},{1,17},{9,25},{17,1},{25,9},{2,18},{10... | collective-permute-start | bytes 884744 | tf_op jit(solution)/shard_map/ppermute | solution.py:176
  37.8 16.9 %collective-permute-start.2 = (bf16[16,72,128]{2,1,0:T(8,128)(2,1)S(1)}, bf16[16,72,128]{2,1,0:T(8,128)(2,1)S(1)}, u32[]{:S(2)}, u32[]{:S(2)}) collective-permute-start(bf16[16,72,128]{2,1,0:T(8,128)(2,1)S(1)} %get-tuple-element.20), channel_id=1, source_target_pairs={{0,24},{8,0},{16,8},{24,16},{1,25},{9,1},{17,9},{25,17},{2,26},{10... | collective-permute-start | bytes 884744 | tf_op jit(solution)/shard_map/ppermute | solution.py:176
  145.3 3.8 %copy-start.8 = (f32[1024]{0:T(1024)S(1)}, f32[1024]{0:T(1024)}, u32[]{:S(2)}) copy-start(f32[1024]{0:T(1024)} %param.9) | copy-start | bytes 12292
  145.3 4.1 %copy-start.9 = (f32[1024]{0:T(1024)S(1)}, f32[1024]{0:T(1024)}, u32[]{:S(2)}) copy-start(f32[1024]{0:T(1024)} %param.10) | copy-start | bytes 12292
  145.3 56.8 %all-to-all-start.1 = ((bf16[16,4,72,128]{3,2,1,0:T(8,128)(2,1)}), bf16[16,4,72,128]{3,2,1,0:T(8,128)(2,1)S(1)}, u32[]{:S(2)}, u32[]{:S(2)}) async-start(bf16[16,4,72,128]{3,2,1,0:T(8,128)(2,1)} %copy.16), calls=%async_computation.1 | async-start | bytes 2359296 | tf_op jit(solution)/shard_map/all_to_all | solution.py:180
  161.5 0.8 copy-start.6
  162.3 43.8 %collective-permute-start.3 = (bf16[1024,256]{1,0:T(8,128)(2,1)S(1)}, bf16[1024,256]{1,0:T(8,128)(2,1)S(1)}, u32[]{:S(2)}, u32[]{:S(2)}) collective-permute-start(bf16[1024,256]{1,0:T(8,128)(2,1)S(1)} %get-tuple-element.24.refs_0_), channel_id=1, source_target_pairs={{0,7},{1,0},{2,1},{3,2},{4,3},{5,4},{6,5},{7,6},{8,15},{9,8},{10,9... | collective-permute-start | bytes 1572872 | tf_op jit(solution)/shard_map/ppermute | solution.py:176
  162.3 43.8 %collective-permute-start.4 = (bf16[1024,256]{1,0:T(8,128)(2,1)S(1)}, bf16[1024,256]{1,0:T(8,128)(2,1)S(1)}, u32[]{:S(2)}, u32[]{:S(2)}) collective-permute-start(bf16[1024,256]{1,0:T(8,128)(2,1)S(1)} %get-tuple-element.24.refs_0_), channel_id=1, source_target_pairs={{0,6},{1,7},{2,0},{3,1},{4,2},{5,3},{6,4},{7,5},{8,14},{9,15},{10,... | collective-permute-start | bytes 1572872 | tf_op jit(solution)/shard_map/ppermute | solution.py:176
  165.0 41.9 %collective-permute-start.5 = (bf16[1024,256]{1,0:T(8,128)(2,1)S(1)}, bf16[1024,256]{1,0:T(8,128)(2,1)}, u32[]{:S(2)}, u32[]{:S(2)}) collective-permute-start(bf16[1024,256]{1,0:T(8,128)(2,1)S(1)} %get-tuple-element.24.refs_0_), channel_id=1, source_target_pairs={{0,5},{1,6},{2,7},{3,0},{4,1},{5,2},{6,3},{7,4},{8,13},{9,14},{10,... | collective-permute-start | bytes 1572872 | tf_op jit(solution)/shard_map/ppermute | solution.py:176
  167.9 39.0 %collective-permute-start.6 = (bf16[1024,256]{1,0:T(8,128)(2,1)S(1)}, bf16[1024,256]{1,0:T(8,128)(2,1)}, u32[]{:S(2)}, u32[]{:S(2)}) collective-permute-start(bf16[1024,256]{1,0:T(8,128)(2,1)S(1)} %get-tuple-element.24.refs_0_), channel_id=1, source_target_pairs={{0,4},{1,5},{2,6},{3,7},{4,0},{5,1},{6,2},{7,3},{8,12},{9,13},{10,... | collective-permute-start | bytes 1572872 | tf_op jit(solution)/shard_map/ppermute | solution.py:176
  202.1 4.8 %copy-start.5 = (bf16[384,384]{1,0:T(8,128)(2,1)S(1)}, bf16[384,384]{1,0:T(8,128)(2,1)}, u32[]{:S(2)}) copy-start(bf16[384,384]{1,0:T(8,128)(2,1)} %constant.18.clone.order_ref) | copy-start | bytes 884740
  202.1 4.8 %copy-start.7 = (f32[1024,1]{1,0:T(8,128)S(1)}, f32[1024,1]{1,0:T(8,128)}, u32[]{:S(2)}) copy-start(f32[1024,1]{1,0:T(8,128)} %copy-done.6) | copy-start | bytes 12292
  206.1 0.8 copy-start.3
  206.9 1.0 copy-start.4
  211.8 14.5 %all-to-all-start.2 = ((bf16[4,96,1280]{2,1,0:T(8,128)(2,1)}), bf16[4,96,1280]{2,1,0:T(8,128)(2,1)S(1)}, u32[]{:S(2)}, u32[]{:S(2)}) async-start(bf16[4,96,1280]{2,1,0:T(8,128)(2,1)} %get-tuple-element.25), calls=%async_computation.2 | async-start | bytes 1966080 | tf_op jit(solution)/shard_map/all_to_all | solution.py:180
  215.5 10.8 %collective-permute-start.10 = (bf16[1024,128]{1,0:T(8,128)(2,1)S(1)}, bf16[1024,128]{1,0:T(8,128)(2,1)S(1)}, u32[]{:S(2)}, u32[]{:S(2)}) collective-permute-start(bf16[1024,128]{1,0:T(8,128)(2,1)S(1)} %hist_next.1.last_ref.refs_0_), channel_id=1, source_target_pairs={{0,4},{1,5},{2,6},{3,7},{4,0},{5,1},{6,2},{7,3},{8,12},{9,13},{10,... | collective-permute-start | bytes 786440 | tf_op jit(solution)/shard_map/ppermute | solution.py:176
  218.8 10.6 %collective-permute-start.7 = (bf16[1024,128]{1,0:T(8,128)(2,1)S(1)}, bf16[1024,128]{1,0:T(8,128)(2,1)S(1)}, u32[]{:S(2)}, u32[]{:S(2)}) collective-permute-start(bf16[1024,128]{1,0:T(8,128)(2,1)S(1)} %hist_next.1.last_ref.refs_0_), channel_id=1, source_target_pairs={{0,7},{1,0},{2,1},{3,2},{4,3},{5,4},{6,5},{7,6},{8,15},{9,8},{10,9... | collective-permute-start | bytes 786440 | tf_op jit(solution)/shard_map/ppermute | solution.py:176
  218.8 17.6 %collective-permute-start.8 = (bf16[1024,128]{1,0:T(8,128)(2,1)S(1)}, bf16[1024,128]{1,0:T(8,128)(2,1)S(1)}, u32[]{:S(2)}, u32[]{:S(2)}) collective-permute-start(bf16[1024,128]{1,0:T(8,128)(2,1)S(1)} %hist_next.1.last_ref.refs_0_), channel_id=1, source_target_pairs={{0,6},{1,7},{2,0},{3,1},{4,2},{5,3},{6,4},{7,5},{8,14},{9,15},{10,... | collective-permute-start | bytes 786440 | tf_op jit(solution)/shard_map/ppermute | solution.py:176
  220.8 16.0 %collective-permute-start.9 = (bf16[1024,128]{1,0:T(8,128)(2,1)S(1)}, bf16[1024,128]{1,0:T(8,128)(2,1)S(1)}, u32[]{:S(2)}, u32[]{:S(2)}) collective-permute-start(bf16[1024,128]{1,0:T(8,128)(2,1)S(1)} %hist_next.1.last_ref.refs_0_), channel_id=1, source_target_pairs={{0,5},{1,6},{2,7},{3,0},{4,1},{5,2},{6,3},{7,4},{8,13},{9,14},{10,... | collective-permute-start | bytes 786440 | tf_op jit(solution)/shard_map/ppermute | solution.py:176

commit v6 on v5

--- a/solution.py
+++ b/solution.py
@@ -126,25 +126,27 @@
     ).astype(jnp.bfloat16)
 
 
-def gram_first(curve_ref, order_ref, last_ref, *refs):
+def gram_first(slots_ref, curve_ref, order_ref, last_ref, *refs):
     firsts, (out_ref, lhs_ref) = refs[:-2], refs[-2:]
     lhs = left_side(curve_ref, order_ref, firsts[0], last_ref)
     lhs_ref[...] = lhs
     wide, step = firsts[0].shape[1], out_ref.shape[1]
     for k, part in enumerate(firsts):
         full = jnp.dot(lhs, part[...], preferred_element_type=jnp.float32).astype(jnp.bfloat16)
+        at = pl.multiple_of(slots_ref[k] * wide, wide)
         for y in range(out_ref.shape[0]):
-            out_ref[y, :, k * wide : (k + 1) * wide] = full[y * step : (y + 1) * step]
-
-
-def gram_last(lhs_ref, *refs):
+            out_ref[y, :, pl.ds(at, wide)] = full[y * step : (y + 1) * step]
+
+
+def gram_last(slots_ref, lhs_ref, *refs):
     lasts, out_ref = refs[:-1], refs[-1]
     lhs = lhs_ref[...]
     wide, step = lasts[0].shape[1], out_ref.shape[1]
     for k, part in enumerate(lasts):
         full = jnp.dot(lhs, part[...], preferred_element_type=jnp.float32).astype(jnp.bfloat16)
+        at = pl.multiple_of(slots_ref[k] * wide, wide)
         for y in range(out_ref.shape[0]):
-            out_ref[y, :, k * wide : (k + 1) * wide] = full[y * step : (y + 1) * step]
+            out_ref[y, :, pl.ds(at, wide)] = full[y * step : (y + 1) * step]
 
 
 def add_across(turns, first_ref, last_ref, out_ref, wide):
@@ -174,6 +176,19 @@
     count = lax.axis_size(axis)
     pairs = [(source, (source + steps) % count) for source in range(count)]
     return lax.ppermute(value, axis, pairs)
+
+
+def partners(tile):
+    count = lax.axis_size("params")
+    if count != 8:
+        return [from_behind(tile, "params", -k) for k in range(1, count // 2 + 1)], list(range(1, count // 2 + 1))
+    pairs = [(source, source ^ 1) for source in range(count)]
+    core = lax.rem(lax.axis_index("params"), 2)
+    four = from_behind(tile, "params", -4)
+    two = from_behind(tile, "params", -2)
+    two_other = lax.ppermute(two, "params", pairs)
+    other = lax.ppermute(jnp.where(core == 1, tile, four), "params", pairs)
+    return [two, four, two_other, other], [2, 4, 3 - 2 * core, 1 + 2 * core]
 
 
 def exchange(value, axis):
@@ -244,8 +259,10 @@
         name="hist_next",
     )(local_b, got_b.reshape(total, COLS))
     turns = groups // 2 + 1
-    firsts = [from_behind(first, "params", -k) if k else first for k in range(turns)]
-    lasts = [from_behind(last, "params", -k) if k else last for k in range(turns)]
+    firsts, slots = partners(first)
+    firsts = [first] + firsts
+    lasts = [last] + partners(last)[0]
+    slots = jnp.stack([jnp.asarray(k, jnp.int32) for k in [0] + slots])
 
     lines = width // owners
     j = np.arange(width)
@@ -258,22 +275,22 @@
             jax.ShapeDtypeStruct((n1, width // n1, turns * 2 * COLS), bf16),
             jax.ShapeDtypeStruct((width, bins_dev), bf16),
         ],
-        in_specs=[VMEM] * (3 + turns),
+        in_specs=[SMEM] + [VMEM] * (3 + turns),
         out_specs=[VMEM] * 2,
         compiler_params=PARAMS,
         cost_estimate=cost(2 * bins_dev * width * 2 * COLS * (turns + 1), 2 * turns * COLS * bins_dev * 2),
         name="gram_first",
-    )(curve, jnp.asarray(order, bf16), last, *firsts)
+    )(slots, curve, jnp.asarray(order, bf16), last, *firsts)
     part_a, lhs = lax.optimization_barrier((exchange(part_a, BINS[1]), lhs))
     part_b = pl.pallas_call(
         gram_last,
         out_shape=jax.ShapeDtypeStruct((n1, width // n1, turns * COLS), bf16),
-        in_specs=[VMEM] * (1 + turns),
+        in_specs=[SMEM] + [VMEM] * (1 + turns),
         out_specs=VMEM,
         compiler_params=PARAMS,
         cost_estimate=cost(2 * bins_dev * width * COLS * turns, turns * COLS * bins_dev * 2),
         name="gram_last",
-    )(lhs, *lasts)
+    )(slots, lhs, *lasts)
     part_b = exchange(part_b, BINS[1])
     packed = -(-lines * turns * width // 128 // 16) * 16
     across = pl.pallas_call(

time: 290 us -> 281 us (0.969)
  blocking collectives: 49.9 us -> 45.9 us
  waiting for transfers between devices: 143 us -> 139 us
    all_to_all x3, waiting for transfers between devices: 119 us -> 99.9 us  [exchange(): return lax.all_to_all(value, axis, split_axis=0, concat_axis=0, tiled=True)]
    ppermute x11 -> x7, waiting for transfers between devices: 24 us -> 37.4 us  [from_behind(): return lax.ppermute(value, axis, pairs)]
    ppermute x11 -> x7, starting transfers between devices: 31.8 us -> 21.9 us  [from_behind(): return lax.ppermute(value, axis, pairs)]
    ppermute x0 -> x4, starting transfers between devices: none -> 7.65 us  [the longest x2 3.83 us: partners(): other = lax.ppermute(jnp.where(core == 1, tile, four), 'params', pairs)]
    all_to_all x2, blocking collectives: 49.9 us -> 45.9 us  [exchange(): return lax.all_to_all(value, axis, split_axis=0, concat_axis=0, tiled=True)]
  transfers between devices with their start and end apart: 14 -> 14, of which waited for: 8 -> 8; matrix products, arithmetic and copies ran while one was open for 2% -> 3% of each run, Pallas kernels for 5% -> 6%
where the time goes in v6:
time: 281 us; the launch traced here: 280 us
  waiting for transfers between devices  139 us (49%)
  starting transfers between devices  56.2 us (20%)
  blocking collectives  45.9 us (16%)
  Pallas kernels  23.9 us (9%)
  local copies, waits for them, and re-layouts  9.63 us (3%)
  other arithmetic  4.98 us (2%)
    all_to_all x3, waiting for transfers between devices, exchange(): return lax.all_to_all(value, axis, split_axis=0, concat_axis=0, tiled=True)  99.9 us
    all_to_all x2, blocking collectives, exchange(): return lax.all_to_all(value, axis, split_axis=0, concat_axis=0, tiled=True)  45.9 us
    ppermute x7, waiting for transfers between devices, from_behind(): return lax.ppermute(value, axis, pairs)  37.4 us
    all_to_all x3, starting transfers between devices, exchange(): return lax.all_to_all(value, axis, split_axis=0, concat_axis=0, tiled=True)  26.6 us
    ppermute x7, starting transfers between devices, from_behind(): return lax.ppermute(value, axis, pairs)  21.9 us
    pallas_call x1, Pallas kernels, body(): pl.pallas_call(hist_first, out_shape=[jax.ShapeDtypeStruct((bins_dev, 2 *...  6.55 us
  transfers between devices with their start and end apart: 14, of which 8 were waited for; matrix products, arithmetic and copies ran while one was open for 3% of the time, Pallas kernels for 6%

profile of v6, /device:TPU:6, one launch (start us, length us, event | category | flops | bytes accessed | tf_op | source)
XLA Modules:
  0.0 279.7 jit_solution(16410112688079942819)
XLA Ops:
  1.7 1.7 copy-done
  4.0 4.1 %pack_first.1 = bf16[64,152,128]{2,1,0:T(8,128)(2,1)} custom-call(s32[64]{0:T(128)S(1)} %convert_reduce_fusion.starts_ref, s32[24,128]{1,0:T(8,128)S(1)} %bitcast.21, f32[24,128]{1,0:T(8,128)S(1)} %bitcast_convert_fusion.nominal_ref, bf16[3072,384]{1,0:T(8,128)(2,1)S(1)} %copy-done), custom_call_target="tpu_custom_call" | custom-call | flops 226492416 | bytes 4980736 | tf_op jit(solution)/shard_map/pack_first/pallas_call | solution.py:209
  8.1 19.1 %all-to-all-start = ((bf16[64,152,128]{2,1,0:T(8,128)(2,1)}), bf16[64,152,128]{2,1,0:T(8,128)(2,1)}, u32[]{:S(2)}, u32[]{:S(2)}) async-start(bf16[64,152,128]{2,1,0:T(8,128)(2,1)} %pack_first.1), calls=%async_computation | async-start | bytes 4980736 | tf_op jit(solution)/shard_map/all_to_all | solution.py:195
  27.3 2.5 pack_rest.1
  29.8 3.4 %collective-permute-start = (bf16[16,72,128]{2,1,0:T(8,128)(2,1)S(1)}, bf16[16,72,128]{2,1,0:T(8,128)(2,1)S(1)}, u32[]{:S(2)}, u32[]{:S(2)}) collective-permute-start(bf16[16,72,128]{2,1,0:T(8,128)(2,1)S(1)} %get-tuple-element.18), channel_id=1, source_target_pairs={{0,8},{8,16},{16,24},{24,0},{1,9},{9,17},{17,25},{25,1},{2,10},{10... | collective-permute-start | bytes 884744 | tf_op jit(solution)/shard_map/ppermute | solution.py:178
  33.2 4.6 %collective-permute-start.1 = (bf16[16,72,128]{2,1,0:T(8,128)(2,1)S(1)}, bf16[16,72,128]{2,1,0:T(8,128)(2,1)S(1)}, u32[]{:S(2)}, u32[]{:S(2)}) collective-permute-start(bf16[16,72,128]{2,1,0:T(8,128)(2,1)S(1)} %get-tuple-element.19), channel_id=1, source_target_pairs={{0,16},{8,24},{16,0},{24,8},{1,17},{9,25},{17,1},{25,9},{2,18},{10... | collective-permute-start | bytes 884744 | tf_op jit(solution)/shard_map/ppermute | solution.py:178
  37.8 3.4 %collective-permute-start.2 = (bf16[16,72,128]{2,1,0:T(8,128)(2,1)S(1)}, bf16[16,72,128]{2,1,0:T(8,128)(2,1)S(1)}, u32[]{:S(2)}, u32[]{:S(2)}) collective-permute-start(bf16[16,72,128]{2,1,0:T(8,128)(2,1)S(1)} %get-tuple-element.20), channel_id=1, source_target_pairs={{0,24},{8,0},{16,8},{24,16},{1,25},{9,1},{17,9},{25,17},{2,26},{10... | collective-permute-start | bytes 884744 | tf_op jit(solution)/shard_map/ppermute | solution.py:178
  41.2 4.1 %collective-permute-done = bf16[16,72,128]{2,1,0:T(8,128)(2,1)S(1)} collective-permute-done((bf16[16,72,128]{2,1,0:T(8,128)(2,1)S(1)}, bf16[16,72,128]{2,1,0:T(8,128)(2,1)S(1)}, u32[]{:S(2)}, u32[]{:S(2)}) %collective-permute-start) | collective-permute-done | bytes 294944 | tf_op jit(solution)/shard_map/ppermute | solution.py:178
  45.3 9.3 %collective-permute-done.1 = bf16[16,72,128]{2,1,0:T(8,128)(2,1)S(1)} collective-permute-done((bf16[16,72,128]{2,1,0:T(8,128)(2,1)S(1)}, bf16[16,72,128]{2,1,0:T(8,128)(2,1)S(1)}, u32[]{:S(2)}, u32[]{:S(2)}) %collective-permute-start.1) | collective-permute-done | bytes 294944 | tf_op jit(solution)/shard_map/ppermute | solution.py:178
  54.8 89.4 %all-to-all-done = bf16[64,152,128]{2,1,0:T(8,128)(2,1)} async-done(((bf16[64,152,128]{2,1,0:T(8,128)(2,1)}), bf16[64,152,128]{2,1,0:T(8,128)(2,1)}, u32[]{:S(2)}, u32[]{:S(2)}) %all-to-all-start) | async-done | bytes 2490400 | tf_op jit(solution)/shard_map/all_to_all | solution.py:195
  145.3 3.8 %all-to-all-start.1 = ((bf16[16,4,72,128]{3,2,1,0:T(8,128)(2,1)}), bf16[16,4,72,128]{3,2,1,0:T(8,128)(2,1)S(1)}, u32[]{:S(2)}, u32[]{:S(2)}) async-start(bf16[16,4,72,128]{3,2,1,0:T(8,128)(2,1)} %copy.16), calls=%async_computation.1 | async-start | bytes 2359296 | tf_op jit(solution)/shard_map/all_to_all | solution.py:195
  153.7 1.8 fusion.4
  155.5 6.6 %hist_first.1 = (bf16[1024,256]{1,0:T(8,128)(2,1)S(1)}, f32[1024,1]{1,0:T(8,128)S(1)}) custom-call(s32[1,4608]{1,0:T(1,128)S(1)} %convert_element_type.35.bins_ref, bf16[8,4608]{1,0:T(8,128)(2,1)S(1)} %broadcast_in_dim.2.nominal_ref, f32[1024,1]{1,0:T(8,128)S(1)} %copy.14.background_ref, f32[1024,1]{1,0:T(8,128)S(1)} %copy.15.observed_ref, ...), custom_call_target="tpu_custom_call" | custom-call | flops 4831838208 | bytes 2359296 | tf_op jit(solution)/shard_map/hist_first/pallas_call | solution.py:241
  162.9 3.4 %collective-permute-start.4 = (bf16[1024,256]{1,0:T(8,128)(2,1)S(1)}, bf16[1024,256]{1,0:T(8,128)(2,1)S(1)}, u32[]{:S(2)}, u32[]{:S(2)}) collective-permute-start(bf16[1024,256]{1,0:T(8,128)(2,1)S(1)} %get-tuple-element.24.refs_0_), channel_id=1, source_target_pairs={{0,4},{1,5},{2,6},{3,7},{4,0},{5,1},{6,2},{7,3},{8,12},{9,13},{10,... | collective-permute-start | bytes 1572872 | tf_op jit(solution)/shard_map/ppermute | solution.py:178
  166.3 1.9 collective-permute-start.3
  168.2 13.1 %collective-permute-done.4.refs_2_ = bf16[1024,256]{1,0:T(8,128)(2,1)S(1)} collective-permute-done((bf16[1024,256]{1,0:T(8,128)(2,1)S(1)}, bf16[1024,256]{1,0:T(8,128)(2,1)S(1)}, u32[]{:S(2)}, u32[]{:S(2)}) %collective-permute-start.4) | collective-permute-done | bytes 524320 | tf_op jit(solution)/shard_map/ppermute | solution.py:178
  182.2 1.9 collective-permute-start.6
  184.1 5.3 %collective-permute-done.3.refs_1_ = bf16[1024,256]{1,0:T(8,128)(2,1)S(1)} collective-permute-done((bf16[1024,256]{1,0:T(8,128)(2,1)S(1)}, bf16[1024,256]{1,0:T(8,128)(2,1)S(1)}, u32[]{:S(2)}, u32[]{:S(2)}) %collective-permute-start.3) | collective-permute-done | bytes 524320 | tf_op jit(solution)/shard_map/ppermute | solution.py:178
  189.4 1.9 collective-permute-start.5
  191.6 10.4 %all-to-all-done.1 = bf16[16,4,72,128]{3,2,1,0:T(8,128)(2,1)S(1)} async-done(((bf16[16,4,72,128]{3,2,1,0:T(8,128)(2,1)}), bf16[16,4,72,128]{3,2,1,0:T(8,128)(2,1)S(1)}, u32[]{:S(2)}, u32[]{:S(2)}) %all-to-all-start.1) | async-done | bytes 1179680 | tf_op jit(solution)/shard_map/all_to_all | solution.py:195
  202.1 4.0 %hist_next.1.last_ref.refs_0_ = bf16[1024,128]{1,0:T(8,128)(2,1)S(1)} custom-call(s32[1,4608]{1,0:T(1,128)S(1)} %reshape.85.bins_ref, bf16[4608,128]{1,0:T(8,128)(2,1)S(1)} %bitcast.17), custom_call_target="tpu_custom_call" | custom-call | flops 2415919104 | bytes 1179648 | tf_op jit(solution)/shard_map/hist_next/pallas_call | solution.py:251
  206.1 3.3 %collective-permute-start.8 = (bf16[1024,128]{1,0:T(8,128)(2,1)S(1)}, bf16[1024,128]{1,0:T(8,128)(2,1)S(1)}, u32[]{:S(2)}, u32[]{:S(2)}) collective-permute-start(bf16[1024,128]{1,0:T(8,128)(2,1)S(1)} %hist_next.1.last_ref.refs_0_), channel_id=1, source_target_pairs={{0,4},{1,5},{2,6},{3,7},{4,0},{5,1},{6,2},{7,3},{8,12},{9,13},{10,... | collective-permute-start | bytes 786440 | tf_op jit(solution)/shard_map/ppermute | solution.py:178
  210.5 3.9 %gram_first.1 = (bf16[4,96,1280]{2,1,0:T(8,128)(2,1)}, bf16[384,1024]{1,0:T(8,128)(2,1)S(1)}) custom-call(s32[5]{0:T(128)S(1)} %stack.26.slots_ref, f32[1024,1]{1,0:T(8,128)S(1)} %copy-done.7, bf16[384,384]{1,0:T(8,128)(2,1)S(1)} %copy-done.5, bf16[1024,128]{1,0:T(8,128)(2,1)S(1)} %hist_next.1.last_ref.refs_0_, ...), custom_call_target="tpu_custom_call" | custom-call | flops 1207959552 | bytes 2621440 | tf_op jit(solution)/shard_map/gram_first/pallas_call | solution.py:272
  214.4 3.7 %all-to-all-start.2 = ((bf16[4,96,1280]{2,1,0:T(8,128)(2,1)}), bf16[4,96,1280]{2,1,0:T(8,128)(2,1)S(1)}, u32[]{:S(2)}, u32[]{:S(2)}) async-start(bf16[4,96,1280]{2,1,0:T(8,128)(2,1)} %get-tuple-element.25), calls=%async_computation.2 | async-start | bytes 1966080 | tf_op jit(solution)/shard_map/all_to_all | solution.py:195
  218.1 1.9 collective-permute-start.7
  220.0 1.9 collective-permute-start.10
  222.0 5.6 %collective-permute-done.7.refs_1_ = bf16[1024,128]{1,0:T(8,128)(2,1)S(1)} collective-permute-done((bf16[1024,128]{1,0:T(8,128)(2,1)S(1)}, bf16[1024,128]{1,0:T(8,128)(2,1)S(1)}, u32[]{:S(2)}, u32[]{:S(2)}) %collective-permute-start.7) | collective-permute-done | bytes 262176 | tf_op jit(solution)/shard_map/ppermute | solution.py:178
  227.5 1.9 collective-permute-start.9
  229.5 1.5 collective-permute-done.9.refs_3_
  231.0 1.7 gram_last.1
  232.7 14.0 %all_to_all.25.last_ref = bf16[4,96,640]{2,1,0:T(8,128)(2,1)S(1)} all-to-all(bf16[4,96,640]{2,1,0:T(8,128)(2,1)S(1)} %gram_last.1), channel_id=1, replica_groups=mesh['bins_0'=16,'bins_1'=4,'params'=8] {'bins_1'}, dimensions={0} | all-to-all | bytes 983040 | tf_op jit(solution)/shard_map/all_to_all | solution.py:195
  247.2 31.9 %all_to_all.26.got_ref = bf16[16,96,128]{2,1,0:T(8,128)(2,1)S(1)} all-to-all(bf16[16,96,128]{2,1,0:T(8,128)(2,1)S(1)} %add_across.1), channel_id=1, replica_groups=mesh['bins_0'=16,'bins_1'=4,'params'=8] {'bins_0'}, dimensions={0} | all-to-all | bytes 786432 | tf_op jit(solution)/shard_map/all_to_all | solution.py:195
  (49 shorter events, 12.3 us)
Async XLA Ops:
  1.7 1.7 copy-start
  3.3 0.7 copy-start.2
  8.1 19.1 %copy-start.1 = (bf16[3072,384]{1,0:T(8,128)(2,1)S(1)}, bf16[3072,384]{1,0:T(8,128)(2,1)}, u32[]{:S(2)}) copy-start(bf16[3072,384]{1,0:T(8,128)(2,1)} %w_ref.3) | copy-start | bytes 7077892
  8.1 136.1 %all-to-all-start = ((bf16[64,152,128]{2,1,0:T(8,128)(2,1)}), bf16[64,152,128]{2,1,0:T(8,128)(2,1)}, u32[]{:S(2)}, u32[]{:S(2)}) async-start(bf16[64,152,128]{2,1,0:T(8,128)(2,1)} %pack_first.1), calls=%async_computation | async-start | bytes 4980736 | tf_op jit(solution)/shard_map/all_to_all | solution.py:195
  29.8 15.5 %collective-permute-start = (bf16[16,72,128]{2,1,0:T(8,128)(2,1)S(1)}, bf16[16,72,128]{2,1,0:T(8,128)(2,1)S(1)}, u32[]{:S(2)}, u32[]{:S(2)}) collective-permute-start(bf16[16,72,128]{2,1,0:T(8,128)(2,1)S(1)} %get-tuple-element.18), channel_id=1, source_target_pairs={{0,8},{8,16},{16,24},{24,0},{1,9},{9,17},{17,25},{25,1},{2,10},{10... | collective-permute-start | bytes 884744 | tf_op jit(solution)/shard_map/ppermute | solution.py:178
  33.2 21.4 %collective-permute-start.1 = (bf16[16,72,128]{2,1,0:T(8,128)(2,1)S(1)}, bf16[16,72,128]{2,1,0:T(8,128)(2,1)S(1)}, u32[]{:S(2)}, u32[]{:S(2)}) collective-permute-start(bf16[16,72,128]{2,1,0:T(8,128)(2,1)S(1)} %get-tuple-element.19), channel_id=1, source_target_pairs={{0,16},{8,24},{16,0},{24,8},{1,17},{9,25},{17,1},{25,9},{2,18},{10... | collective-permute-start | bytes 884744 | tf_op jit(solution)/shard_map/ppermute | solution.py:178
  37.8 16.8 %collective-permute-start.2 = (bf16[16,72,128]{2,1,0:T(8,128)(2,1)S(1)}, bf16[16,72,128]{2,1,0:T(8,128)(2,1)S(1)}, u32[]{:S(2)}, u32[]{:S(2)}) collective-permute-start(bf16[16,72,128]{2,1,0:T(8,128)(2,1)S(1)} %get-tuple-element.20), channel_id=1, source_target_pairs={{0,24},{8,0},{16,8},{24,16},{1,25},{9,1},{17,9},{25,17},{2,26},{10... | collective-permute-start | bytes 884744 | tf_op jit(solution)/shard_map/ppermute | solution.py:178
  145.3 3.8 %copy-start.9 = (f32[1024]{0:T(1024)S(1)}, f32[1024]{0:T(1024)}, u32[]{:S(2)}) copy-start(f32[1024]{0:T(1024)} %param.9) | copy-start | bytes 12292
  145.3 4.1 %copy-start.10 = (f32[1024]{0:T(1024)S(1)}, f32[1024]{0:T(1024)}, u32[]{:S(2)}) copy-start(f32[1024]{0:T(1024)} %param.10) | copy-start | bytes 12292
  145.3 56.8 %all-to-all-start.1 = ((bf16[16,4,72,128]{3,2,1,0:T(8,128)(2,1)}), bf16[16,4,72,128]{3,2,1,0:T(8,128)(2,1)S(1)}, u32[]{:S(2)}, u32[]{:S(2)}) async-start(bf16[16,4,72,128]{3,2,1,0:T(8,128)(2,1)} %copy.16), calls=%async_computation.1 | async-start | bytes 2359296 | tf_op jit(solution)/shard_map/all_to_all | solution.py:195
  162.1 0.8 copy-start.6
  162.9 28.6 %copy-start.8 = (s32[64,1,72]{2,1,0:T(1,128)S(1)}, s32[64,1,72]{2,1,0:T(1,128)}, u32[]{:S(2)}) copy-start(s32[64,1,72]{2,1,0:T(1,128)} %get-tuple-element.30) | copy-start | bytes 55300
  162.9 18.4 %collective-permute-start.4 = (bf16[1024,256]{1,0:T(8,128)(2,1)S(1)}, bf16[1024,256]{1,0:T(8,128)(2,1)S(1)}, u32[]{:S(2)}, u32[]{:S(2)}) collective-permute-start(bf16[1024,256]{1,0:T(8,128)(2,1)S(1)} %get-tuple-element.24.refs_0_), channel_id=1, source_target_pairs={{0,4},{1,5},{2,6},{3,7},{4,0},{5,1},{6,2},{7,3},{8,12},{9,13},{10,... | collective-permute-start | bytes 1572872 | tf_op jit(solution)/shard_map/ppermute | solution.py:178
  166.3 23.1 %collective-permute-start.3 = (bf16[1024,256]{1,0:T(8,128)(2,1)S(1)}, bf16[1024,256]{1,0:T(8,128)(2,1)S(1)}, u32[]{:S(2)}, u32[]{:S(2)}) collective-permute-start(bf16[1024,256]{1,0:T(8,128)(2,1)S(1)} %get-tuple-element.24.refs_0_), channel_id=1, source_target_pairs={{0,6},{1,7},{2,0},{3,1},{4,2},{5,3},{6,4},{7,5},{8,14},{9,15},{10,... | collective-permute-start | bytes 1572872 | tf_op jit(solution)/shard_map/ppermute | solution.py:178
  182.2 27.3 %collective-permute-start.6 = (bf16[1024,256]{1,0:T(8,128)(2,1)}, bf16[1024,256]{1,0:T(8,128)(2,1)}, u32[]{:S(2)}, u32[]{:S(2)}) collective-permute-start(bf16[1024,256]{1,0:T(8,128)(2,1)} %broadcast_select_fusion), channel_id=1, source_target_pairs={{0,1},{1,0},{2,3},{3,2},{4,5},{5,4},{6,7},{7,6},{8,9},{9,8},{10,11... | collective-permute-start | bytes 1572872 | tf_op jit(solution)/shard_map/ppermute | solution.py:190
  189.4 16.7 %copy-start.3 = (bf16[1024,256]{1,0:T(8,128)(2,1)}, bf16[1024,256]{1,0:T(8,128)(2,1)S(1)}, u32[]{:S(2)}) copy-start(bf16[1024,256]{1,0:T(8,128)(2,1)S(1)} %collective-permute-done.3.refs_1_) | copy-start | bytes 1572868
  189.4 20.0 %collective-permute-start.5 = (bf16[1024,256]{1,0:T(8,128)(2,1)S(1)}, bf16[1024,256]{1,0:T(8,128)(2,1)}, u32[]{:S(2)}, u32[]{:S(2)}) collective-permute-start(bf16[1024,256]{1,0:T(8,128)(2,1)S(1)} %collective-permute-done.3.refs_1_), channel_id=1, source_target_pairs={{0,1},{1,0},{2,3},{3,2},{4,5},{5,4},{6,7},{7,6},{8,9},{9,8},{10,11... | collective-permute-start | bytes 1572872 | tf_op jit(solution)/shard_map/ppermute | solution.py:189
  202.1 7.3 %copy-start.5 = (bf16[384,384]{1,0:T(8,128)(2,1)S(1)}, bf16[384,384]{1,0:T(8,128)(2,1)}, u32[]{:S(2)}) copy-start(bf16[384,384]{1,0:T(8,128)(2,1)} %constant.33.clone.order_ref) | copy-start | bytes 884740
  202.1 7.4 %copy-start.7 = (f32[1024,1]{1,0:T(8,128)S(1)}, f32[1024,1]{1,0:T(8,128)}, u32[]{:S(2)}) copy-start(f32[1024,1]{1,0:T(8,128)} %copy-done.6) | copy-start | bytes 12292
  206.1 13.9 %collective-permute-start.8 = (bf16[1024,128]{1,0:T(8,128)(2,1)S(1)}, bf16[1024,128]{1,0:T(8,128)(2,1)S(1)}, u32[]{:S(2)}, u32[]{:S(2)}) collective-permute-start(bf16[1024,128]{1,0:T(8,128)(2,1)S(1)} %hist_next.1.last_ref.refs_0_), channel_id=1, source_target_pairs={{0,4},{1,5},{2,6},{3,7},{4,0},{5,1},{6,2},{7,3},{8,12},{9,13},{10,... | collective-permute-start | bytes 786440 | tf_op jit(solution)/shard_map/ppermute | solution.py:178
  209.4 1.0 copy-start.4
  214.4 15.1 %all-to-all-start.2 = ((bf16[4,96,1280]{2,1,0:T(8,128)(2,1)}), bf16[4,96,1280]{2,1,0:T(8,128)(2,1)S(1)}, u32[]{:S(2)}, u32[]{:S(2)}) async-start(bf16[4,96,1280]{2,1,0:T(8,128)(2,1)} %get-tuple-element.25), calls=%async_computation.2 | async-start | bytes 1966080 | tf_op jit(solution)/shard_map/all_to_all | solution.py:195
  218.1 9.5 %collective-permute-start.7 = (bf16[1024,128]{1,0:T(8,128)(2,1)S(1)}, bf16[1024,128]{1,0:T(8,128)(2,1)S(1)}, u32[]{:S(2)}, u32[]{:S(2)}) collective-permute-start(bf16[1024,128]{1,0:T(8,128)(2,1)S(1)} %hist_next.1.last_ref.refs_0_), channel_id=1, source_target_pairs={{0,6},{1,7},{2,0},{3,1},{4,2},{5,3},{6,4},{7,5},{8,14},{9,15},{10,... | collective-permute-start | bytes 786440 | tf_op jit(solution)/shard_map/ppermute | solution.py:178
  220.0 9.4 %collective-permute-start.10 = (bf16[1024,128]{1,0:T(8,128)(2,1)S(1)}, bf16[1024,128]{1,0:T(8,128)(2,1)S(1)}, u32[]{:S(2)}, u32[]{:S(2)}) collective-permute-start(bf16[1024,128]{1,0:T(8,128)(2,1)S(1)} %broadcast_select_fusion.1), channel_id=1, source_target_pairs={{0,1},{1,0},{2,3},{3,2},{4,5},{5,4},{6,7},{7,6},{8,9},{9,8},{10,11... | collective-permute-start | bytes 786440 | tf_op jit(solution)/shard_map/ppermute | solution.py:190
  227.5 3.4 %collective-permute-start.9 = (bf16[1024,128]{1,0:T(8,128)(2,1)S(1)}, bf16[1024,128]{1,0:T(8,128)(2,1)S(1)}, u32[]{:S(2)}, u32[]{:S(2)}) collective-permute-start(bf16[1024,128]{1,0:T(8,128)(2,1)S(1)} %collective-permute-done.7.refs_1_), channel_id=1, source_target_pairs={{0,1},{1,0},{2,3},{3,2},{4,5},{5,4},{6,7},{7,6},{8,9},{9,8},{10,11... | collective-permute-start | bytes 786440 | tf_op jit(solution)/shard_map/ppermute | solution.py:189

commit v7 on v6

--- a/solution.py
+++ b/solution.py
@@ -138,38 +138,48 @@
             out_ref[y, :, pl.ds(at, wide)] = full[y * step : (y + 1) * step]
 
 
-def gram_last(slots_ref, lhs_ref, *refs):
-    lasts, out_ref = refs[:-1], refs[-1]
-    lhs = lhs_ref[...]
-    wide, step = lasts[0].shape[1], out_ref.shape[1]
-    for k, part in enumerate(lasts):
-        full = jnp.dot(lhs, part[...], preferred_element_type=jnp.float32).astype(jnp.bfloat16)
-        at = pl.multiple_of(slots_ref[k] * wide, wide)
-        for y in range(out_ref.shape[0]):
-            out_ref[y, :, pl.ds(at, wide)] = full[y * step : (y + 1) * step]
-
-
-def add_across(turns, first_ref, last_ref, out_ref, wide):
+def gram_last(n1, slots_ref, place_ref, lhs_ref, *refs):
+    lasts, out_refs = refs[:-n1], refs[-n1:]
+    step = out_refs[0].shape[0]
+    wide = lasts[0].shape[1]
+    for turn, out_ref in enumerate(out_refs):
+        at = pl.multiple_of(lax.rem(place_ref[0] + turn, n1) * step, step)
+        lhs = lhs_ref[pl.ds(at, step), :]
+        for k, part in enumerate(lasts):
+            full = jnp.dot(lhs, part[...], preferred_element_type=jnp.float32).astype(jnp.bfloat16)
+            out_ref[:, pl.ds(pl.multiple_of(slots_ref[k] * wide, wide), wide)] = full
+
+
+def rows_by_z(total, out_ref, wide):
     n0 = out_ref.shape[0]
-    lines = first_ref.shape[1] // n0
-    first = jnp.sum(first_ref[...].astype(jnp.float32), axis=0)
-    last = jnp.sum(last_ref[...].astype(jnp.float32), axis=0)
+    lines = total.shape[0] // n0
     wide[...] = jnp.zeros_like(wide)
+    for j in range(total.shape[1] // COLS):
+        for z in range(n0):
+            wide[z, j * lines : (j + 1) * lines] = total[z * lines : (z + 1) * lines, j * COLS : (j + 1) * COLS]
+    out_ref[...] = wide[...].astype(jnp.bfloat16)
+
+
+def add_first(got_ref, out_ref, wide):
+    rows_by_z(jnp.sum(got_ref[...].astype(jnp.float32), axis=0), out_ref, wide)
+
+
+def add_last(*refs):
+    total = refs[0][...].astype(jnp.float32)
+    for ref in refs[1:-2]:
+        total += ref[...].astype(jnp.float32)
+    rows_by_z(total, *refs[-2:])
+
+
+def add_along(scale, turns, first_ref, last_ref, out_ref):
+    lines = out_ref.shape[0]
+    first = jnp.sum(first_ref[...].astype(jnp.float32), axis=0) * scale
+    last = jnp.sum(last_ref[...].astype(jnp.float32), axis=0) * scale
     for k in range(turns):
         for t in range(3):
-            tile, at = (last, k * COLS) if t == 2 else (first, (2 * k + t) * COLS)
-            tile = tile[:, at : at + COLS]
-            at = (3 * k + t) * lines
-            for z in range(n0):
-                wide[z, at : at + lines] = tile[z * lines : (z + 1) * lines]
-    out_ref[...] = wide[...].astype(jnp.bfloat16)
-
-
-def add_along(scale, got_ref, out_ref):
-    lines = out_ref.shape[0]
-    total = jnp.sum(got_ref[...].astype(jnp.float32), axis=0) * scale
-    for j in range(out_ref.shape[1] // 128):
-        out_ref[:, j * 128 : (j + 1) * 128] = total[j * lines : (j + 1) * lines]
+            tile, j = (last, k) if t == 2 else (first, 2 * k + t)
+            at = (3 * k + t) * COLS
+            out_ref[:, at : at + COLS] = tile[j * lines : (j + 1) * lines]
 
 
 def from_behind(value, axis, steps):
@@ -226,7 +236,6 @@
         name="pack_rest",
     )(place.reshape(1).astype(jnp.int32), starts, event_weights)
     mid = jnp.stack([from_behind(x, BINS[1], t) if t else x for t, x in enumerate(sends)], axis=1)
-    mid, got_a = lax.optimization_barrier((mid, got_a))
     got_b = exchange(mid, BINS[0])
 
     total = owners * CAP
@@ -281,35 +290,43 @@
         cost_estimate=cost(2 * bins_dev * width * 2 * COLS * (turns + 1), 2 * turns * COLS * bins_dev * 2),
         name="gram_first",
     )(slots, curve, jnp.asarray(order, bf16), last, *firsts)
-    part_a, lhs = lax.optimization_barrier((exchange(part_a, BINS[1]), lhs))
-    part_b = pl.pallas_call(
-        gram_last,
-        out_shape=jax.ShapeDtypeStruct((n1, width // n1, turns * COLS), bf16),
-        in_specs=[SMEM] + [VMEM] * (1 + turns),
-        out_specs=VMEM,
+    part_a = lax.optimization_barrier((exchange(part_a, BINS[1]), *lasts[1:]))[0]
+    parts_b = pl.pallas_call(
+        functools.partial(gram_last, n1),
+        out_shape=[jax.ShapeDtypeStruct((width // n1, turns * COLS), bf16)] * n1,
+        in_specs=[SMEM, SMEM] + [VMEM] * (1 + turns),
+        out_specs=[VMEM] * n1,
         compiler_params=PARAMS,
         cost_estimate=cost(2 * bins_dev * width * COLS * turns, turns * COLS * bins_dev * 2),
         name="gram_last",
-    )(slots, lhs, *lasts)
-    part_b = exchange(part_b, BINS[1])
-    packed = -(-lines * turns * width // 128 // 16) * 16
-    across = pl.pallas_call(
-        functools.partial(add_across, turns),
-        out_shape=jax.ShapeDtypeStruct((n0, packed, 128), bf16),
+    )(slots, place.reshape(1).astype(jnp.int32), lhs, *lasts)
+    parts_b = [from_behind(x, BINS[1], t) if t else x for t, x in enumerate(parts_b)]
+
+    def by_z(kernel, tiles, *args):
+        packed = -(-lines * tiles // 16) * 16
+        return pl.pallas_call(
+            kernel,
+            out_shape=jax.ShapeDtypeStruct((n0, packed, COLS), bf16),
+            in_specs=[VMEM] * len(args),
+            out_specs=VMEM,
+            scratch_shapes=[pltpu.VMEM((n0, packed, COLS), f32)],
+            compiler_params=PARAMS,
+            cost_estimate=cost(0, 8 * n0 * packed * COLS),
+            name=kernel.__name__,
+        )(*args)
+
+    sum_a = exchange(by_z(add_first, 2 * turns, part_a), BINS[0])
+    sum_b = by_z(add_last, turns, *parts_b)
+    sum_b, sum_a = lax.optimization_barrier((sum_b, sum_a))
+    sum_b = exchange(sum_b, BINS[0])
+    return pl.pallas_call(
+        functools.partial(add_along, 1.0 / (bins_dev * owners), turns),
+        out_shape=jax.ShapeDtypeStruct((lines, turns * width), f32),
         in_specs=[VMEM] * 2,
         out_specs=VMEM,
-        scratch_shapes=[pltpu.VMEM((n0, packed, 128), f32)],
-        compiler_params=PARAMS,
-        name="add_across",
-    )(part_a, part_b)
-    return pl.pallas_call(
-        functools.partial(add_along, 1.0 / (bins_dev * owners)),
-        out_shape=jax.ShapeDtypeStruct((lines, turns * width), f32),
-        in_specs=[VMEM],
-        out_specs=VMEM,
         compiler_params=PARAMS,
         name="add_along",
-    )(exchange(across, BINS[0]))
+    )(sum_a, sum_b)
 
 
 def solution(mesh):

time: 281 us -> 285 us (1.014)
  blocking collectives: 45.9 us -> 23.4 us
  starting transfers between devices: 56.2 us -> 77.8 us
  waiting for transfers between devices: 139 us -> 143 us
    all_to_all x2 -> x1, blocking collectives: 45.9 us -> 23.4 us  [exchange(): return lax.all_to_all(value, axis, split_axis=0, concat_axis=0, tiled=True)]
    ppermute x7 -> x10, starting transfers between devices: 21.9 us -> 33.4 us  [from_behind(): return lax.ppermute(value, axis, pairs)]
    all_to_all x3 -> x4, starting transfers between devices: 26.6 us -> 36.7 us  [exchange(): return lax.all_to_all(value, axis, split_axis=0, concat_axis=0, tiled=True)]
    ppermute x7 -> x10, waiting for transfers between devices: 37.4 us -> 40.8 us  [from_behind(): return lax.ppermute(value, axis, pairs)]
    all_to_all x3 -> x4, waiting for transfers between devices: 99.9 us -> 100 us  [exchange(): return lax.all_to_all(value, axis, split_axis=0, concat_axis=0, tiled=True)]
  transfers between devices with their start and end apart: 14 -> 18, of which waited for: 8 -> 11; matrix products, arithmetic and copies ran while one was open for 3% -> 3% of each run, Pallas kernels for 6% -> 7%
where the time goes in v7:
time: 285 us; the launch traced here: 284 us
  waiting for transfers between devices  143 us (50%)
  starting transfers between devices  77.8 us (27%)
  Pallas kernels  24.6 us (9%)
  blocking collectives  23.4 us (8%)
  local copies, waits for them, and re-layouts  9.67 us (3%)
  other arithmetic  4.96 us (2%)
    all_to_all x4, waiting for transfers between devices, exchange(): return lax.all_to_all(value, axis, split_axis=0, concat_axis=0, tiled=True)  100 us
    ppermute x10, waiting for transfers between devices, from_behind(): return lax.ppermute(value, axis, pairs)  40.8 us
    all_to_all x4, starting transfers between devices, exchange(): return lax.all_to_all(value, axis, split_axis=0, concat_axis=0, tiled=True)  36.7 us
    ppermute x10, starting transfers between devices, from_behind(): return lax.ppermute(value, axis, pairs)  33.4 us
    all_to_all x1, blocking collectives, exchange(): return lax.all_to_all(value, axis, split_axis=0, concat_axis=0, tiled=True)  23.4 us
    pallas_call x1, Pallas kernels, body(): pl.pallas_call(hist_first, out_shape=[jax.ShapeDtypeStruct((bins_dev, 2 *...  6.55 us
  transfers between devices with their start and end apart: 18, of which 11 were waited for; matrix products, arithmetic and copies ran while one was open for 3% of the time, Pallas kernels for 7%

profile of v7, /device:TPU:6, one launch (start us, length us, event | category | flops | bytes accessed | tf_op | source)
XLA Modules:
  0.0 283.5 jit_solution(9612901848176475649)
XLA Ops:
  4.0 4.1 %pack_first.1 = bf16[64,152,128]{2,1,0:T(8,128)(2,1)} custom-call(s32[64]{0:T(128)S(1)} %convert_reduce_fusion.starts_ref, s32[24,128]{1,0:T(8,128)S(1)} %bitcast.21, f32[24,128]{1,0:T(8,128)S(1)} %bitcast_convert_fusion.nominal_ref, bf16[3072,384]{1,0:T(8,128)(2,1)S(1)} %copy-done), custom_call_target="tpu_custom_call" | custom-call | flops 226492416 | bytes 4980736 | tf_op jit(solution)/shard_map/pack_first/pallas_call | solution.py:219
  8.2 19.1 %all-to-all-start = ((bf16[64,152,128]{2,1,0:T(8,128)(2,1)}), bf16[64,152,128]{2,1,0:T(8,128)(2,1)}, u32[]{:S(2)}, u32[]{:S(2)}) async-start(bf16[64,152,128]{2,1,0:T(8,128)(2,1)} %pack_first.1), calls=%async_computation | async-start | bytes 4980736 | tf_op jit(solution)/shard_map/all_to_all | solution.py:205
  27.3 2.5 pack_rest.1
  29.8 3.4 %collective-permute-start = (bf16[16,72,128]{2,1,0:T(8,128)(2,1)S(1)}, bf16[16,72,128]{2,1,0:T(8,128)(2,1)S(1)}, u32[]{:S(2)}, u32[]{:S(2)}) collective-permute-start(bf16[16,72,128]{2,1,0:T(8,128)(2,1)S(1)} %get-tuple-element.22), channel_id=1, source_target_pairs={{0,8},{8,16},{16,24},{24,0},{1,9},{9,17},{17,25},{25,1},{2,10},{10... | collective-permute-start | bytes 884744 | tf_op jit(solution)/shard_map/ppermute | solution.py:188
  33.2 4.6 %collective-permute-start.1 = (bf16[16,72,128]{2,1,0:T(8,128)(2,1)S(1)}, bf16[16,72,128]{2,1,0:T(8,128)(2,1)S(1)}, u32[]{:S(2)}, u32[]{:S(2)}) collective-permute-start(bf16[16,72,128]{2,1,0:T(8,128)(2,1)S(1)} %get-tuple-element.23), channel_id=1, source_target_pairs={{0,16},{8,24},{16,0},{24,8},{1,17},{9,25},{17,1},{25,9},{2,18},{10... | collective-permute-start | bytes 884744 | tf_op jit(solution)/shard_map/ppermute | solution.py:188
  37.8 3.4 %collective-permute-start.2 = (bf16[16,72,128]{2,1,0:T(8,128)(2,1)S(1)}, bf16[16,72,128]{2,1,0:T(8,128)(2,1)S(1)}, u32[]{:S(2)}, u32[]{:S(2)}) collective-permute-start(bf16[16,72,128]{2,1,0:T(8,128)(2,1)S(1)} %get-tuple-element.24), channel_id=1, source_target_pairs={{0,24},{8,0},{16,8},{24,16},{1,25},{9,1},{17,9},{25,17},{2,26},{10... | collective-permute-start | bytes 884744 | tf_op jit(solution)/shard_map/ppermute | solution.py:188
  41.2 4.1 %collective-permute-done = bf16[16,72,128]{2,1,0:T(8,128)(2,1)S(1)} collective-permute-done((bf16[16,72,128]{2,1,0:T(8,128)(2,1)S(1)}, bf16[16,72,128]{2,1,0:T(8,128)(2,1)S(1)}, u32[]{:S(2)}, u32[]{:S(2)}) %collective-permute-start) | collective-permute-done | bytes 294944 | tf_op jit(solution)/shard_map/ppermute | solution.py:188
  45.3 9.4 %collective-permute-done.1 = bf16[16,72,128]{2,1,0:T(8,128)(2,1)S(1)} collective-permute-done((bf16[16,72,128]{2,1,0:T(8,128)(2,1)S(1)}, bf16[16,72,128]{2,1,0:T(8,128)(2,1)S(1)}, u32[]{:S(2)}, u32[]{:S(2)}) %collective-permute-start.1) | collective-permute-done | bytes 294944 | tf_op jit(solution)/shard_map/ppermute | solution.py:188
  56.0 88.2 %all-to-all-done = bf16[64,152,128]{2,1,0:T(8,128)(2,1)} async-done(((bf16[64,152,128]{2,1,0:T(8,128)(2,1)}), bf16[64,152,128]{2,1,0:T(8,128)(2,1)}, u32[]{:S(2)}, u32[]{:S(2)}) %all-to-all-start) | async-done | bytes 2490400 | tf_op jit(solution)/shard_map/all_to_all | solution.py:205
  144.2 3.7 %all-to-all-start.1 = ((bf16[16,4,72,128]{3,2,1,0:T(8,128)(2,1)}), bf16[16,4,72,128]{3,2,1,0:T(8,128)(2,1)S(1)}, u32[]{:S(2)}, u32[]{:S(2)}) async-start(bf16[16,4,72,128]{3,2,1,0:T(8,128)(2,1)} %copy.16), calls=%async_computation.1 | async-start | bytes 2359296 | tf_op jit(solution)/shard_map/all_to_all | solution.py:205
  154.2 6.5 %hist_first.1 = (bf16[1024,256]{1,0:T(8,128)(2,1)S(1)}, f32[1024,1]{1,0:T(8,128)S(1)}) custom-call(s32[1,4608]{1,0:T(1,128)S(1)} %convert_element_type.35.bins_ref, bf16[8,4608]{1,0:T(8,128)(2,1)S(1)} %broadcast_in_dim.2.nominal_ref, f32[1024,1]{1,0:T(8,128)S(1)} %copy.14.background_ref, f32[1024,1]{1,0:T(8,128)S(1)} %copy.15.observed_ref, ...), custom_call_target="tpu_custom_call" | custom-call | flops 4831838208 | bytes 2359296 | tf_op jit(solution)/shard_map/hist_first/pallas_call | solution.py:250
  161.6 3.4 %collective-permute-start.4 = (bf16[1024,256]{1,0:T(8,128)(2,1)S(1)}, bf16[1024,256]{1,0:T(8,128)(2,1)S(1)}, u32[]{:S(2)}, u32[]{:S(2)}) collective-permute-start(bf16[1024,256]{1,0:T(8,128)(2,1)S(1)} %get-tuple-element.25.refs_0_), channel_id=1, source_target_pairs={{0,4},{1,5},{2,6},{3,7},{4,0},{5,1},{6,2},{7,3},{8,12},{9,13},{10,... | collective-permute-start | bytes 1572872 | tf_op jit(solution)/shard_map/ppermute | solution.py:188
  165.1 1.9 collective-permute-start.3
  167.0 13.0 %collective-permute-done.4.refs_2_ = bf16[1024,256]{1,0:T(8,128)(2,1)S(1)} collective-permute-done((bf16[1024,256]{1,0:T(8,128)(2,1)S(1)}, bf16[1024,256]{1,0:T(8,128)(2,1)S(1)}, u32[]{:S(2)}, u32[]{:S(2)}) %collective-permute-start.4) | collective-permute-done | bytes 524320 | tf_op jit(solution)/shard_map/ppermute | solution.py:188
  180.9 1.9 collective-permute-start.6
  182.8 5.3 %collective-permute-done.3.refs_1_ = bf16[1024,256]{1,0:T(8,128)(2,1)S(1)} collective-permute-done((bf16[1024,256]{1,0:T(8,128)(2,1)S(1)}, bf16[1024,256]{1,0:T(8,128)(2,1)S(1)}, u32[]{:S(2)}, u32[]{:S(2)}) %collective-permute-start.3) | collective-permute-done | bytes 524320 | tf_op jit(solution)/shard_map/ppermute | solution.py:188
  188.2 1.9 collective-permute-start.5
  190.4 10.5 %all-to-all-done.1 = bf16[16,4,72,128]{3,2,1,0:T(8,128)(2,1)S(1)} async-done(((bf16[16,4,72,128]{3,2,1,0:T(8,128)(2,1)}), bf16[16,4,72,128]{3,2,1,0:T(8,128)(2,1)S(1)}, u32[]{:S(2)}, u32[]{:S(2)}) %all-to-all-start.1) | async-done | bytes 1179680 | tf_op jit(solution)/shard_map/all_to_all | solution.py:205
  200.9 4.0 %hist_next.1.last_ref.refs_0_ = bf16[1024,128]{1,0:T(8,128)(2,1)S(1)} custom-call(s32[1,4608]{1,0:T(1,128)S(1)} %reshape.86.bins_ref, bf16[4608,128]{1,0:T(8,128)(2,1)S(1)} %bitcast.17), custom_call_target="tpu_custom_call" | custom-call | flops 2415919104 | bytes 1179648 | tf_op jit(solution)/shard_map/hist_next/pallas_call | solution.py:260
  204.9 3.3 %collective-permute-start.8 = (bf16[1024,128]{1,0:T(8,128)(2,1)S(1)}, bf16[1024,128]{1,0:T(8,128)(2,1)S(1)}, u32[]{:S(2)}, u32[]{:S(2)}) collective-permute-start(bf16[1024,128]{1,0:T(8,128)(2,1)S(1)} %hist_next.1.last_ref.refs_0_), channel_id=1, source_target_pairs={{0,4},{1,5},{2,6},{3,7},{4,0},{5,1},{6,2},{7,3},{8,12},{9,13},{10,... | collective-permute-start | bytes 786440 | tf_op jit(solution)/shard_map/ppermute | solution.py:188
  209.3 3.9 %gram_first.1 = (bf16[4,96,1280]{2,1,0:T(8,128)(2,1)}, bf16[384,1024]{1,0:T(8,128)(2,1)S(1)}) custom-call(s32[5]{0:T(128)S(1)} %stack.26.slots_ref, f32[1024,1]{1,0:T(8,128)S(1)} %copy-done.7, bf16[384,384]{1,0:T(8,128)(2,1)S(1)} %copy-done.5, bf16[1024,128]{1,0:T(8,128)(2,1)S(1)} %hist_next.1.last_ref.refs_0_, ...), custom_call_target="tpu_custom_call" | custom-call | flops 1207959552 | bytes 2621440 | tf_op jit(solution)/shard_map/gram_first/pallas_call | solution.py:281
  213.1 3.7 %all-to-all-start.2 = ((bf16[4,96,1280]{2,1,0:T(8,128)(2,1)}), bf16[4,96,1280]{2,1,0:T(8,128)(2,1)S(1)}, u32[]{:S(2)}, u32[]{:S(2)}) async-start(bf16[4,96,1280]{2,1,0:T(8,128)(2,1)} %get-tuple-element.31), calls=%async_computation.2 | async-start | bytes 1966080 | tf_op jit(solution)/shard_map/all_to_all | solution.py:205
  216.9 1.9 collective-permute-start.7
  218.8 1.9 collective-permute-start.10
  220.7 5.6 %collective-permute-done.7.refs_1_ = bf16[1024,128]{1,0:T(8,128)(2,1)S(1)} collective-permute-done((bf16[1024,128]{1,0:T(8,128)(2,1)S(1)}, bf16[1024,128]{1,0:T(8,128)(2,1)S(1)}, u32[]{:S(2)}, u32[]{:S(2)}) %collective-permute-start.7) | collective-permute-done | bytes 262176 | tf_op jit(solution)/shard_map/ppermute | solution.py:188
  226.3 1.9 collective-permute-start.9
  230.8 10.2 %all-to-all-start.3 = ((bf16[16,64,128]{2,1,0:T(8,128)(2,1)}), bf16[16,64,128]{2,1,0:T(8,128)(2,1)S(1)}, u32[]{:S(2)}, u32[]{:S(2)}) async-start(bf16[16,64,128]{2,1,0:T(8,128)(2,1)} %add_first.1), calls=%async_computation.3 | async-start | bytes 524288 | tf_op jit(solution)/shard_map/all_to_all | solution.py:205
  242.7 3.5 %collective-permute-start.11 = (bf16[96,640]{1,0:T(8,128)(2,1)S(1)}, bf16[96,640]{1,0:T(8,128)(2,1)S(1)}, u32[]{:S(2)}, u32[]{:S(2)}) collective-permute-start(bf16[96,640]{1,0:T(8,128)(2,1)S(1)} %get-tuple-element.28), channel_id=1, source_target_pairs={{0,8},{8,16},{16,24},{24,0},{1,9},{9,17},{17,25},{25,1},{2,10},{10... | collective-permute-start | bytes 368648 | tf_op jit(solution)/shard_map/ppermute | solution.py:188
  246.3 4.6 %collective-permute-start.12 = (bf16[96,640]{1,0:T(8,128)(2,1)S(1)}, bf16[96,640]{1,0:T(8,128)(2,1)S(1)}, u32[]{:S(2)}, u32[]{:S(2)}) collective-permute-start(bf16[96,640]{1,0:T(8,128)(2,1)S(1)} %get-tuple-element.29), channel_id=1, source_target_pairs={{0,16},{8,24},{16,0},{24,8},{1,17},{9,25},{17,1},{25,9},{2,18},{10... | collective-permute-start | bytes 368648 | tf_op jit(solution)/shard_map/ppermute | solution.py:188
  250.9 3.4 %collective-permute-start.13 = (bf16[96,640]{1,0:T(8,128)(2,1)S(1)}, bf16[96,640]{1,0:T(8,128)(2,1)S(1)}, u32[]{:S(2)}, u32[]{:S(2)}) collective-permute-start(bf16[96,640]{1,0:T(8,128)(2,1)S(1)} %get-tuple-element.30), channel_id=1, source_target_pairs={{0,24},{8,0},{16,8},{24,16},{1,25},{9,1},{17,9},{25,17},{2,26},{10... | collective-permute-start | bytes 368648 | tf_op jit(solution)/shard_map/ppermute | solution.py:188
  254.6 3.0 %collective-permute-done.13.refs_3_ = bf16[96,640]{1,0:T(8,128)(2,1)S(1)} collective-permute-done((bf16[96,640]{1,0:T(8,128)(2,1)S(1)}, bf16[96,640]{1,0:T(8,128)(2,1)S(1)}, u32[]{:S(2)}, u32[]{:S(2)}) %collective-permute-start.13) | collective-permute-done | bytes 122912 | tf_op jit(solution)/shard_map/ppermute | solution.py:188
  259.4 23.4 %all_to_all.25.last_ref = bf16[16,32,128]{2,1,0:T(8,128)(2,1)S(1)} all-to-all(bf16[16,32,128]{2,1,0:T(8,128)(2,1)S(1)} %add_last.1), channel_id=1, replica_groups=mesh['bins_0'=16,'bins_1'=4,'params'=8] {'bins_0'}, dimensions={0} | all-to-all | bytes 262144 | tf_op jit(solution)/shard_map/all_to_all | solution.py:205
  (57 shorter events, 21.7 us)
Async XLA Ops:
  1.7 1.7 copy-start
  3.3 0.7 copy-start.2
  8.2 19.1 %copy-start.1 = (bf16[3072,384]{1,0:T(8,128)(2,1)S(1)}, bf16[3072,384]{1,0:T(8,128)(2,1)}, u32[]{:S(2)}) copy-start(bf16[3072,384]{1,0:T(8,128)(2,1)} %w_ref.3) | copy-start | bytes 7077892
  8.2 136.1 %all-to-all-start = ((bf16[64,152,128]{2,1,0:T(8,128)(2,1)}), bf16[64,152,128]{2,1,0:T(8,128)(2,1)}, u32[]{:S(2)}, u32[]{:S(2)}) async-start(bf16[64,152,128]{2,1,0:T(8,128)(2,1)} %pack_first.1), calls=%async_computation | async-start | bytes 4980736 | tf_op jit(solution)/shard_map/all_to_all | solution.py:205
  29.8 15.5 %collective-permute-start = (bf16[16,72,128]{2,1,0:T(8,128)(2,1)S(1)}, bf16[16,72,128]{2,1,0:T(8,128)(2,1)S(1)}, u32[]{:S(2)}, u32[]{:S(2)}) collective-permute-start(bf16[16,72,128]{2,1,0:T(8,128)(2,1)S(1)} %get-tuple-element.22), channel_id=1, source_target_pairs={{0,8},{8,16},{16,24},{24,0},{1,9},{9,17},{17,25},{25,1},{2,10},{10... | collective-permute-start | bytes 884744 | tf_op jit(solution)/shard_map/ppermute | solution.py:188
  33.2 21.4 %collective-permute-start.1 = (bf16[16,72,128]{2,1,0:T(8,128)(2,1)S(1)}, bf16[16,72,128]{2,1,0:T(8,128)(2,1)S(1)}, u32[]{:S(2)}, u32[]{:S(2)}) collective-permute-start(bf16[16,72,128]{2,1,0:T(8,128)(2,1)S(1)} %get-tuple-element.23), channel_id=1, source_target_pairs={{0,16},{8,24},{16,0},{24,8},{1,17},{9,25},{17,1},{25,9},{2,18},{10... | collective-permute-start | bytes 884744 | tf_op jit(solution)/shard_map/ppermute | solution.py:188
  37.8 16.9 %collective-permute-start.2 = (bf16[16,72,128]{2,1,0:T(8,128)(2,1)S(1)}, bf16[16,72,128]{2,1,0:T(8,128)(2,1)S(1)}, u32[]{:S(2)}, u32[]{:S(2)}) collective-permute-start(bf16[16,72,128]{2,1,0:T(8,128)(2,1)S(1)} %get-tuple-element.24), channel_id=1, source_target_pairs={{0,24},{8,0},{16,8},{24,16},{1,25},{9,1},{17,9},{25,17},{2,26},{10... | collective-permute-start | bytes 884744 | tf_op jit(solution)/shard_map/ppermute | solution.py:188
  56.0 92.0 %copy-start.9 = (f32[1024]{0:T(1024)S(1)}, f32[1024]{0:T(1024)}, u32[]{:S(2)}) copy-start(f32[1024]{0:T(1024)} %param.9) | copy-start | bytes 12292
  56.0 92.2 %copy-start.10 = (f32[1024]{0:T(1024)S(1)}, f32[1024]{0:T(1024)}, u32[]{:S(2)}) copy-start(f32[1024]{0:T(1024)} %param.10) | copy-start | bytes 12292
  144.2 56.6 %all-to-all-start.1 = ((bf16[16,4,72,128]{3,2,1,0:T(8,128)(2,1)}), bf16[16,4,72,128]{3,2,1,0:T(8,128)(2,1)S(1)}, u32[]{:S(2)}, u32[]{:S(2)}) async-start(bf16[16,4,72,128]{3,2,1,0:T(8,128)(2,1)} %copy.16), calls=%async_computation.1 | async-start | bytes 2359296 | tf_op jit(solution)/shard_map/all_to_all | solution.py:205
  160.8 0.8 copy-start.6
  161.6 28.6 %copy-start.8 = (s32[64,1,72]{2,1,0:T(1,128)S(1)}, s32[64,1,72]{2,1,0:T(1,128)}, u32[]{:S(2)}) copy-start(s32[64,1,72]{2,1,0:T(1,128)} %get-tuple-element.36) | copy-start | bytes 55300
  161.6 18.4 %collective-permute-start.4 = (bf16[1024,256]{1,0:T(8,128)(2,1)S(1)}, bf16[1024,256]{1,0:T(8,128)(2,1)S(1)}, u32[]{:S(2)}, u32[]{:S(2)}) collective-permute-start(bf16[1024,256]{1,0:T(8,128)(2,1)S(1)} %get-tuple-element.25.refs_0_), channel_id=1, source_target_pairs={{0,4},{1,5},{2,6},{3,7},{4,0},{5,1},{6,2},{7,3},{8,12},{9,13},{10,... | collective-permute-start | bytes 1572872 | tf_op jit(solution)/shard_map/ppermute | solution.py:188
  165.1 23.1 %collective-permute-start.3 = (bf16[1024,256]{1,0:T(8,128)(2,1)S(1)}, bf16[1024,256]{1,0:T(8,128)(2,1)S(1)}, u32[]{:S(2)}, u32[]{:S(2)}) collective-permute-start(bf16[1024,256]{1,0:T(8,128)(2,1)S(1)} %get-tuple-element.25.refs_0_), channel_id=1, source_target_pairs={{0,6},{1,7},{2,0},{3,1},{4,2},{5,3},{6,4},{7,5},{8,14},{9,15},{10,... | collective-permute-start | bytes 1572872 | tf_op jit(solution)/shard_map/ppermute | solution.py:188
  180.9 27.3 %collective-permute-start.6 = (bf16[1024,256]{1,0:T(8,128)(2,1)}, bf16[1024,256]{1,0:T(8,128)(2,1)}, u32[]{:S(2)}, u32[]{:S(2)}) collective-permute-start(bf16[1024,256]{1,0:T(8,128)(2,1)} %broadcast_select_fusion), channel_id=1, source_target_pairs={{0,1},{1,0},{2,3},{3,2},{4,5},{5,4},{6,7},{7,6},{8,9},{9,8},{10,11... | collective-permute-start | bytes 1572872 | tf_op jit(solution)/shard_map/ppermute | solution.py:200
  188.2 16.7 %copy-start.3 = (bf16[1024,256]{1,0:T(8,128)(2,1)}, bf16[1024,256]{1,0:T(8,128)(2,1)S(1)}, u32[]{:S(2)}) copy-start(bf16[1024,256]{1,0:T(8,128)(2,1)S(1)} %collective-permute-done.3.refs_1_) | copy-start | bytes 1572868
  188.2 20.0 %collective-permute-start.5 = (bf16[1024,256]{1,0:T(8,128)(2,1)S(1)}, bf16[1024,256]{1,0:T(8,128)(2,1)}, u32[]{:S(2)}, u32[]{:S(2)}) collective-permute-start(bf16[1024,256]{1,0:T(8,128)(2,1)S(1)} %collective-permute-done.3.refs_1_), channel_id=1, source_target_pairs={{0,1},{1,0},{2,3},{3,2},{4,5},{5,4},{6,7},{7,6},{8,9},{9,8},{10,11... | collective-permute-start | bytes 1572872 | tf_op jit(solution)/shard_map/ppermute | solution.py:199
  200.9 7.3 %copy-start.5 = (bf16[384,384]{1,0:T(8,128)(2,1)S(1)}, bf16[384,384]{1,0:T(8,128)(2,1)}, u32[]{:S(2)}) copy-start(bf16[384,384]{1,0:T(8,128)(2,1)} %constant.33.clone.order_ref) | copy-start | bytes 884740
  200.9 7.3 %copy-start.7 = (f32[1024,1]{1,0:T(8,128)S(1)}, f32[1024,1]{1,0:T(8,128)}, u32[]{:S(2)}) copy-start(f32[1024,1]{1,0:T(8,128)} %copy-done.6) | copy-start | bytes 12292
  204.9 13.9 %collective-permute-start.8 = (bf16[1024,128]{1,0:T(8,128)(2,1)S(1)}, bf16[1024,128]{1,0:T(8,128)(2,1)S(1)}, u32[]{:S(2)}, u32[]{:S(2)}) collective-permute-start(bf16[1024,128]{1,0:T(8,128)(2,1)S(1)} %hist_next.1.last_ref.refs_0_), channel_id=1, source_target_pairs={{0,4},{1,5},{2,6},{3,7},{4,0},{5,1},{6,2},{7,3},{8,12},{9,13},{10,... | collective-permute-start | bytes 786440 | tf_op jit(solution)/shard_map/ppermute | solution.py:188
  208.2 1.0 copy-start.4
  213.1 16.6 %all-to-all-start.2 = ((bf16[4,96,1280]{2,1,0:T(8,128)(2,1)}), bf16[4,96,1280]{2,1,0:T(8,128)(2,1)S(1)}, u32[]{:S(2)}, u32[]{:S(2)}) async-start(bf16[4,96,1280]{2,1,0:T(8,128)(2,1)} %get-tuple-element.31), calls=%async_computation.2 | async-start | bytes 1966080 | tf_op jit(solution)/shard_map/all_to_all | solution.py:205
  216.9 9.5 %collective-permute-start.7 = (bf16[1024,128]{1,0:T(8,128)(2,1)S(1)}, bf16[1024,128]{1,0:T(8,128)(2,1)S(1)}, u32[]{:S(2)}, u32[]{:S(2)}) collective-permute-start(bf16[1024,128]{1,0:T(8,128)(2,1)S(1)} %hist_next.1.last_ref.refs_0_), channel_id=1, source_target_pairs={{0,6},{1,7},{2,0},{3,1},{4,2},{5,3},{6,4},{7,5},{8,14},{9,15},{10,... | collective-permute-start | bytes 786440 | tf_op jit(solution)/shard_map/ppermute | solution.py:188
  218.8 9.4 %collective-permute-start.10 = (bf16[1024,128]{1,0:T(8,128)(2,1)S(1)}, bf16[1024,128]{1,0:T(8,128)(2,1)S(1)}, u32[]{:S(2)}, u32[]{:S(2)}) collective-permute-start(bf16[1024,128]{1,0:T(8,128)(2,1)S(1)} %broadcast_select_fusion.1), channel_id=1, source_target_pairs={{0,1},{1,0},{2,3},{3,2},{4,5},{5,4},{6,7},{7,6},{8,9},{9,8},{10,11... | collective-permute-start | bytes 786440 | tf_op jit(solution)/shard_map/ppermute | solution.py:200
  226.3 3.4 %collective-permute-start.9 = (bf16[1024,128]{1,0:T(8,128)(2,1)S(1)}, bf16[1024,128]{1,0:T(8,128)(2,1)S(1)}, u32[]{:S(2)}, u32[]{:S(2)}) collective-permute-start(bf16[1024,128]{1,0:T(8,128)(2,1)S(1)} %collective-permute-done.7.refs_1_), channel_id=1, source_target_pairs={{0,1},{1,0},{2,3},{3,2},{4,5},{5,4},{6,7},{7,6},{8,9},{9,8},{10,11... | collective-permute-start | bytes 786440 | tf_op jit(solution)/shard_map/ppermute | solution.py:199
  230.8 28.7 %all-to-all-start.3 = ((bf16[16,64,128]{2,1,0:T(8,128)(2,1)}), bf16[16,64,128]{2,1,0:T(8,128)(2,1)S(1)}, u32[]{:S(2)}, u32[]{:S(2)}) async-start(bf16[16,64,128]{2,1,0:T(8,128)(2,1)} %add_first.1), calls=%async_computation.3 | async-start | bytes 524288 | tf_op jit(solution)/shard_map/all_to_all | solution.py:205
  242.7 11.5 %collective-permute-start.11 = (bf16[96,640]{1,0:T(8,128)(2,1)S(1)}, bf16[96,640]{1,0:T(8,128)(2,1)S(1)}, u32[]{:S(2)}, u32[]{:S(2)}) collective-permute-start(bf16[96,640]{1,0:T(8,128)(2,1)S(1)} %get-tuple-element.28), channel_id=1, source_target_pairs={{0,8},{8,16},{16,24},{24,0},{1,9},{9,17},{17,25},{25,1},{2,10},{10... | collective-permute-start | bytes 368648 | tf_op jit(solution)/shard_map/ppermute | solution.py:188
  246.3 8.3 %collective-permute-start.12 = (bf16[96,640]{1,0:T(8,128)(2,1)S(1)}, bf16[96,640]{1,0:T(8,128)(2,1)S(1)}, u32[]{:S(2)}, u32[]{:S(2)}) collective-permute-start(bf16[96,640]{1,0:T(8,128)(2,1)S(1)} %get-tuple-element.29), channel_id=1, source_target_pairs={{0,16},{8,24},{16,0},{24,8},{1,17},{9,25},{17,1},{25,9},{2,18},{10... | collective-permute-start | bytes 368648 | tf_op jit(solution)/shard_map/ppermute | solution.py:188
  250.9 6.8 %collective-permute-start.13 = (bf16[96,640]{1,0:T(8,128)(2,1)S(1)}, bf16[96,640]{1,0:T(8,128)(2,1)S(1)}, u32[]{:S(2)}, u32[]{:S(2)}) collective-permute-start(bf16[96,640]{1,0:T(8,128)(2,1)S(1)} %get-tuple-element.30), channel_id=1, source_target_pairs={{0,24},{8,0},{16,8},{24,16},{1,25},{9,1},{17,9},{25,17},{2,26},{10... | collective-permute-start | bytes 368648 | tf_op jit(solution)/shard_map/ppermute | solution.py:188

commit v8 on v6

--- a/solution.py
+++ b/solution.py
@@ -226,7 +226,6 @@
         name="pack_rest",
     )(place.reshape(1).astype(jnp.int32), starts, event_weights)
     mid = jnp.stack([from_behind(x, BINS[1], t) if t else x for t, x in enumerate(sends)], axis=1)
-    mid, got_a = lax.optimization_barrier((mid, got_a))
     got_b = exchange(mid, BINS[0])
 
     total = owners * CAP

time: 281 us -> 280 us (level)
  no operation moved by 1% of the time
where the time goes in v8:
time: 280 us; the launch traced here: 278 us
  waiting for transfers between devices  138 us (49%)
  starting transfers between devices  56.1 us (20%)
  blocking collectives  45.9 us (16%)
  Pallas kernels  23.9 us (9%)
  local copies, waits for them, and re-layouts  9.65 us (3%)
  other arithmetic  4.9 us (2%)
    all_to_all x3, waiting for transfers between devices, exchange(): return lax.all_to_all(value, axis, split_axis=0, concat_axis=0, tiled=True)  98.8 us
    all_to_all x2, blocking collectives, exchange(): return lax.all_to_all(value, axis, split_axis=0, concat_axis=0, tiled=True)  45.9 us
    ppermute x7, waiting for transfers between devices, from_behind(): return lax.ppermute(value, axis, pairs)  37.4 us
    all_to_all x3, starting transfers between devices, exchange(): return lax.all_to_all(value, axis, split_axis=0, concat_axis=0, tiled=True)  26.5 us
    ppermute x7, starting transfers between devices, from_behind(): return lax.ppermute(value, axis, pairs)  21.9 us
    pallas_call x1, Pallas kernels, body(): pl.pallas_call(hist_first, out_shape=[jax.ShapeDtypeStruct((bins_dev, 2 *...  6.55 us
  transfers between devices with their start and end apart: 14, of which 8 were waited for; matrix products, arithmetic and copies ran while one was open for 3% of the time, Pallas kernels for 6%

profile of v8, /device:TPU:6, one launch (start us, length us, event | category | flops | bytes accessed | tf_op | source)
XLA Modules:
  0.0 278.5 jit_solution(14225070154113000743)
XLA Ops:
  1.7 1.7 copy-done
  4.0 4.1 %pack_first.1 = bf16[64,152,128]{2,1,0:T(8,128)(2,1)} custom-call(s32[64]{0:T(128)S(1)} %convert_reduce_fusion.starts_ref, s32[24,128]{1,0:T(8,128)S(1)} %bitcast.21, f32[24,128]{1,0:T(8,128)S(1)} %bitcast_convert_fusion.nominal_ref, bf16[3072,384]{1,0:T(8,128)(2,1)S(1)} %copy-done), custom_call_target="tpu_custom_call" | custom-call | flops 226492416 | bytes 4980736 | tf_op jit(solution)/shard_map/pack_first/pallas_call | solution.py:209
  8.1 19.1 %all-to-all-start = ((bf16[64,152,128]{2,1,0:T(8,128)(2,1)}), bf16[64,152,128]{2,1,0:T(8,128)(2,1)}, u32[]{:S(2)}, u32[]{:S(2)}) async-start(bf16[64,152,128]{2,1,0:T(8,128)(2,1)} %pack_first.1), calls=%async_computation | async-start | bytes 4980736 | tf_op jit(solution)/shard_map/all_to_all | solution.py:195
  27.3 2.5 pack_rest.1
  29.8 3.4 %collective-permute-start = (bf16[16,72,128]{2,1,0:T(8,128)(2,1)S(1)}, bf16[16,72,128]{2,1,0:T(8,128)(2,1)S(1)}, u32[]{:S(2)}, u32[]{:S(2)}) collective-permute-start(bf16[16,72,128]{2,1,0:T(8,128)(2,1)S(1)} %get-tuple-element.17), channel_id=1, source_target_pairs={{0,8},{8,16},{16,24},{24,0},{1,9},{9,17},{17,25},{25,1},{2,10},{10... | collective-permute-start | bytes 884744 | tf_op jit(solution)/shard_map/ppermute | solution.py:178
  33.2 4.6 %collective-permute-start.1 = (bf16[16,72,128]{2,1,0:T(8,128)(2,1)S(1)}, bf16[16,72,128]{2,1,0:T(8,128)(2,1)S(1)}, u32[]{:S(2)}, u32[]{:S(2)}) collective-permute-start(bf16[16,72,128]{2,1,0:T(8,128)(2,1)S(1)} %get-tuple-element.18), channel_id=1, source_target_pairs={{0,16},{8,24},{16,0},{24,8},{1,17},{9,25},{17,1},{25,9},{2,18},{10... | collective-permute-start | bytes 884744 | tf_op jit(solution)/shard_map/ppermute | solution.py:178
  37.8 3.4 %collective-permute-start.2 = (bf16[16,72,128]{2,1,0:T(8,128)(2,1)S(1)}, bf16[16,72,128]{2,1,0:T(8,128)(2,1)S(1)}, u32[]{:S(2)}, u32[]{:S(2)}) collective-permute-start(bf16[16,72,128]{2,1,0:T(8,128)(2,1)S(1)} %get-tuple-element.19), channel_id=1, source_target_pairs={{0,24},{8,0},{16,8},{24,16},{1,25},{9,1},{17,9},{25,17},{2,26},{10... | collective-permute-start | bytes 884744 | tf_op jit(solution)/shard_map/ppermute | solution.py:178
  41.2 4.1 %collective-permute-done = bf16[16,72,128]{2,1,0:T(8,128)(2,1)S(1)} collective-permute-done((bf16[16,72,128]{2,1,0:T(8,128)(2,1)S(1)}, bf16[16,72,128]{2,1,0:T(8,128)(2,1)S(1)}, u32[]{:S(2)}, u32[]{:S(2)}) %collective-permute-start) | collective-permute-done | bytes 294944 | tf_op jit(solution)/shard_map/ppermute | solution.py:178
  45.3 9.3 %collective-permute-done.1 = bf16[16,72,128]{2,1,0:T(8,128)(2,1)S(1)} collective-permute-done((bf16[16,72,128]{2,1,0:T(8,128)(2,1)S(1)}, bf16[16,72,128]{2,1,0:T(8,128)(2,1)S(1)}, u32[]{:S(2)}, u32[]{:S(2)}) %collective-permute-start.1) | collective-permute-done | bytes 294944 | tf_op jit(solution)/shard_map/ppermute | solution.py:178
  56.0 88.2 %all-to-all-done = bf16[64,152,128]{2,1,0:T(8,128)(2,1)} async-done(((bf16[64,152,128]{2,1,0:T(8,128)(2,1)}), bf16[64,152,128]{2,1,0:T(8,128)(2,1)}, u32[]{:S(2)}, u32[]{:S(2)}) %all-to-all-start) | async-done | bytes 2490400 | tf_op jit(solution)/shard_map/all_to_all | solution.py:195
  144.2 3.7 %all-to-all-start.1 = ((bf16[16,4,72,128]{3,2,1,0:T(8,128)(2,1)}), bf16[16,4,72,128]{3,2,1,0:T(8,128)(2,1)S(1)}, u32[]{:S(2)}, u32[]{:S(2)}) async-start(bf16[16,4,72,128]{3,2,1,0:T(8,128)(2,1)} %copy.16), calls=%async_computation.1 | async-start | bytes 2359296 | tf_op jit(solution)/shard_map/all_to_all | solution.py:195
  152.3 1.8 fusion.4
  154.1 6.6 %hist_first.1 = (bf16[1024,256]{1,0:T(8,128)(2,1)S(1)}, f32[1024,1]{1,0:T(8,128)S(1)}) custom-call(s32[1,4608]{1,0:T(1,128)S(1)} %convert_element_type.35.bins_ref, bf16[8,4608]{1,0:T(8,128)(2,1)S(1)} %broadcast_in_dim.2.nominal_ref, f32[1024,1]{1,0:T(8,128)S(1)} %copy.14.background_ref, f32[1024,1]{1,0:T(8,128)S(1)} %copy.15.observed_ref, ...), custom_call_target="tpu_custom_call" | custom-call | flops 4831838208 | bytes 2359296 | tf_op jit(solution)/shard_map/hist_first/pallas_call | solution.py:240
  161.5 3.4 %collective-permute-start.4 = (bf16[1024,256]{1,0:T(8,128)(2,1)S(1)}, bf16[1024,256]{1,0:T(8,128)(2,1)S(1)}, u32[]{:S(2)}, u32[]{:S(2)}) collective-permute-start(bf16[1024,256]{1,0:T(8,128)(2,1)S(1)} %get-tuple-element.20.refs_0_), channel_id=1, source_target_pairs={{0,4},{1,5},{2,6},{3,7},{4,0},{5,1},{6,2},{7,3},{8,12},{9,13},{10,... | collective-permute-start | bytes 1572872 | tf_op jit(solution)/shard_map/ppermute | solution.py:178
  165.0 1.9 collective-permute-start.3
  166.9 13.1 %collective-permute-done.4.refs_2_ = bf16[1024,256]{1,0:T(8,128)(2,1)S(1)} collective-permute-done((bf16[1024,256]{1,0:T(8,128)(2,1)S(1)}, bf16[1024,256]{1,0:T(8,128)(2,1)S(1)}, u32[]{:S(2)}, u32[]{:S(2)}) %collective-permute-start.4) | collective-permute-done | bytes 524320 | tf_op jit(solution)/shard_map/ppermute | solution.py:178
  180.8 1.9 collective-permute-start.6
  182.7 5.3 %collective-permute-done.3.refs_1_ = bf16[1024,256]{1,0:T(8,128)(2,1)S(1)} collective-permute-done((bf16[1024,256]{1,0:T(8,128)(2,1)S(1)}, bf16[1024,256]{1,0:T(8,128)(2,1)S(1)}, u32[]{:S(2)}, u32[]{:S(2)}) %collective-permute-start.3) | collective-permute-done | bytes 524320 | tf_op jit(solution)/shard_map/ppermute | solution.py:178
  188.0 1.9 collective-permute-start.5
  190.3 10.5 %all-to-all-done.1 = bf16[16,4,72,128]{3,2,1,0:T(8,128)(2,1)S(1)} async-done(((bf16[16,4,72,128]{3,2,1,0:T(8,128)(2,1)}), bf16[16,4,72,128]{3,2,1,0:T(8,128)(2,1)S(1)}, u32[]{:S(2)}, u32[]{:S(2)}) %all-to-all-start.1) | async-done | bytes 1179680 | tf_op jit(solution)/shard_map/all_to_all | solution.py:195
  200.8 4.0 %hist_next.1.last_ref.refs_0_ = bf16[1024,128]{1,0:T(8,128)(2,1)S(1)} custom-call(s32[1,4608]{1,0:T(1,128)S(1)} %reshape.84.bins_ref, bf16[4608,128]{1,0:T(8,128)(2,1)S(1)} %bitcast.17), custom_call_target="tpu_custom_call" | custom-call | flops 2415919104 | bytes 1179648 | tf_op jit(solution)/shard_map/hist_next/pallas_call | solution.py:250
  204.8 3.3 %collective-permute-start.8 = (bf16[1024,128]{1,0:T(8,128)(2,1)S(1)}, bf16[1024,128]{1,0:T(8,128)(2,1)S(1)}, u32[]{:S(2)}, u32[]{:S(2)}) collective-permute-start(bf16[1024,128]{1,0:T(8,128)(2,1)S(1)} %hist_next.1.last_ref.refs_0_), channel_id=1, source_target_pairs={{0,4},{1,5},{2,6},{3,7},{4,0},{5,1},{6,2},{7,3},{8,12},{9,13},{10,... | collective-permute-start | bytes 786440 | tf_op jit(solution)/shard_map/ppermute | solution.py:178
  209.2 3.9 %gram_first.1 = (bf16[4,96,1280]{2,1,0:T(8,128)(2,1)}, bf16[384,1024]{1,0:T(8,128)(2,1)S(1)}) custom-call(s32[5]{0:T(128)S(1)} %stack.26.slots_ref, f32[1024,1]{1,0:T(8,128)S(1)} %copy-done.7, bf16[384,384]{1,0:T(8,128)(2,1)S(1)} %copy-done.5, bf16[1024,128]{1,0:T(8,128)(2,1)S(1)} %hist_next.1.last_ref.refs_0_, ...), custom_call_target="tpu_custom_call" | custom-call | flops 1207959552 | bytes 2621440 | tf_op jit(solution)/shard_map/gram_first/pallas_call | solution.py:271
  213.1 3.7 %all-to-all-start.2 = ((bf16[4,96,1280]{2,1,0:T(8,128)(2,1)}), bf16[4,96,1280]{2,1,0:T(8,128)(2,1)S(1)}, u32[]{:S(2)}, u32[]{:S(2)}) async-start(bf16[4,96,1280]{2,1,0:T(8,128)(2,1)} %get-tuple-element.21), calls=%async_computation.2 | async-start | bytes 1966080 | tf_op jit(solution)/shard_map/all_to_all | solution.py:195
  216.8 1.9 collective-permute-start.7
  218.8 1.9 collective-permute-start.10
  220.7 5.6 %collective-permute-done.7.refs_1_ = bf16[1024,128]{1,0:T(8,128)(2,1)S(1)} collective-permute-done((bf16[1024,128]{1,0:T(8,128)(2,1)S(1)}, bf16[1024,128]{1,0:T(8,128)(2,1)S(1)}, u32[]{:S(2)}, u32[]{:S(2)}) %collective-permute-start.7) | collective-permute-done | bytes 262176 | tf_op jit(solution)/shard_map/ppermute | solution.py:178
  226.3 1.9 collective-permute-start.9
  228.2 1.5 collective-permute-done.9.refs_3_
  229.7 1.7 gram_last.1
  231.4 14.0 %all_to_all.25.last_ref = bf16[4,96,640]{2,1,0:T(8,128)(2,1)S(1)} all-to-all(bf16[4,96,640]{2,1,0:T(8,128)(2,1)S(1)} %gram_last.1), channel_id=1, replica_groups=mesh['bins_0'=16,'bins_1'=4,'params'=8] {'bins_1'}, dimensions={0} | all-to-all | bytes 983040 | tf_op jit(solution)/shard_map/all_to_all | solution.py:195
  245.9 31.9 %all_to_all.26.got_ref = bf16[16,96,128]{2,1,0:T(8,128)(2,1)S(1)} all-to-all(bf16[16,96,128]{2,1,0:T(8,128)(2,1)S(1)} %add_across.1), channel_id=1, replica_groups=mesh['bins_0'=16,'bins_1'=4,'params'=8] {'bins_0'}, dimensions={0} | all-to-all | bytes 786432 | tf_op jit(solution)/shard_map/all_to_all | solution.py:195
  (49 shorter events, 12.2 us)
Async XLA Ops:
  1.7 1.7 copy-start
  3.3 0.7 copy-start.2
  8.1 19.1 %copy-start.1 = (bf16[3072,384]{1,0:T(8,128)(2,1)S(1)}, bf16[3072,384]{1,0:T(8,128)(2,1)}, u32[]{:S(2)}) copy-start(bf16[3072,384]{1,0:T(8,128)(2,1)} %w_ref.3) | copy-start | bytes 7077892
  8.1 136.1 %all-to-all-start = ((bf16[64,152,128]{2,1,0:T(8,128)(2,1)}), bf16[64,152,128]{2,1,0:T(8,128)(2,1)}, u32[]{:S(2)}, u32[]{:S(2)}) async-start(bf16[64,152,128]{2,1,0:T(8,128)(2,1)} %pack_first.1), calls=%async_computation | async-start | bytes 4980736 | tf_op jit(solution)/shard_map/all_to_all | solution.py:195
  29.8 15.5 %collective-permute-start = (bf16[16,72,128]{2,1,0:T(8,128)(2,1)S(1)}, bf16[16,72,128]{2,1,0:T(8,128)(2,1)S(1)}, u32[]{:S(2)}, u32[]{:S(2)}) collective-permute-start(bf16[16,72,128]{2,1,0:T(8,128)(2,1)S(1)} %get-tuple-element.17), channel_id=1, source_target_pairs={{0,8},{8,16},{16,24},{24,0},{1,9},{9,17},{17,25},{25,1},{2,10},{10... | collective-permute-start | bytes 884744 | tf_op jit(solution)/shard_map/ppermute | solution.py:178
  33.2 21.4 %collective-permute-start.1 = (bf16[16,72,128]{2,1,0:T(8,128)(2,1)S(1)}, bf16[16,72,128]{2,1,0:T(8,128)(2,1)S(1)}, u32[]{:S(2)}, u32[]{:S(2)}) collective-permute-start(bf16[16,72,128]{2,1,0:T(8,128)(2,1)S(1)} %get-tuple-element.18), channel_id=1, source_target_pairs={{0,16},{8,24},{16,0},{24,8},{1,17},{9,25},{17,1},{25,9},{2,18},{10... | collective-permute-start | bytes 884744 | tf_op jit(solution)/shard_map/ppermute | solution.py:178
  37.8 16.8 %collective-permute-start.2 = (bf16[16,72,128]{2,1,0:T(8,128)(2,1)S(1)}, bf16[16,72,128]{2,1,0:T(8,128)(2,1)S(1)}, u32[]{:S(2)}, u32[]{:S(2)}) collective-permute-start(bf16[16,72,128]{2,1,0:T(8,128)(2,1)S(1)} %get-tuple-element.19), channel_id=1, source_target_pairs={{0,24},{8,0},{16,8},{24,16},{1,25},{9,1},{17,9},{25,17},{2,26},{10... | collective-permute-start | bytes 884744 | tf_op jit(solution)/shard_map/ppermute | solution.py:178
  56.0 92.0 %copy-start.9 = (f32[1024]{0:T(1024)S(1)}, f32[1024]{0:T(1024)}, u32[]{:S(2)}) copy-start(f32[1024]{0:T(1024)} %param.9) | copy-start | bytes 12292
  56.0 92.2 %copy-start.10 = (f32[1024]{0:T(1024)S(1)}, f32[1024]{0:T(1024)}, u32[]{:S(2)}) copy-start(f32[1024]{0:T(1024)} %param.10) | copy-start | bytes 12292
  144.2 56.6 %all-to-all-start.1 = ((bf16[16,4,72,128]{3,2,1,0:T(8,128)(2,1)}), bf16[16,4,72,128]{3,2,1,0:T(8,128)(2,1)S(1)}, u32[]{:S(2)}, u32[]{:S(2)}) async-start(bf16[16,4,72,128]{3,2,1,0:T(8,128)(2,1)} %copy.16), calls=%async_computation.1 | async-start | bytes 2359296 | tf_op jit(solution)/shard_map/all_to_all | solution.py:195
  160.7 0.8 copy-start.6
  161.5 28.6 %copy-start.8 = (s32[64,1,72]{2,1,0:T(1,128)S(1)}, s32[64,1,72]{2,1,0:T(1,128)}, u32[]{:S(2)}) copy-start(s32[64,1,72]{2,1,0:T(1,128)} %get-tuple-element.26) | copy-start | bytes 55300
  161.5 18.4 %collective-permute-start.4 = (bf16[1024,256]{1,0:T(8,128)(2,1)S(1)}, bf16[1024,256]{1,0:T(8,128)(2,1)S(1)}, u32[]{:S(2)}, u32[]{:S(2)}) collective-permute-start(bf16[1024,256]{1,0:T(8,128)(2,1)S(1)} %get-tuple-element.20.refs_0_), channel_id=1, source_target_pairs={{0,4},{1,5},{2,6},{3,7},{4,0},{5,1},{6,2},{7,3},{8,12},{9,13},{10,... | collective-permute-start | bytes 1572872 | tf_op jit(solution)/shard_map/ppermute | solution.py:178
  165.0 23.1 %collective-permute-start.3 = (bf16[1024,256]{1,0:T(8,128)(2,1)S(1)}, bf16[1024,256]{1,0:T(8,128)(2,1)S(1)}, u32[]{:S(2)}, u32[]{:S(2)}) collective-permute-start(bf16[1024,256]{1,0:T(8,128)(2,1)S(1)} %get-tuple-element.20.refs_0_), channel_id=1, source_target_pairs={{0,6},{1,7},{2,0},{3,1},{4,2},{5,3},{6,4},{7,5},{8,14},{9,15},{10,... | collective-permute-start | bytes 1572872 | tf_op jit(solution)/shard_map/ppermute | solution.py:178
  180.8 27.4 %collective-permute-start.6 = (bf16[1024,256]{1,0:T(8,128)(2,1)}, bf16[1024,256]{1,0:T(8,128)(2,1)}, u32[]{:S(2)}, u32[]{:S(2)}) collective-permute-start(bf16[1024,256]{1,0:T(8,128)(2,1)} %broadcast_select_fusion), channel_id=1, source_target_pairs={{0,1},{1,0},{2,3},{3,2},{4,5},{5,4},{6,7},{7,6},{8,9},{9,8},{10,11... | collective-permute-start | bytes 1572872 | tf_op jit(solution)/shard_map/ppermute | solution.py:190
  188.0 16.8 %copy-start.3 = (bf16[1024,256]{1,0:T(8,128)(2,1)}, bf16[1024,256]{1,0:T(8,128)(2,1)S(1)}, u32[]{:S(2)}) copy-start(bf16[1024,256]{1,0:T(8,128)(2,1)S(1)} %collective-permute-done.3.refs_1_) | copy-start | bytes 1572868
  188.0 20.1 %collective-permute-start.5 = (bf16[1024,256]{1,0:T(8,128)(2,1)S(1)}, bf16[1024,256]{1,0:T(8,128)(2,1)}, u32[]{:S(2)}, u32[]{:S(2)}) collective-permute-start(bf16[1024,256]{1,0:T(8,128)(2,1)S(1)} %collective-permute-done.3.refs_1_), channel_id=1, source_target_pairs={{0,1},{1,0},{2,3},{3,2},{4,5},{5,4},{6,7},{7,6},{8,9},{9,8},{10,11... | collective-permute-start | bytes 1572872 | tf_op jit(solution)/shard_map/ppermute | solution.py:189
  200.8 7.3 %copy-start.5 = (bf16[384,384]{1,0:T(8,128)(2,1)S(1)}, bf16[384,384]{1,0:T(8,128)(2,1)}, u32[]{:S(2)}) copy-start(bf16[384,384]{1,0:T(8,128)(2,1)} %constant.33.clone.order_ref) | copy-start | bytes 884740
  200.8 7.3 %copy-start.7 = (f32[1024,1]{1,0:T(8,128)S(1)}, f32[1024,1]{1,0:T(8,128)}, u32[]{:S(2)}) copy-start(f32[1024,1]{1,0:T(8,128)} %copy-done.6) | copy-start | bytes 12292
  204.8 13.9 %collective-permute-start.8 = (bf16[1024,128]{1,0:T(8,128)(2,1)S(1)}, bf16[1024,128]{1,0:T(8,128)(2,1)S(1)}, u32[]{:S(2)}, u32[]{:S(2)}) collective-permute-start(bf16[1024,128]{1,0:T(8,128)(2,1)S(1)} %hist_next.1.last_ref.refs_0_), channel_id=1, source_target_pairs={{0,4},{1,5},{2,6},{3,7},{4,0},{5,1},{6,2},{7,3},{8,12},{9,13},{10,... | collective-permute-start | bytes 786440 | tf_op jit(solution)/shard_map/ppermute | solution.py:178
  208.2 1.0 copy-start.4
  213.1 15.1 %all-to-all-start.2 = ((bf16[4,96,1280]{2,1,0:T(8,128)(2,1)}), bf16[4,96,1280]{2,1,0:T(8,128)(2,1)S(1)}, u32[]{:S(2)}, u32[]{:S(2)}) async-start(bf16[4,96,1280]{2,1,0:T(8,128)(2,1)} %get-tuple-element.21), calls=%async_computation.2 | async-start | bytes 1966080 | tf_op jit(solution)/shard_map/all_to_all | solution.py:195
  216.8 9.5 %collective-permute-start.7 = (bf16[1024,128]{1,0:T(8,128)(2,1)S(1)}, bf16[1024,128]{1,0:T(8,128)(2,1)S(1)}, u32[]{:S(2)}, u32[]{:S(2)}) collective-permute-start(bf16[1024,128]{1,0:T(8,128)(2,1)S(1)} %hist_next.1.last_ref.refs_0_), channel_id=1, source_target_pairs={{0,6},{1,7},{2,0},{3,1},{4,2},{5,3},{6,4},{7,5},{8,14},{9,15},{10,... | collective-permute-start | bytes 786440 | tf_op jit(solution)/shard_map/ppermute | solution.py:178
  218.8 9.4 %collective-permute-start.10 = (bf16[1024,128]{1,0:T(8,128)(2,1)S(1)}, bf16[1024,128]{1,0:T(8,128)(2,1)S(1)}, u32[]{:S(2)}, u32[]{:S(2)}) collective-permute-start(bf16[1024,128]{1,0:T(8,128)(2,1)S(1)} %broadcast_select_fusion.1), channel_id=1, source_target_pairs={{0,1},{1,0},{2,3},{3,2},{4,5},{5,4},{6,7},{7,6},{8,9},{9,8},{10,11... | collective-permute-start | bytes 786440 | tf_op jit(solution)/shard_map/ppermute | solution.py:190
  226.3 3.4 %collective-permute-start.9 = (bf16[1024,128]{1,0:T(8,128)(2,1)S(1)}, bf16[1024,128]{1,0:T(8,128)(2,1)S(1)}, u32[]{:S(2)}, u32[]{:S(2)}) collective-permute-start(bf16[1024,128]{1,0:T(8,128)(2,1)S(1)} %collective-permute-done.7.refs_1_), channel_id=1, source_target_pairs={{0,1},{1,0},{2,3},{3,2},{4,5},{5,4},{6,7},{7,6},{8,9},{9,8},{10,11... | collective-permute-start | bytes 786440 | tf_op jit(solution)/shard_map/ppermute | solution.py:189

commit v9 on v8

--- a/solution.py
+++ b/solution.py
@@ -118,17 +118,18 @@
     out_ref[...] = acc[...].astype(jnp.bfloat16)
 
 
-def left_side(curve_ref, order_ref, first_ref, last_ref):
-    own = jnp.concatenate([first_ref[...], last_ref[...]], axis=1)
-    weighted = (curve_ref[...] * own.astype(jnp.float32)).astype(jnp.bfloat16)
-    return lax.dot_general(
-        order_ref[...], weighted, (((1,), (1,)), ((), ())), preferred_element_type=jnp.float32
-    ).astype(jnp.bfloat16)
-
-
-def gram_first(slots_ref, curve_ref, order_ref, last_ref, *refs):
+def side_of(curve_ref, order, own_ref):
+    weighted = (curve_ref[...] * own_ref[...].astype(jnp.float32)).astype(jnp.bfloat16)
+    return lax.dot_general(order, weighted, (((1,), (1,)), ((), ())), preferred_element_type=jnp.float32)
+
+
+def side_first(curve_ref, order_ref, first_ref, out_ref):
+    out_ref[...] = side_of(curve_ref, order_ref[:, : 2 * COLS], first_ref).astype(jnp.bfloat16)
+
+
+def gram_first(slots_ref, curve_ref, order_ref, side_ref, last_ref, *refs):
     firsts, (out_ref, lhs_ref) = refs[:-2], refs[-2:]
-    lhs = left_side(curve_ref, order_ref, firsts[0], last_ref)
+    lhs = side_ref[...] + side_of(curve_ref, order_ref[:, 2 * COLS :], last_ref).astype(jnp.bfloat16)
     lhs_ref[...] = lhs
     wide, step = firsts[0].shape[1], out_ref.shape[1]
     for k, part in enumerate(firsts):
@@ -247,6 +248,21 @@
         cost_estimate=cost(2 * total * bins_dev * 512, 2 * total * COLS * 2),
         name="hist_first",
     )(local, nom, background.reshape(bins_dev, 1), observed.reshape(bins_dev, 1), left, right)
+    lines = width // owners
+    j = np.arange(width)
+    source = ((j % (width // n1)) // lines * n1 + j // (width // n1)) * lines + j % lines
+    order = np.zeros((width, width), np.float32)
+    order[j, source] = 1.0
+    side = pl.pallas_call(
+        side_first,
+        out_shape=jax.ShapeDtypeStruct((width, bins_dev), bf16),
+        in_specs=[VMEM] * 3,
+        out_specs=VMEM,
+        compiler_params=PARAMS,
+        cost_estimate=cost(2 * bins_dev * width * 2 * COLS, 2 * bins_dev * width * 2),
+        name="side_first",
+    )(curve, jnp.asarray(order, bf16), first)
+    side, got_b = lax.optimization_barrier((side, got_b))
     last = pl.pallas_call(
         hist_next,
         out_shape=jax.ShapeDtypeStruct((bins_dev, COLS), bf16),
@@ -263,23 +279,18 @@
     lasts = [last] + partners(last)[0]
     slots = jnp.stack([jnp.asarray(k, jnp.int32) for k in [0] + slots])
 
-    lines = width // owners
-    j = np.arange(width)
-    source = ((j % (width // n1)) // lines * n1 + j // (width // n1)) * lines + j % lines
-    order = np.zeros((width, width), np.float32)
-    order[j, source] = 1.0
     part_a, lhs = pl.pallas_call(
         gram_first,
         out_shape=[
             jax.ShapeDtypeStruct((n1, width // n1, turns * 2 * COLS), bf16),
             jax.ShapeDtypeStruct((width, bins_dev), bf16),
         ],
-        in_specs=[SMEM] + [VMEM] * (3 + turns),
+        in_specs=[SMEM] + [VMEM] * (4 + turns),
         out_specs=[VMEM] * 2,
         compiler_params=PARAMS,
         cost_estimate=cost(2 * bins_dev * width * 2 * COLS * (turns + 1), 2 * turns * COLS * bins_dev * 2),
         name="gram_first",
-    )(slots, curve, jnp.asarray(order, bf16), last, *firsts)
+    )(slots, curve, jnp.asarray(order, bf16), side, last, *firsts)
     part_a, lhs = lax.optimization_barrier((exchange(part_a, BINS[1]), lhs))
     part_b = pl.pallas_call(
         gram_last,

time: 280 us -> 279 us (level)
  blocking collectives: 45.9 us -> 40.1 us
    all_to_all x2, blocking collectives: 45.9 us -> 40.1 us  [exchange(): return lax.all_to_all(value, axis, split_axis=0, concat_axis=0, tiled=True)]
  transfers between devices with their start and end apart: 14 -> 14, of which waited for: 8 -> 7; matrix products, arithmetic and copies ran while one was open for 3% -> 3% of each run, Pallas kernels for 6% -> 6%
where the time goes in v9:
time: 279 us; the launch traced here: 276 us
  waiting for transfers between devices  138 us (49%)
  starting transfers between devices  58.2 us (21%)
  blocking collectives  40.1 us (14%)
  Pallas kernels  24.7 us (9%)
  local copies, waits for them, and re-layouts  10.5 us (4%)
  other arithmetic  4.42 us (2%)
    all_to_all x3, waiting for transfers between devices, exchange(): return lax.all_to_all(value, axis, split_axis=0, concat_axis=0, tiled=True)  101 us
    all_to_all x2, blocking collectives, exchange(): return lax.all_to_all(value, axis, split_axis=0, concat_axis=0, tiled=True)  40.1 us
    ppermute x7, waiting for transfers between devices, from_behind(): return lax.ppermute(value, axis, pairs)  37 us
    all_to_all x3, starting transfers between devices, exchange(): return lax.all_to_all(value, axis, split_axis=0, concat_axis=0, tiled=True)  27.7 us
    ppermute x7, starting transfers between devices, from_behind(): return lax.ppermute(value, axis, pairs)  21.8 us
    pallas_call x1, Pallas kernels, body(): pl.pallas_call(hist_first, out_shape=[jax.ShapeDtypeStruct((bins_dev, 2 *...  6.55 us
  transfers between devices with their start and end apart: 14, of which 7 were waited for; matrix products, arithmetic and copies ran while one was open for 3% of the time, Pallas kernels for 6%

profile of v9, /device:TPU:6, one launch (start us, length us, event | category | flops | bytes accessed | tf_op | source)
XLA Modules:
  0.0 276.0 jit_solution(11528882841236093359)
XLA Ops:
  1.7 1.7 copy-done
  4.0 4.1 %pack_first.1 = bf16[64,152,128]{2,1,0:T(8,128)(2,1)} custom-call(s32[64]{0:T(128)S(1)} %convert_reduce_fusion.starts_ref, s32[24,128]{1,0:T(8,128)S(1)} %bitcast.20, f32[24,128]{1,0:T(8,128)S(1)} %bitcast_convert_fusion.nominal_ref, bf16[3072,384]{1,0:T(8,128)(2,1)S(1)} %copy-done), custom_call_target="tpu_custom_call" | custom-call | flops 226492416 | bytes 4980736 | tf_op jit(solution)/shard_map/pack_first/pallas_call | solution.py:210
  8.1 19.1 %all-to-all-start = ((bf16[64,152,128]{2,1,0:T(8,128)(2,1)}), bf16[64,152,128]{2,1,0:T(8,128)(2,1)}, u32[]{:S(2)}, u32[]{:S(2)}) async-start(bf16[64,152,128]{2,1,0:T(8,128)(2,1)} %pack_first.1), calls=%async_computation | async-start | bytes 4980736 | tf_op jit(solution)/shard_map/all_to_all | solution.py:196
  27.3 2.5 pack_rest.1
  29.8 4.6 %collective-permute-start.2 = (bf16[16,72,128]{2,1,0:T(8,128)(2,1)S(1)}, bf16[16,72,128]{2,1,0:T(8,128)(2,1)S(1)}, u32[]{:S(2)}, u32[]{:S(2)}) collective-permute-start(bf16[16,72,128]{2,1,0:T(8,128)(2,1)S(1)} %get-tuple-element.22), channel_id=1, source_target_pairs={{0,24},{8,0},{16,8},{24,16},{1,25},{9,1},{17,9},{25,17},{2,26},{10... | collective-permute-start | bytes 884744 | tf_op jit(solution)/shard_map/ppermute | solution.py:179
  34.4 2.8 %collective-permute-start.1 = (bf16[16,72,128]{2,1,0:T(8,128)(2,1)S(1)}, bf16[16,72,128]{2,1,0:T(8,128)(2,1)S(1)}, u32[]{:S(2)}, u32[]{:S(2)}) collective-permute-start(bf16[16,72,128]{2,1,0:T(8,128)(2,1)S(1)} %get-tuple-element.21), channel_id=1, source_target_pairs={{0,16},{8,24},{16,0},{24,8},{1,17},{9,25},{17,1},{25,9},{2,18},{10... | collective-permute-start | bytes 884744 | tf_op jit(solution)/shard_map/ppermute | solution.py:179
  37.2 2.8 %collective-permute-start = (bf16[16,72,128]{2,1,0:T(8,128)(2,1)S(1)}, bf16[16,72,128]{2,1,0:T(8,128)(2,1)S(1)}, u32[]{:S(2)}, u32[]{:S(2)}) collective-permute-start(bf16[16,72,128]{2,1,0:T(8,128)(2,1)S(1)} %get-tuple-element.20), channel_id=1, source_target_pairs={{0,8},{8,16},{16,24},{24,0},{1,9},{9,17},{17,25},{25,1},{2,10},{10... | collective-permute-start | bytes 884744 | tf_op jit(solution)/shard_map/ppermute | solution.py:179
  40.0 9.5 %collective-permute-done.2 = bf16[16,72,128]{2,1,0:T(8,128)(2,1)S(1)} collective-permute-done((bf16[16,72,128]{2,1,0:T(8,128)(2,1)S(1)}, bf16[16,72,128]{2,1,0:T(8,128)(2,1)S(1)}, u32[]{:S(2)}, u32[]{:S(2)}) %collective-permute-start.2) | collective-permute-done | bytes 294944 | tf_op jit(solution)/shard_map/ppermute | solution.py:179
  50.4 6.7 %collective-permute-done = bf16[16,72,128]{2,1,0:T(8,128)(2,1)S(1)} collective-permute-done((bf16[16,72,128]{2,1,0:T(8,128)(2,1)S(1)}, bf16[16,72,128]{2,1,0:T(8,128)(2,1)S(1)}, u32[]{:S(2)}, u32[]{:S(2)}) %collective-permute-start) | collective-permute-done | bytes 294944 | tf_op jit(solution)/shard_map/ppermute | solution.py:179
  57.3 1.1 copy.17
  58.5 85.7 %all-to-all-done = bf16[64,152,128]{2,1,0:T(8,128)(2,1)} async-done(((bf16[64,152,128]{2,1,0:T(8,128)(2,1)}), bf16[64,152,128]{2,1,0:T(8,128)(2,1)}, u32[]{:S(2)}, u32[]{:S(2)}) %all-to-all-start) | async-done | bytes 2490400 | tf_op jit(solution)/shard_map/all_to_all | solution.py:196
  144.2 4.4 %all-to-all-start.1 = ((bf16[16,4,72,128]{3,2,1,0:T(8,128)(2,1)}), bf16[16,4,72,128]{3,2,1,0:T(8,128)(2,1)}, u32[]{:S(2)}, u32[]{:S(2)}) async-start(bf16[16,4,72,128]{3,2,1,0:T(8,128)(2,1)} %copy.17), calls=%async_computation.1 | async-start | bytes 2359296 | tf_op jit(solution)/shard_map/all_to_all | solution.py:196
  148.8 1.0 copy.16.observed_ref
  153.3 1.9 fusion.4
  155.2 6.6 %hist_first.1 = (bf16[1024,256]{1,0:T(8,128)(2,1)S(1)}, f32[1024,1]{1,0:T(8,128)S(1)}) custom-call(s32[1,4608]{1,0:T(1,128)S(1)} %convert_element_type.35.bins_ref, bf16[8,4608]{1,0:T(8,128)(2,1)S(1)} %broadcast_in_dim.2.nominal_ref, f32[1024,1]{1,0:T(8,128)S(1)} %copy.15.background_ref, f32[1024,1]{1,0:T(8,128)S(1)} %copy-done.6, ...), custom_call_target="tpu_custom_call" | custom-call | flops 4831838208 | bytes 2359296 | tf_op jit(solution)/shard_map/hist_first/pallas_call | solution.py:241
  161.8 2.9 %collective-permute-start.3 = (bf16[1024,256]{1,0:T(8,128)(2,1)S(1)}, bf16[1024,256]{1,0:T(8,128)(2,1)}, u32[]{:S(2)}, u32[]{:S(2)}) collective-permute-start(bf16[1024,256]{1,0:T(8,128)(2,1)S(1)} %get-tuple-element.18.first_ref.refs_0_), channel_id=1, source_target_pairs={{0,6},{1,7},{2,0},{3,1},{4,2},{5,3},{6,4},{7,5},{8,14},{9,15},{10,... | collective-permute-start | bytes 1572872 | tf_op jit(solution)/shard_map/ppermute | solution.py:179
  164.7 3.0 %collective-permute-start.4 = (bf16[1024,256]{1,0:T(8,128)(2,1)S(1)}, bf16[1024,256]{1,0:T(8,128)(2,1)S(1)}, u32[]{:S(2)}, u32[]{:S(2)}) collective-permute-start(bf16[1024,256]{1,0:T(8,128)(2,1)S(1)} %get-tuple-element.18.first_ref.refs_0_), channel_id=1, source_target_pairs={{0,4},{1,5},{2,6},{3,7},{4,0},{5,1},{6,2},{7,3},{8,12},{9,13},{10,... | collective-permute-start | bytes 1572872 | tf_op jit(solution)/shard_map/ppermute | solution.py:179
  167.7 19.8 %collective-permute-done.3.refs_1_ = bf16[1024,256]{1,0:T(8,128)(2,1)} collective-permute-done((bf16[1024,256]{1,0:T(8,128)(2,1)S(1)}, bf16[1024,256]{1,0:T(8,128)(2,1)}, u32[]{:S(2)}, u32[]{:S(2)}) %collective-permute-start.3) | collective-permute-done | bytes 524320 | tf_op jit(solution)/shard_map/ppermute | solution.py:179
  187.5 1.9 collective-permute-start.5
  190.3 2.4 collective-permute-start.6
  193.3 7.4 %all-to-all-done.1 = bf16[16,4,72,128]{3,2,1,0:T(8,128)(2,1)} async-done(((bf16[16,4,72,128]{3,2,1,0:T(8,128)(2,1)}), bf16[16,4,72,128]{3,2,1,0:T(8,128)(2,1)}, u32[]{:S(2)}, u32[]{:S(2)}) %all-to-all-start.1) | async-done | bytes 1179680 | tf_op jit(solution)/shard_map/all_to_all | solution.py:196
  200.9 5.3 %hist_next.1.last_ref.refs_0_ = bf16[1024,128]{1,0:T(8,128)(2,1)S(1)} custom-call(s32[1,4608]{1,0:T(1,128)S(1)} %reshape.85.bins_ref, bf16[4608,128]{1,0:T(8,128)(2,1)} %bitcast.14.rows_ref), custom_call_target="tpu_custom_call" | custom-call | flops 2415919104 | bytes 1179648 | tf_op jit(solution)/shard_map/hist_next/pallas_call | solution.py:266
  206.2 2.7 collective-permute-start.7
  208.9 3.0 %collective-permute-start.8 = (bf16[1024,128]{1,0:T(8,128)(2,1)S(1)}, bf16[1024,128]{1,0:T(8,128)(2,1)S(1)}, u32[]{:S(2)}, u32[]{:S(2)}) collective-permute-start(bf16[1024,128]{1,0:T(8,128)(2,1)S(1)} %hist_next.1.last_ref.refs_0_), channel_id=1, source_target_pairs={{0,4},{1,5},{2,6},{3,7},{4,0},{5,1},{6,2},{7,3},{8,12},{9,13},{10,... | collective-permute-start | bytes 786440 | tf_op jit(solution)/shard_map/ppermute | solution.py:179
  212.0 2.9 %gram_first.1 = (bf16[4,96,1280]{2,1,0:T(8,128)(2,1)S(1)}, bf16[384,1024]{1,0:T(8,128)(2,1)S(1)}) custom-call(s32[5]{0:T(128)S(1)} %stack.26.slots_ref, f32[1024,1]{1,0:T(8,128)S(1)} %get-tuple-element.17.curve_ref, bf16[384,384]{1,0:T(8,128)(2,1)S(1)} %copy-done.2, bf16[384,1024]{1,0:T(8,128)(2,1)S(1)} %side_first.1.side_ref, ...), custom_call_target="tpu_custom_call" | custom-call | flops 1207959552 | bytes 2621440 | tf_op jit(solution)/shard_map/gram_first/pallas_call | solution.py:282
  216.8 4.3 %all-to-all-start.2 = ((bf16[4,96,1280]{2,1,0:T(8,128)(2,1)}), bf16[4,96,1280]{2,1,0:T(8,128)(2,1)S(1)}, u32[]{:S(2)}, u32[]{:S(2)}) async-start(bf16[4,96,1280]{2,1,0:T(8,128)(2,1)} %copy-done.3), calls=%async_computation.2 | async-start | bytes 1966080 | tf_op jit(solution)/shard_map/all_to_all | solution.py:196
  221.1 1.9 collective-permute-start.9
  223.0 2.4 collective-permute-start.10
  225.4 7.5 %all-to-all-done.2.first_ref = bf16[4,96,1280]{2,1,0:T(8,128)(2,1)S(1)} async-done(((bf16[4,96,1280]{2,1,0:T(8,128)(2,1)}), bf16[4,96,1280]{2,1,0:T(8,128)(2,1)S(1)}, u32[]{:S(2)}, u32[]{:S(2)}) %all-to-all-start.2) | async-done | bytes 983072 | tf_op jit(solution)/shard_map/all_to_all | solution.py:196
  232.9 1.7 gram_last.1
  234.7 10.3 %all_to_all.25.last_ref = bf16[4,96,640]{2,1,0:T(8,128)(2,1)S(1)} all-to-all(bf16[4,96,640]{2,1,0:T(8,128)(2,1)S(1)} %gram_last.1), channel_id=1, replica_groups=mesh['bins_0'=16,'bins_1'=4,'params'=8] {'bins_1'}, dimensions={0} | all-to-all | bytes 983040 | tf_op jit(solution)/shard_map/all_to_all | solution.py:196
  245.4 29.9 %all_to_all.26.got_ref = bf16[16,96,128]{2,1,0:T(8,128)(2,1)S(1)} all-to-all(bf16[16,96,128]{2,1,0:T(8,128)(2,1)S(1)} %add_across.1), channel_id=1, replica_groups=mesh['bins_0'=16,'bins_1'=4,'params'=8] {'bins_0'}, dimensions={0} | all-to-all | bytes 786432 | tf_op jit(solution)/shard_map/all_to_all | solution.py:196
  (48 shorter events, 11.8 us)
Async XLA Ops:
  1.7 1.7 copy-start
  3.3 0.7 copy-start.7
  8.1 19.1 %copy-start.1 = (bf16[3072,384]{1,0:T(8,128)(2,1)S(1)}, bf16[3072,384]{1,0:T(8,128)(2,1)}, u32[]{:S(2)}) copy-start(bf16[3072,384]{1,0:T(8,128)(2,1)} %w_ref.3) | copy-start | bytes 7077892
  8.1 136.1 %all-to-all-start = ((bf16[64,152,128]{2,1,0:T(8,128)(2,1)}), bf16[64,152,128]{2,1,0:T(8,128)(2,1)}, u32[]{:S(2)}, u32[]{:S(2)}) async-start(bf16[64,152,128]{2,1,0:T(8,128)(2,1)} %pack_first.1), calls=%async_computation | async-start | bytes 4980736 | tf_op jit(solution)/shard_map/all_to_all | solution.py:196
  29.8 19.7 %collective-permute-start.2 = (bf16[16,72,128]{2,1,0:T(8,128)(2,1)S(1)}, bf16[16,72,128]{2,1,0:T(8,128)(2,1)S(1)}, u32[]{:S(2)}, u32[]{:S(2)}) collective-permute-start(bf16[16,72,128]{2,1,0:T(8,128)(2,1)S(1)} %get-tuple-element.22), channel_id=1, source_target_pairs={{0,24},{8,0},{16,8},{24,16},{1,25},{9,1},{17,9},{25,17},{2,26},{10... | collective-permute-start | bytes 884744 | tf_op jit(solution)/shard_map/ppermute | solution.py:179
  34.4 16.0 %collective-permute-start.1 = (bf16[16,72,128]{2,1,0:T(8,128)(2,1)S(1)}, bf16[16,72,128]{2,1,0:T(8,128)(2,1)S(1)}, u32[]{:S(2)}, u32[]{:S(2)}) collective-permute-start(bf16[16,72,128]{2,1,0:T(8,128)(2,1)S(1)} %get-tuple-element.21), channel_id=1, source_target_pairs={{0,16},{8,24},{16,0},{24,8},{1,17},{9,25},{17,1},{25,9},{2,18},{10... | collective-permute-start | bytes 884744 | tf_op jit(solution)/shard_map/ppermute | solution.py:179
  37.2 20.0 %collective-permute-start = (bf16[16,72,128]{2,1,0:T(8,128)(2,1)S(1)}, bf16[16,72,128]{2,1,0:T(8,128)(2,1)S(1)}, u32[]{:S(2)}, u32[]{:S(2)}) collective-permute-start(bf16[16,72,128]{2,1,0:T(8,128)(2,1)S(1)} %get-tuple-element.20), channel_id=1, source_target_pairs={{0,8},{8,16},{16,24},{24,0},{1,9},{9,17},{17,25},{25,1},{2,10},{10... | collective-permute-start | bytes 884744 | tf_op jit(solution)/shard_map/ppermute | solution.py:179
  58.5 90.1 %copy-start.8 = (f32[1024]{0:T(1024)S(1)}, f32[1024]{0:T(1024)}, u32[]{:S(2)}) copy-start(f32[1024]{0:T(1024)} %param.10) | copy-start | bytes 12292
  58.5 90.4 %copy-start.9 = (f32[1024]{0:T(1024)S(1)}, f32[1024]{0:T(1024)}, u32[]{:S(2)}) copy-start(f32[1024]{0:T(1024)} %param.11) | copy-start | bytes 12292
  144.2 56.5 %all-to-all-start.1 = ((bf16[16,4,72,128]{3,2,1,0:T(8,128)(2,1)}), bf16[16,4,72,128]{3,2,1,0:T(8,128)(2,1)}, u32[]{:S(2)}, u32[]{:S(2)}) async-start(bf16[16,4,72,128]{3,2,1,0:T(8,128)(2,1)} %copy.17), calls=%async_computation.1 | async-start | bytes 2359296 | tf_op jit(solution)/shard_map/all_to_all | solution.py:196
  153.3 1.9 copy-start.6
  161.8 31.0 %copy-start.2 = (bf16[384,384]{1,0:T(8,128)(2,1)S(1)}, bf16[384,384]{1,0:T(8,128)(2,1)}, u32[]{:S(2)}) copy-start(bf16[384,384]{1,0:T(8,128)(2,1)} %constant.33.clone.order_ref) | copy-start | bytes 884740
  161.8 25.7 %collective-permute-start.3 = (bf16[1024,256]{1,0:T(8,128)(2,1)S(1)}, bf16[1024,256]{1,0:T(8,128)(2,1)}, u32[]{:S(2)}, u32[]{:S(2)}) collective-permute-start(bf16[1024,256]{1,0:T(8,128)(2,1)S(1)} %get-tuple-element.18.first_ref.refs_0_), channel_id=1, source_target_pairs={{0,6},{1,7},{2,0},{3,1},{4,2},{5,3},{6,4},{7,5},{8,14},{9,15},{10,... | collective-permute-start | bytes 1572872 | tf_op jit(solution)/shard_map/ppermute | solution.py:179
  164.7 24.8 %collective-permute-start.4 = (bf16[1024,256]{1,0:T(8,128)(2,1)S(1)}, bf16[1024,256]{1,0:T(8,128)(2,1)S(1)}, u32[]{:S(2)}, u32[]{:S(2)}) collective-permute-start(bf16[1024,256]{1,0:T(8,128)(2,1)S(1)} %get-tuple-element.18.first_ref.refs_0_), channel_id=1, source_target_pairs={{0,4},{1,5},{2,6},{3,7},{4,0},{5,1},{6,2},{7,3},{8,12},{9,13},{10,... | collective-permute-start | bytes 1572872 | tf_op jit(solution)/shard_map/ppermute | solution.py:179
  187.5 24.4 %collective-permute-start.5 = (bf16[1024,256]{1,0:T(8,128)(2,1)}, bf16[1024,256]{1,0:T(8,128)(2,1)}, u32[]{:S(2)}, u32[]{:S(2)}) collective-permute-start(bf16[1024,256]{1,0:T(8,128)(2,1)} %collective-permute-done.3.refs_1_), channel_id=1, source_target_pairs={{0,1},{1,0},{2,3},{3,2},{4,5},{5,4},{6,7},{7,6},{8,9},{9,8},{10,11... | collective-permute-start | bytes 1572872 | tf_op jit(solution)/shard_map/ppermute | solution.py:190
  190.3 21.7 %collective-permute-start.6 = (bf16[1024,256]{1,0:T(8,128)(2,1)}, bf16[1024,256]{1,0:T(8,128)(2,1)}, u32[]{:S(2)}, u32[]{:S(2)}) collective-permute-start(bf16[1024,256]{1,0:T(8,128)(2,1)} %broadcast_select_fusion), channel_id=1, source_target_pairs={{0,1},{1,0},{2,3},{3,2},{4,5},{5,4},{6,7},{7,6},{8,9},{9,8},{10,11... | collective-permute-start | bytes 1572872 | tf_op jit(solution)/shard_map/ppermute | solution.py:191
  206.2 14.9 %collective-permute-start.7 = (bf16[1024,128]{1,0:T(8,128)(2,1)S(1)}, bf16[1024,128]{1,0:T(8,128)(2,1)S(1)}, u32[]{:S(2)}, u32[]{:S(2)}) collective-permute-start(bf16[1024,128]{1,0:T(8,128)(2,1)S(1)} %hist_next.1.last_ref.refs_0_), channel_id=1, source_target_pairs={{0,6},{1,7},{2,0},{3,1},{4,2},{5,3},{6,4},{7,5},{8,14},{9,15},{10,... | collective-permute-start | bytes 786440 | tf_op jit(solution)/shard_map/ppermute | solution.py:179
  208.9 14.0 %collective-permute-start.8 = (bf16[1024,128]{1,0:T(8,128)(2,1)S(1)}, bf16[1024,128]{1,0:T(8,128)(2,1)S(1)}, u32[]{:S(2)}, u32[]{:S(2)}) collective-permute-start(bf16[1024,128]{1,0:T(8,128)(2,1)S(1)} %hist_next.1.last_ref.refs_0_), channel_id=1, source_target_pairs={{0,4},{1,5},{2,6},{3,7},{4,0},{5,1},{6,2},{7,3},{8,12},{9,13},{10,... | collective-permute-start | bytes 786440 | tf_op jit(solution)/shard_map/ppermute | solution.py:179
  214.9 1.0 copy-start.3
  215.9 0.9 copy-start.4
  216.8 16.1 %copy-start.5 = (bf16[384,1024]{1,0:T(8,128)(2,1)S(1)}, bf16[384,1024]{1,0:T(8,128)(2,1)}, u32[]{:S(2)}) copy-start(bf16[384,1024]{1,0:T(8,128)(2,1)} %copy-done.4) | copy-start | bytes 2359300
  216.8 16.1 %all-to-all-start.2 = ((bf16[4,96,1280]{2,1,0:T(8,128)(2,1)}), bf16[4,96,1280]{2,1,0:T(8,128)(2,1)S(1)}, u32[]{:S(2)}, u32[]{:S(2)}) async-start(bf16[4,96,1280]{2,1,0:T(8,128)(2,1)} %copy-done.3), calls=%async_computation.2 | async-start | bytes 1966080 | tf_op jit(solution)/shard_map/all_to_all | solution.py:196
  221.1 11.9 %collective-permute-start.9 = (bf16[1024,128]{1,0:T(8,128)(2,1)S(1)}, bf16[1024,128]{1,0:T(8,128)(2,1)S(1)}, u32[]{:S(2)}, u32[]{:S(2)}) collective-permute-start(bf16[1024,128]{1,0:T(8,128)(2,1)S(1)} %collective-permute-done.7.refs_1_), channel_id=1, source_target_pairs={{0,1},{1,0},{2,3},{3,2},{4,5},{5,4},{6,7},{7,6},{8,9},{9,8},{10,11... | collective-permute-start | bytes 786440 | tf_op jit(solution)/shard_map/ppermute | solution.py:190
  223.0 9.9 %collective-permute-start.10 = (bf16[1024,128]{1,0:T(8,128)(2,1)S(1)}, bf16[1024,128]{1,0:T(8,128)(2,1)S(1)}, u32[]{:S(2)}, u32[]{:S(2)}) collective-permute-start(bf16[1024,128]{1,0:T(8,128)(2,1)S(1)} %broadcast_select_fusion.1), channel_id=1, source_target_pairs={{0,1},{1,0},{2,3},{3,2},{4,5},{5,4},{6,7},{7,6},{8,9},{9,8},{10,11... | collective-permute-start | bytes 786440 | tf_op jit(solution)/shard_map/ppermute | solution.py:191

commit v10 on v9

--- a/solution.py
+++ b/solution.py
@@ -128,9 +128,8 @@
 
 
 def gram_first(slots_ref, curve_ref, order_ref, side_ref, last_ref, *refs):
-    firsts, (out_ref, lhs_ref) = refs[:-2], refs[-2:]
+    firsts, out_ref = refs[:-1], refs[-1]
     lhs = side_ref[...] + side_of(curve_ref, order_ref[:, 2 * COLS :], last_ref).astype(jnp.bfloat16)
-    lhs_ref[...] = lhs
     wide, step = firsts[0].shape[1], out_ref.shape[1]
     for k, part in enumerate(firsts):
         full = jnp.dot(lhs, part[...], preferred_element_type=jnp.float32).astype(jnp.bfloat16)
@@ -139,9 +138,9 @@
             out_ref[y, :, pl.ds(at, wide)] = full[y * step : (y + 1) * step]
 
 
-def gram_last(slots_ref, lhs_ref, *refs):
+def gram_last(slots_ref, curve_ref, order_ref, side_ref, *refs):
     lasts, out_ref = refs[:-1], refs[-1]
-    lhs = lhs_ref[...]
+    lhs = side_ref[...] + side_of(curve_ref, order_ref[:, 2 * COLS :], lasts[0]).astype(jnp.bfloat16)
     wide, step = lasts[0].shape[1], out_ref.shape[1]
     for k, part in enumerate(lasts):
         full = jnp.dot(lhs, part[...], preferred_element_type=jnp.float32).astype(jnp.bfloat16)
@@ -279,28 +278,25 @@
     lasts = [last] + partners(last)[0]
     slots = jnp.stack([jnp.asarray(k, jnp.int32) for k in [0] + slots])
 
-    part_a, lhs = pl.pallas_call(
+    part_a = pl.pallas_call(
         gram_first,
-        out_shape=[
-            jax.ShapeDtypeStruct((n1, width // n1, turns * 2 * COLS), bf16),
-            jax.ShapeDtypeStruct((width, bins_dev), bf16),
-        ],
+        out_shape=jax.ShapeDtypeStruct((n1, width // n1, turns * 2 * COLS), bf16),
         in_specs=[SMEM] + [VMEM] * (4 + turns),
-        out_specs=[VMEM] * 2,
+        out_specs=VMEM,
         compiler_params=PARAMS,
         cost_estimate=cost(2 * bins_dev * width * 2 * COLS * (turns + 1), 2 * turns * COLS * bins_dev * 2),
         name="gram_first",
     )(slots, curve, jnp.asarray(order, bf16), side, last, *firsts)
-    part_a, lhs = lax.optimization_barrier((exchange(part_a, BINS[1]), lhs))
+    part_a, side = lax.optimization_barrier((exchange(part_a, BINS[1]), side))
     part_b = pl.pallas_call(
         gram_last,
         out_shape=jax.ShapeDtypeStruct((n1, width // n1, turns * COLS), bf16),
-        in_specs=[SMEM] + [VMEM] * (1 + turns),
+        in_specs=[SMEM] + [VMEM] * (3 + turns),
         out_specs=VMEM,
         compiler_params=PARAMS,
         cost_estimate=cost(2 * bins_dev * width * COLS * turns, turns * COLS * bins_dev * 2),
         name="gram_last",
-    )(slots, lhs, *lasts)
+    )(slots, curve, jnp.asarray(order, bf16), side, *lasts)
     part_b = exchange(part_b, BINS[1])
     packed = -(-lines * turns * width // 128 // 16) * 16
     across = pl.pallas_call(

time: 279 us -> 283 us (1.014)
  blocking collectives: 40.1 us -> 45.6 us
  waiting for transfers between devices: 138 us -> 135 us
    all_to_all x2, blocking collectives: 40.1 us -> 45.6 us  [exchange(): return lax.all_to_all(value, axis, split_axis=0, concat_axis=0, tiled=True)]
    unnamed x20 -> x22, local copies, waits for them, and re-layouts: 4.26 us -> 6.63 us
  transfers between devices with their start and end apart: 14 -> 14, of which waited for: 7 -> 9; matrix products, arithmetic and copies ran while one was open for 3% -> 3% of each run, Pallas kernels for 6% -> 6%
where the time goes in v10:
time: 283 us; the launch traced here: 282 us
  waiting for transfers between devices  135 us (48%)
  starting transfers between devices  57.2 us (20%)
  blocking collectives  45.6 us (16%)
  Pallas kernels  25.6 us (9%)
  local copies, waits for them, and re-layouts  12 us (4%)
  other arithmetic  6.08 us (2%)
    all_to_all x3, waiting for transfers between devices, exchange(): return lax.all_to_all(value, axis, split_axis=0, concat_axis=0, tiled=True)  99.6 us
    all_to_all x2, blocking collectives, exchange(): return lax.all_to_all(value, axis, split_axis=0, concat_axis=0, tiled=True)  45.6 us
    ppermute x7, waiting for transfers between devices, from_behind(): return lax.ppermute(value, axis, pairs)  35.3 us
    all_to_all x3, starting transfers between devices, exchange(): return lax.all_to_all(value, axis, split_axis=0, concat_axis=0, tiled=True)  27.6 us
    ppermute x7, starting transfers between devices, from_behind(): return lax.ppermute(value, axis, pairs)  22 us
    unnamed x22, local copies, waits for them, and re-layouts  6.63 us
    pallas_call x1, Pallas kernels, body(): pl.pallas_call(hist_first, out_shape=[jax.ShapeDtypeStruct((bins_dev, 2 *...  6.55 us
  transfers between devices with their start and end apart: 14, of which 9 were waited for; matrix products, arithmetic and copies ran while one was open for 3% of the time, Pallas kernels for 6%

profile of v10, /device:TPU:6, one launch (start us, length us, event | category | flops | bytes accessed | tf_op | source)
XLA Modules:
  0.0 281.8 jit_solution(15978843697153044375)
XLA Ops:
  1.7 1.7 copy-done
  4.0 4.1 %pack_first.1 = bf16[64,152,128]{2,1,0:T(8,128)(2,1)} custom-call(s32[64]{0:T(128)S(1)} %convert_reduce_fusion.starts_ref, s32[24,128]{1,0:T(8,128)S(1)} %bitcast.20, f32[24,128]{1,0:T(8,128)S(1)} %bitcast_convert_fusion.nominal_ref, bf16[3072,384]{1,0:T(8,128)(2,1)S(1)} %copy-done), custom_call_target="tpu_custom_call" | custom-call | flops 226492416 | bytes 4980736 | tf_op jit(solution)/shard_map/pack_first/pallas_call | solution.py:209
  8.1 19.1 %all-to-all-start = ((bf16[64,152,128]{2,1,0:T(8,128)(2,1)}), bf16[64,152,128]{2,1,0:T(8,128)(2,1)}, u32[]{:S(2)}, u32[]{:S(2)}) async-start(bf16[64,152,128]{2,1,0:T(8,128)(2,1)} %pack_first.1), calls=%async_computation | async-start | bytes 4980736 | tf_op jit(solution)/shard_map/all_to_all | solution.py:195
  27.3 2.5 pack_rest.1
  29.8 3.4 %collective-permute-start = (bf16[16,72,128]{2,1,0:T(8,128)(2,1)S(1)}, bf16[16,72,128]{2,1,0:T(8,128)(2,1)S(1)}, u32[]{:S(2)}, u32[]{:S(2)}) collective-permute-start(bf16[16,72,128]{2,1,0:T(8,128)(2,1)S(1)} %get-tuple-element.18), channel_id=1, source_target_pairs={{0,8},{8,16},{16,24},{24,0},{1,9},{9,17},{17,25},{25,1},{2,10},{10... | collective-permute-start | bytes 884744 | tf_op jit(solution)/shard_map/ppermute | solution.py:178
  33.2 4.6 %collective-permute-start.1 = (bf16[16,72,128]{2,1,0:T(8,128)(2,1)S(1)}, bf16[16,72,128]{2,1,0:T(8,128)(2,1)S(1)}, u32[]{:S(2)}, u32[]{:S(2)}) collective-permute-start(bf16[16,72,128]{2,1,0:T(8,128)(2,1)S(1)} %get-tuple-element.19), channel_id=1, source_target_pairs={{0,16},{8,24},{16,0},{24,8},{1,17},{9,25},{17,1},{25,9},{2,18},{10... | collective-permute-start | bytes 884744 | tf_op jit(solution)/shard_map/ppermute | solution.py:178
  37.8 3.4 %collective-permute-start.2 = (bf16[16,72,128]{2,1,0:T(8,128)(2,1)S(1)}, bf16[16,72,128]{2,1,0:T(8,128)(2,1)S(1)}, u32[]{:S(2)}, u32[]{:S(2)}) collective-permute-start(bf16[16,72,128]{2,1,0:T(8,128)(2,1)S(1)} %get-tuple-element.20), channel_id=1, source_target_pairs={{0,24},{8,0},{16,8},{24,16},{1,25},{9,1},{17,9},{25,17},{2,26},{10... | collective-permute-start | bytes 884744 | tf_op jit(solution)/shard_map/ppermute | solution.py:178
  41.2 4.1 %collective-permute-done = bf16[16,72,128]{2,1,0:T(8,128)(2,1)S(1)} collective-permute-done((bf16[16,72,128]{2,1,0:T(8,128)(2,1)S(1)}, bf16[16,72,128]{2,1,0:T(8,128)(2,1)S(1)}, u32[]{:S(2)}, u32[]{:S(2)}) %collective-permute-start) | collective-permute-done | bytes 294944 | tf_op jit(solution)/shard_map/ppermute | solution.py:178
  45.3 9.4 %collective-permute-done.1 = bf16[16,72,128]{2,1,0:T(8,128)(2,1)S(1)} collective-permute-done((bf16[16,72,128]{2,1,0:T(8,128)(2,1)S(1)}, bf16[16,72,128]{2,1,0:T(8,128)(2,1)S(1)}, u32[]{:S(2)}, u32[]{:S(2)}) %collective-permute-start.1) | collective-permute-done | bytes 294944 | tf_op jit(solution)/shard_map/ppermute | solution.py:178
  56.0 88.2 %all-to-all-done = bf16[64,152,128]{2,1,0:T(8,128)(2,1)} async-done(((bf16[64,152,128]{2,1,0:T(8,128)(2,1)}), bf16[64,152,128]{2,1,0:T(8,128)(2,1)}, u32[]{:S(2)}, u32[]{:S(2)}) %all-to-all-start) | async-done | bytes 2490400 | tf_op jit(solution)/shard_map/all_to_all | solution.py:195
  144.2 4.4 %all-to-all-start.1 = ((bf16[16,4,72,128]{3,2,1,0:T(8,128)(2,1)}), bf16[16,4,72,128]{3,2,1,0:T(8,128)(2,1)}, u32[]{:S(2)}, u32[]{:S(2)}) async-start(bf16[16,4,72,128]{3,2,1,0:T(8,128)(2,1)} %copy.18), calls=%async_computation.1 | async-start | bytes 2359296 | tf_op jit(solution)/shard_map/all_to_all | solution.py:195
  152.5 1.8 fusion.4
  154.4 6.6 %hist_first.1 = (bf16[1024,256]{1,0:T(8,128)(2,1)S(1)}, f32[1024,1]{1,0:T(8,128)S(1)}) custom-call(s32[1,4608]{1,0:T(1,128)S(1)} %convert_element_type.35.bins_ref, bf16[8,4608]{1,0:T(8,128)(2,1)S(1)} %broadcast_in_dim.2.nominal_ref, f32[1024,1]{1,0:T(8,128)S(1)} %copy.16.background_ref, f32[1024,1]{1,0:T(8,128)S(1)} %copy.17.observed_ref, ...), custom_call_target="tpu_custom_call" | custom-call | flops 4831838208 | bytes 2359296 | tf_op jit(solution)/shard_map/hist_first/pallas_call | solution.py:240
  160.9 3.4 %collective-permute-start.4 = (bf16[1024,256]{1,0:T(8,128)(2,1)S(1)}, bf16[1024,256]{1,0:T(8,128)(2,1)S(1)}, u32[]{:S(2)}, u32[]{:S(2)}) collective-permute-start(bf16[1024,256]{1,0:T(8,128)(2,1)S(1)} %get-tuple-element.16.first_ref.refs_0_), channel_id=1, source_target_pairs={{0,4},{1,5},{2,6},{3,7},{4,0},{5,1},{6,2},{7,3},{8,12},{9,13},{10,... | collective-permute-start | bytes 1572872 | tf_op jit(solution)/shard_map/ppermute | solution.py:178
  164.4 1.9 collective-permute-start.3
  166.3 13.1 %collective-permute-done.4.refs_2_ = bf16[1024,256]{1,0:T(8,128)(2,1)S(1)} collective-permute-done((bf16[1024,256]{1,0:T(8,128)(2,1)S(1)}, bf16[1024,256]{1,0:T(8,128)(2,1)S(1)}, u32[]{:S(2)}, u32[]{:S(2)}) %collective-permute-start.4) | collective-permute-done | bytes 524320 | tf_op jit(solution)/shard_map/ppermute | solution.py:178
  180.2 1.9 collective-permute-start.6
  182.2 4.8 %collective-permute-done.3.refs_1_ = bf16[1024,256]{1,0:T(8,128)(2,1)} collective-permute-done((bf16[1024,256]{1,0:T(8,128)(2,1)S(1)}, bf16[1024,256]{1,0:T(8,128)(2,1)}, u32[]{:S(2)}, u32[]{:S(2)}) %collective-permute-start.3) | collective-permute-done | bytes 524320 | tf_op jit(solution)/shard_map/ppermute | solution.py:178
  187.0 1.9 collective-permute-start.5
  189.5 11.3 %all-to-all-done.1 = bf16[16,4,72,128]{3,2,1,0:T(8,128)(2,1)} async-done(((bf16[16,4,72,128]{3,2,1,0:T(8,128)(2,1)}), bf16[16,4,72,128]{3,2,1,0:T(8,128)(2,1)}, u32[]{:S(2)}, u32[]{:S(2)}) %all-to-all-start.1) | async-done | bytes 1179680 | tf_op jit(solution)/shard_map/all_to_all | solution.py:195
  200.9 5.3 %hist_next.1.last_ref.refs_0_ = bf16[1024,128]{1,0:T(8,128)(2,1)S(1)} custom-call(s32[1,4608]{1,0:T(1,128)S(1)} %reshape.85.bins_ref, bf16[4608,128]{1,0:T(8,128)(2,1)} %bitcast.14.rows_ref), custom_call_target="tpu_custom_call" | custom-call | flops 2415919104 | bytes 1179648 | tf_op jit(solution)/shard_map/hist_next/pallas_call | solution.py:265
  206.2 3.3 %collective-permute-start.8 = (bf16[1024,128]{1,0:T(8,128)(2,1)S(1)}, bf16[1024,128]{1,0:T(8,128)(2,1)}, u32[]{:S(2)}, u32[]{:S(2)}) collective-permute-start(bf16[1024,128]{1,0:T(8,128)(2,1)S(1)} %hist_next.1.last_ref.refs_0_), channel_id=1, source_target_pairs={{0,4},{1,5},{2,6},{3,7},{4,0},{5,1},{6,2},{7,3},{8,12},{9,13},{10,... | collective-permute-start | bytes 786440 | tf_op jit(solution)/shard_map/ppermute | solution.py:178
  209.5 2.9 %gram_first.1 = bf16[4,96,1280]{2,1,0:T(8,128)(2,1)S(1)} custom-call(s32[5]{0:T(128)S(1)} %stack.26.slots_ref, f32[1024,1]{1,0:T(8,128)S(1)} %get-tuple-element.15.curve_ref, bf16[384,384]{1,0:T(8,128)(2,1)S(1)} %copy-done.3, bf16[384,1024]{1,0:T(8,128)(2,1)S(1)} %side_first.1.side_ref, bf16[1024,128]{1,0:T(8,128)(2,1)S(1)} %hist_next.1.last_ref.refs_0_, ...), custom_call_target="tpu_custom_call" | custom-call | flops 1207959552 | bytes 2621440 | tf_op jit(solution)/shard_map/gram_first/pallas_call | solution.py:281
  213.4 4.1 %all-to-all-start.2 = ((bf16[4,96,1280]{2,1,0:T(8,128)(2,1)}), bf16[4,96,1280]{2,1,0:T(8,128)(2,1)S(1)}, u32[]{:S(2)}, u32[]{:S(2)}) async-start(bf16[4,96,1280]{2,1,0:T(8,128)(2,1)} %copy-done.2), calls=%async_computation.2 | async-start | bytes 1966080 | tf_op jit(solution)/shard_map/all_to_all | solution.py:195
  217.6 1.9 collective-permute-start.7
  219.5 1.7 broadcast_select_fusion.1
  221.2 1.9 collective-permute-start.10
  223.1 3.9 %collective-permute-done.7.refs_1_ = bf16[1024,128]{1,0:T(8,128)(2,1)S(1)} collective-permute-done((bf16[1024,128]{1,0:T(8,128)(2,1)S(1)}, bf16[1024,128]{1,0:T(8,128)(2,1)S(1)}, u32[]{:S(2)}, u32[]{:S(2)}) %collective-permute-start.7) | collective-permute-done | bytes 262176 | tf_op jit(solution)/shard_map/ppermute | solution.py:178
  227.0 1.9 collective-permute-start.9
  232.5 2.6 gram_last.1
  235.1 14.2 %all_to_all.25.last_ref = bf16[4,96,640]{2,1,0:T(8,128)(2,1)S(1)} all-to-all(bf16[4,96,640]{2,1,0:T(8,128)(2,1)S(1)} %gram_last.1), channel_id=1, replica_groups=mesh['bins_0'=16,'bins_1'=4,'params'=8] {'bins_1'}, dimensions={0} | all-to-all | bytes 983040 | tf_op jit(solution)/shard_map/all_to_all | solution.py:195
  249.7 31.4 %all_to_all.26.got_ref = bf16[16,96,128]{2,1,0:T(8,128)(2,1)S(1)} all-to-all(bf16[16,96,128]{2,1,0:T(8,128)(2,1)S(1)} %add_across.1), channel_id=1, replica_groups=mesh['bins_0'=16,'bins_1'=4,'params'=8] {'bins_0'}, dimensions={0} | all-to-all | bytes 786432 | tf_op jit(solution)/shard_map/all_to_all | solution.py:195
  (50 shorter events, 14.8 us)
Async XLA Ops:
  1.7 1.7 copy-start
  3.3 0.7 copy-start.8
  8.1 19.1 %copy-start.1 = (bf16[3072,384]{1,0:T(8,128)(2,1)S(1)}, bf16[3072,384]{1,0:T(8,128)(2,1)}, u32[]{:S(2)}) copy-start(bf16[3072,384]{1,0:T(8,128)(2,1)} %w_ref.3) | copy-start | bytes 7077892
  8.1 136.1 %all-to-all-start = ((bf16[64,152,128]{2,1,0:T(8,128)(2,1)}), bf16[64,152,128]{2,1,0:T(8,128)(2,1)}, u32[]{:S(2)}, u32[]{:S(2)}) async-start(bf16[64,152,128]{2,1,0:T(8,128)(2,1)} %pack_first.1), calls=%async_computation | async-start | bytes 4980736 | tf_op jit(solution)/shard_map/all_to_all | solution.py:195
  29.8 15.5 %collective-permute-start = (bf16[16,72,128]{2,1,0:T(8,128)(2,1)S(1)}, bf16[16,72,128]{2,1,0:T(8,128)(2,1)S(1)}, u32[]{:S(2)}, u32[]{:S(2)}) collective-permute-start(bf16[16,72,128]{2,1,0:T(8,128)(2,1)S(1)} %get-tuple-element.18), channel_id=1, source_target_pairs={{0,8},{8,16},{16,24},{24,0},{1,9},{9,17},{17,25},{25,1},{2,10},{10... | collective-permute-start | bytes 884744 | tf_op jit(solution)/shard_map/ppermute | solution.py:178
  33.2 21.4 %collective-permute-start.1 = (bf16[16,72,128]{2,1,0:T(8,128)(2,1)S(1)}, bf16[16,72,128]{2,1,0:T(8,128)(2,1)S(1)}, u32[]{:S(2)}, u32[]{:S(2)}) collective-permute-start(bf16[16,72,128]{2,1,0:T(8,128)(2,1)S(1)} %get-tuple-element.19), channel_id=1, source_target_pairs={{0,16},{8,24},{16,0},{24,8},{1,17},{9,25},{17,1},{25,9},{2,18},{10... | collective-permute-start | bytes 884744 | tf_op jit(solution)/shard_map/ppermute | solution.py:178
  37.8 16.9 %collective-permute-start.2 = (bf16[16,72,128]{2,1,0:T(8,128)(2,1)S(1)}, bf16[16,72,128]{2,1,0:T(8,128)(2,1)S(1)}, u32[]{:S(2)}, u32[]{:S(2)}) collective-permute-start(bf16[16,72,128]{2,1,0:T(8,128)(2,1)S(1)} %get-tuple-element.20), channel_id=1, source_target_pairs={{0,24},{8,0},{16,8},{24,16},{1,25},{9,1},{17,9},{25,17},{2,26},{10... | collective-permute-start | bytes 884744 | tf_op jit(solution)/shard_map/ppermute | solution.py:178
  56.0 92.6 %copy-start.9 = (f32[1024]{0:T(1024)S(1)}, f32[1024]{0:T(1024)}, u32[]{:S(2)}) copy-start(f32[1024]{0:T(1024)} %param.11) | copy-start | bytes 12292
  56.0 92.9 %copy-start.10 = (f32[1024]{0:T(1024)S(1)}, f32[1024]{0:T(1024)}, u32[]{:S(2)}) copy-start(f32[1024]{0:T(1024)} %param.12) | copy-start | bytes 12292
  144.2 56.5 %all-to-all-start.1 = ((bf16[16,4,72,128]{3,2,1,0:T(8,128)(2,1)}), bf16[16,4,72,128]{3,2,1,0:T(8,128)(2,1)}, u32[]{:S(2)}, u32[]{:S(2)}) async-start(bf16[16,4,72,128]{3,2,1,0:T(8,128)(2,1)} %copy.18), calls=%async_computation.1 | async-start | bytes 2359296 | tf_op jit(solution)/shard_map/all_to_all | solution.py:195
  160.9 28.0 %copy-start.3 = (bf16[384,384]{1,0:T(8,128)(2,1)S(1)}, bf16[384,384]{1,0:T(8,128)(2,1)}, u32[]{:S(2)}) copy-start(bf16[384,384]{1,0:T(8,128)(2,1)} %constant.33.clone.order_ref) | copy-start | bytes 884740
  160.9 18.4 %collective-permute-start.4 = (bf16[1024,256]{1,0:T(8,128)(2,1)S(1)}, bf16[1024,256]{1,0:T(8,128)(2,1)S(1)}, u32[]{:S(2)}, u32[]{:S(2)}) collective-permute-start(bf16[1024,256]{1,0:T(8,128)(2,1)S(1)} %get-tuple-element.16.first_ref.refs_0_), channel_id=1, source_target_pairs={{0,4},{1,5},{2,6},{3,7},{4,0},{5,1},{6,2},{7,3},{8,12},{9,13},{10,... | collective-permute-start | bytes 1572872 | tf_op jit(solution)/shard_map/ppermute | solution.py:178
  164.4 22.6 %collective-permute-start.3 = (bf16[1024,256]{1,0:T(8,128)(2,1)S(1)}, bf16[1024,256]{1,0:T(8,128)(2,1)}, u32[]{:S(2)}, u32[]{:S(2)}) collective-permute-start(bf16[1024,256]{1,0:T(8,128)(2,1)S(1)} %get-tuple-element.16.first_ref.refs_0_), channel_id=1, source_target_pairs={{0,6},{1,7},{2,0},{3,1},{4,2},{5,3},{6,4},{7,5},{8,14},{9,15},{10,... | collective-permute-start | bytes 1572872 | tf_op jit(solution)/shard_map/ppermute | solution.py:178
  180.2 29.3 %collective-permute-start.6 = (bf16[1024,256]{1,0:T(8,128)(2,1)}, bf16[1024,256]{1,0:T(8,128)(2,1)}, u32[]{:S(2)}, u32[]{:S(2)}) collective-permute-start(bf16[1024,256]{1,0:T(8,128)(2,1)} %broadcast_select_fusion), channel_id=1, source_target_pairs={{0,1},{1,0},{2,3},{3,2},{4,5},{5,4},{6,7},{7,6},{8,9},{9,8},{10,11... | collective-permute-start | bytes 1572872 | tf_op jit(solution)/shard_map/ppermute | solution.py:190
  187.0 22.6 %collective-permute-start.5 = (bf16[1024,256]{1,0:T(8,128)(2,1)}, bf16[1024,256]{1,0:T(8,128)(2,1)}, u32[]{:S(2)}, u32[]{:S(2)}) collective-permute-start(bf16[1024,256]{1,0:T(8,128)(2,1)} %collective-permute-done.3.refs_1_), channel_id=1, source_target_pairs={{0,1},{1,0},{2,3},{3,2},{4,5},{5,4},{6,7},{7,6},{8,9},{9,8},{10,11... | collective-permute-start | bytes 1572872 | tf_op jit(solution)/shard_map/ppermute | solution.py:189
  206.2 13.3 %collective-permute-start.8 = (bf16[1024,128]{1,0:T(8,128)(2,1)S(1)}, bf16[1024,128]{1,0:T(8,128)(2,1)}, u32[]{:S(2)}, u32[]{:S(2)}) collective-permute-start(bf16[1024,128]{1,0:T(8,128)(2,1)S(1)} %hist_next.1.last_ref.refs_0_), channel_id=1, source_target_pairs={{0,4},{1,5},{2,6},{3,7},{4,0},{5,1},{6,2},{7,3},{8,12},{9,13},{10,... | collective-permute-start | bytes 786440 | tf_op jit(solution)/shard_map/ppermute | solution.py:178
  212.5 1.0 copy-start.2
  213.4 16.3 %all-to-all-start.2 = ((bf16[4,96,1280]{2,1,0:T(8,128)(2,1)}), bf16[4,96,1280]{2,1,0:T(8,128)(2,1)S(1)}, u32[]{:S(2)}, u32[]{:S(2)}) async-start(bf16[4,96,1280]{2,1,0:T(8,128)(2,1)} %copy-done.2), calls=%async_computation.2 | async-start | bytes 1966080 | tf_op jit(solution)/shard_map/all_to_all | solution.py:195
  217.6 9.5 %collective-permute-start.7 = (bf16[1024,128]{1,0:T(8,128)(2,1)S(1)}, bf16[1024,128]{1,0:T(8,128)(2,1)S(1)}, u32[]{:S(2)}, u32[]{:S(2)}) collective-permute-start(bf16[1024,128]{1,0:T(8,128)(2,1)S(1)} %hist_next.1.last_ref.refs_0_), channel_id=1, source_target_pairs={{0,6},{1,7},{2,0},{3,1},{4,2},{5,3},{6,4},{7,5},{8,14},{9,15},{10,... | collective-permute-start | bytes 786440 | tf_op jit(solution)/shard_map/ppermute | solution.py:178
  221.2 8.5 %collective-permute-start.10 = (bf16[1024,128]{1,0:T(8,128)(2,1)}, bf16[1024,128]{1,0:T(8,128)(2,1)S(1)}, u32[]{:S(2)}, u32[]{:S(2)}) collective-permute-start(bf16[1024,128]{1,0:T(8,128)(2,1)} %broadcast_select_fusion.1), channel_id=1, source_target_pairs={{0,1},{1,0},{2,3},{3,2},{4,5},{5,4},{6,7},{7,6},{8,9},{9,8},{10,11... | collective-permute-start | bytes 786440 | tf_op jit(solution)/shard_map/ppermute | solution.py:190
  227.0 3.6 %collective-permute-start.9 = (bf16[1024,128]{1,0:T(8,128)(2,1)S(1)}, bf16[1024,128]{1,0:T(8,128)(2,1)}, u32[]{:S(2)}, u32[]{:S(2)}) collective-permute-start(bf16[1024,128]{1,0:T(8,128)(2,1)S(1)} %collective-permute-done.7.refs_1_), channel_id=1, source_target_pairs={{0,1},{1,0},{2,3},{3,2},{4,5},{5,4},{6,7},{7,6},{8,9},{9,8},{10,11... | collective-permute-start | bytes 786440 | tf_op jit(solution)/shard_map/ppermute | solution.py:189
  228.9 0.7 copy-start.4
  229.7 0.7 copy-start.6
  230.6 1.0 copy-start.5
  231.5 0.9 copy-start.7
